TPU v7x, 32 devices: a whole 2x2x4 slice. The times are simulated.
32 devices in a mesh: section: 2 (over core), dp: 16 (over z, y, x).
Axes of the slice: x: 2, y: 2, z: 4, core: 2. Of those that a mesh axis runs over, the one named last changes fastest.
Arguments:
- inputs: bfloat16 [4, 64, 160, 400], P(None, 'dp'), may hold values from -6 to 6
- cotangent: bfloat16 [4, 64, 160, 400], P(None, 'dp'), may hold values from -6 to 6
- land: int32 [64, 160], P('dp'), may hold values from 0 to 1, as said below
- kernel: float32 [2, 49, 400], P('section'), may hold values from -0.875 to 0.875
- bn_gain: float32 [2, 400], P('section'), may hold values from 0.25 to 1.75
- bn_bias: float32 [2, 400], P('section'), may hold values from -3 to 3
- bias_in: float32 [2, 1600], P('section'), may hold values from -3 to 3
- bias_out: float32 [2, 400], P('section'), may hold values from -2 to 2
- w_in: float32 [2, 640000], P('section', 'dp'), may hold values from -0.3125 to 0.3125
- w_out: float32 [2, 640000], P('section', 'dp'), may hold values from -0.21875 to 0.21875
- resample: float32 [2, 1280000], P('section', 'dp'), may hold values from -0.15625 to 0.15625
- merge: float32 [320000], P(('section', 'dp')), may hold values from -0.21875 to 0.21875
Outputs:
- activations: bfloat16 [2, 4, 64, 160, 400], P('section', None, 'dp')
- grad_input: float32 [2, 4, 64, 160, 400], P('section', None, 'dp')
- grad_kernel: float32 [2, 49, 400], P('section')
- grad_gain: float32 [2, 400], P('section')
- grad_shift: float32 [2, 400], P('section')
- grad_bias_in: float32 [2, 1600], P('section')
- grad_bias_out: float32 [2, 400], P('section')
- grad_w_in: float32 [2, 640000], P('section', 'dp')
- grad_w_out: float32 [2, 640000], P('section', 'dp')
- grad_resample: float32 [2, 1280000], P('section', 'dp')
- grad_merge: float32 [320000], P(('section', 'dp'))
Inputs may be any that keep to these rules, and one draw needn't show every extreme that they name: 1 marks an ocean cell and 0 a land cell.
All inputs are finite; a program needn't handle non-finite values.
Results may differ from a plain program's by a relative error of at most 0.015.
Values may be sent and summed in bfloat16 or wider, within the bound.
A program may use at most 320 MiB of HBM per device.

v0:
```python
import jax
import jax.numpy as jnp
from jax import lax
from jax.sharding import PartitionSpec as P

eps_norm = 1e-05


def extended(cells, sides, width):
    for axis, dim in sides:
        count = lax.axis_size(axis)
        ends = count - 1
        head = lax.slice_in_dim(cells, 0, width, axis=dim)
        tail = lax.slice_in_dim(cells, cells.shape[dim] - width, cells.shape[dim], axis=dim)
        cells = jnp.concatenate(
            [
                lax.ppermute(tail, axis, [(i, (i + 1) % count) for i in range(ends)]),
                cells,
                lax.ppermute(head, axis, [((i + 1) % count, i) for i in range(ends)]),
            ],
            axis=dim,
        )
    return cells


def passed_along(value, axis, steps):
    count = lax.axis_size(axis)
    initial, last = (max(0, -steps), min(count, count - steps))
    return lax.ppermute(value, axis, [(source, source + steps) for source in range(initial, last)])


def gelu_exact(value):
    return jax.nn.gelu(value, approximate=False)


def wrap_cols(field):
    return jnp.concatenate([field[:, -3:], field, field[:, :3]], axis=1)


def depthwise(padded, kernel_taps, height, across):
    summed = jnp.zeros((height, across, kernel_taps.shape[1]), jnp.float32)
    for offset in range(49):
        window = padded[offset // 7 : offset // 7 + height, offset % 7 : offset % 7 + across]
        summed = summed + window.astype(jnp.float32) * kernel_taps[offset]
    return summed


def depthwise_back(padded_grad, kernel_taps, height, across):
    summed = jnp.zeros((height, across, kernel_taps.shape[1]), jnp.float32)
    for offset in range(49):
        row_start = 6 - offset // 7
        col_start = 6 - offset % 7
        window = padded_grad[row_start : row_start + height, col_start : col_start + across]
        summed = summed + window.astype(jnp.float32) * kernel_taps[offset]
    return summed


def kernel_grad(padded, depth_low, height, across):
    grad_float = depth_low.astype(jnp.float32)
    columns = []
    for offset in range(49):
        window = padded[offset // 7 : offset // 7 + height, offset % 7 : offset % 7 + across]
        columns.append(jnp.sum(window.astype(jnp.float32) * grad_float, axis=(0, 1)))
    return jnp.stack(columns)


def on_device(
    inputs,
    cotangent,
    land,
    kernel,
    bn_gain,
    bn_bias,
    bias_in,
    bias_out,
    w_in,
    w_out,
    resample,
    merge,
):
    batches, height, across, channels = inputs.shape
    hidden_units = bias_in.shape[1]
    is_encoder = lax.axis_index("section") == 0
    kernel_taps = kernel[0]
    norm_gain = bn_gain[0]
    norm_shift = bn_bias[0]
    in_bias = bias_in[0]
    out_bias = bias_out[0]
    gathered_in, gathered_out, gathered_res = (
        lax.all_gather(w_in.astype(jnp.bfloat16), "dp", axis=1, tiled=True),
        lax.all_gather(w_out.astype(jnp.bfloat16), "dp", axis=1, tiled=True),
        lax.all_gather(resample.astype(jnp.bfloat16), "dp", axis=1, tiled=True),
    )
    matrix_in = gathered_in.reshape(channels, hidden_units)
    matrix_out = gathered_out.reshape(hidden_units, channels)
    flat_size = gathered_res.shape[1]
    deep_width = flat_size // (4 * channels)
    down_map = gathered_res.reshape(2, 2 * channels, deep_width)
    up_map = gathered_res.reshape(deep_width, 2, 2 * channels)
    merge_map = lax.all_gather(
        merge.astype(jnp.bfloat16), ("section", "dp"), axis=0, tiled=True
    ).reshape(2 * channels, channels)
    ocean = land.astype(jnp.float32)
    ocean_cells = ocean[:, :, None]
    coarse = jnp.min(land.reshape(height // 2, 2, across // 2, 2), axis=(1, 3)).astype(jnp.float32)[
        :, :, None
    ]
    counted_local = jnp.sum(ocean)
    zero_skip = jnp.zeros((height, across, channels), jnp.bfloat16)
    zero_deep = jnp.zeros((height // 2, across // 2, deep_width), jnp.bfloat16)
    zero_flat = jnp.zeros((flat_size,), jnp.float32)
    zero_merge = jnp.zeros((2 * channels, channels), jnp.float32)

    def decoder_in(deep_recv, skip_recv):
        upsampled = jnp.einsum(
            "abk,kin->aibn", deep_recv, up_map, preferred_element_type=jnp.float32
        )
        upsampled = upsampled.reshape(height, across, channels).astype(jnp.bfloat16)
        joined = jnp.einsum(
            "hwc,cn->hwn", upsampled, merge_map[:channels], preferred_element_type=jnp.float32
        )
        joined = joined + jnp.einsum(
            "hwc,cn->hwn", skip_recv, merge_map[channels:], preferred_element_type=jnp.float32
        )
        return (joined, upsampled)

    def block_input(enc_batch, deep_recv, skip_recv):
        return lax.cond(
            is_encoder,
            lambda: (inputs[enc_batch].astype(jnp.float32), zero_skip),
            lambda: decoder_in(deep_recv, skip_recv),
        )

    def front(source):
        padded = wrap_cols(extended(source.astype(jnp.bfloat16), (("dp", 0),), 3))
        return (padded, depthwise(padded, kernel_taps, height, across))

    def hidden_part(depth_out, mean_value, inverse):
        normed = ((depth_out - mean_value) * inverse * norm_gain + norm_shift).astype(jnp.bfloat16)
        expanded = (
            jnp.einsum("hwc,ce->hwe", normed, matrix_in, preferred_element_type=jnp.float32)
            + in_bias
        )
        activated = gelu_exact(expanded).astype(jnp.bfloat16)
        return (normed, expanded, activated)

    def encoder_out(block_out):
        patches = block_out.reshape(height // 2, 2, across // 2, 2 * channels)
        deep_value = jnp.einsum(
            "aibk,ikn->abn", patches, down_map, preferred_element_type=jnp.float32
        )
        return (coarse * deep_value).astype(jnp.bfloat16)

    skip_recv, deep_recv = (zero_skip, zero_deep)
    records = []
    outputs_step = []
    for moment in range(batches + 1):
        source, upsampled = block_input(min(moment, batches - 1), deep_recv, skip_recv)
        padded, depth_out = front(source)
        ocean_sum, square_sum, counted = lax.psum(
            (
                jnp.sum(depth_out * ocean_cells, axis=(0, 1)),
                jnp.sum(depth_out * depth_out * ocean_cells, axis=(0, 1)),
                counted_local,
            ),
            "dp",
        )
        mean_value = ocean_sum / counted
        inverse = lax.rsqrt(square_sum / counted - mean_value * mean_value + eps_norm)
        normed, expanded, activated = hidden_part(depth_out, mean_value, inverse)
        branch = (
            jnp.einsum("hwe,ec->hwc", activated, matrix_out, preferred_element_type=jnp.float32)
            + out_bias
        )
        block_out = (ocean_cells * (source + branch)).astype(jnp.bfloat16)
        deep_send = lax.cond(is_encoder, lambda: encoder_out(block_out), lambda: zero_deep)
        stored = (deep_recv, skip_recv, mean_value, inverse, counted)
        records.append(stored)
        outputs_step.append(block_out)
        skip_recv, deep_recv = passed_along((block_out, deep_send), "section", 1)
    activations = jnp.stack(
        [
            jnp.where(is_encoder, outputs_step[position], outputs_step[position + 1])
            for position in range(batches)
        ]
    )[None]

    def encoder_back(deep_grad, skip_grad, block_out):
        deep_masked = (deep_grad.astype(jnp.float32) * coarse).astype(jnp.bfloat16)
        patches = block_out.reshape(height // 2, 2, across // 2, 2 * channels)
        resample_part = jnp.einsum(
            "aibk,abn->ikn", patches, deep_masked, preferred_element_type=jnp.float32
        ).reshape(-1)
        spread = jnp.einsum(
            "abn,ikn->aibk", deep_masked, down_map, preferred_element_type=jnp.float32
        )
        return (
            skip_grad.astype(jnp.float32) + spread.reshape(height, across, channels),
            resample_part,
        )

    grad_taps = jnp.zeros((49, channels), jnp.float32)
    grad_gain = jnp.zeros((channels,), jnp.float32)
    grad_shift = jnp.zeros((channels,), jnp.float32)
    grad_bias_in = jnp.zeros((hidden_units,), jnp.float32)
    grad_bias_out = jnp.zeros((channels,), jnp.float32)
    grad_merge_full = zero_merge
    total_in = jnp.zeros((channels, hidden_units), jnp.float32)
    total_out = jnp.zeros((hidden_units, channels), jnp.float32)
    total_res = zero_flat
    grad_recv_skip, grad_recv_deep = (zero_skip, zero_deep)
    input_grads = []
    for moment in range(batches + 1):
        stored = records[batches - moment]
        deep_kept, skip_kept, mean_value, inverse, counted = stored[:5]
        enc_batch = min(batches - moment, batches - 1)
        dec_batch = max(batches - 1 - moment, 0)
        live_scale = jnp.where(
            is_encoder, 1.0 if moment >= 1 else 0.0, 1.0 if moment < batches else 0.0
        )
        source, upsampled = block_input(enc_batch, deep_kept, skip_kept)
        padded, depth_out = front(source)
        normed, expanded, activated = hidden_part(depth_out, mean_value, inverse)
        block_out = outputs_step[batches - moment]
        out_grad, resample_part = lax.cond(
            is_encoder,
            lambda: encoder_back(grad_recv_deep, grad_recv_skip, block_out),
            lambda: (cotangent[dec_batch].astype(jnp.float32), zero_flat),
        )
        out_grad = out_grad * live_scale
        ocean_grad = ocean_cells * out_grad
        branch_grad = ocean_grad.astype(jnp.bfloat16)
        grad_bias_out = grad_bias_out + jnp.sum(branch_grad.astype(jnp.float32), axis=(0, 1))
        step_out = jnp.einsum(
            "hwe,hwc->ec", activated, branch_grad, preferred_element_type=jnp.float32
        )
        act_grad = jnp.einsum(
            "hwc,ec->hwe", branch_grad, matrix_out, preferred_element_type=jnp.float32
        )
        expanded_grad = jax.vjp(gelu_exact, expanded)[1](act_grad)[0].astype(jnp.bfloat16)
        grad_bias_in = grad_bias_in + jnp.sum(expanded_grad.astype(jnp.float32), axis=(0, 1))
        step_in = jnp.einsum(
            "hwc,hwe->ce", normed, expanded_grad, preferred_element_type=jnp.float32
        )
        normed_grad = jnp.einsum(
            "hwe,ce->hwc", expanded_grad, matrix_in, preferred_element_type=jnp.float32
        )
        centered = (depth_out - mean_value) * inverse
        plain_sum, scaled_sum = lax.psum(
            (jnp.sum(normed_grad, axis=(0, 1)), jnp.sum(normed_grad * centered, axis=(0, 1))), "dp"
        )
        grad_shift = grad_shift + plain_sum
        grad_gain = grad_gain + scaled_sum
        depth_grad = inverse * norm_gain * normed_grad + ocean_cells / counted * (
            -inverse * norm_gain * plain_sum
            - inverse * inverse * norm_gain * scaled_sum * (depth_out - mean_value)
        )
        depth_low = depth_grad.astype(jnp.bfloat16)
        grad_taps = grad_taps + kernel_grad(padded, depth_low, height, across)
        grad_padded = wrap_cols(extended(depth_low, (("dp", 0),), 3))
        source_grad = ocean_grad + depthwise_back(grad_padded, kernel_taps, height, across)

        def decoder_back():
            joined_grad = source_grad.astype(jnp.bfloat16)
            merge_part = jnp.concatenate(
                [
                    jnp.einsum(
                        "hwc,hwn->cn", upsampled, joined_grad, preferred_element_type=jnp.float32
                    ),
                    jnp.einsum(
                        "hwc,hwn->cn", skip_kept, joined_grad, preferred_element_type=jnp.float32
                    ),
                ],
                axis=0,
            )
            up_grad = jnp.einsum(
                "hwn,cn->hwc", joined_grad, merge_map[:channels], preferred_element_type=jnp.float32
            ).astype(jnp.bfloat16)
            skip_grad = jnp.einsum(
                "hwn,cn->hwc", joined_grad, merge_map[channels:], preferred_element_type=jnp.float32
            ).astype(jnp.bfloat16)
            up_view = up_grad.reshape(height // 2, 2, across // 2, 2 * channels)
            front_part = jnp.einsum(
                "abk,aibn->kin", deep_kept, up_view, preferred_element_type=jnp.float32
            ).reshape(-1)
            deep_grad = jnp.einsum(
                "aibn,kin->abk", up_view, up_map, preferred_element_type=jnp.float32
            ).astype(jnp.bfloat16)
            return (skip_grad.astype(jnp.float32), front_part, merge_part, skip_grad, deep_grad)

        def encoder_front_back():
            return (source_grad, zero_flat, zero_merge, zero_skip, zero_deep)

        input_grad, front_part, merge_part, skip_send, deep_send = lax.cond(
            is_encoder, encoder_front_back, decoder_back
        )
        step_res = resample_part + front_part
        total_in = total_in + step_in
        total_out = total_out + step_out
        total_res = total_res + step_res
        grad_merge_full = grad_merge_full + merge_part
        input_grads.append(input_grad)
        grad_recv_skip, grad_recv_deep = passed_along((skip_send, deep_send), "section", -1)
    grad_in, grad_out, grad_res = (
        lax.psum_scatter(total_in.reshape(1, -1), "dp", scatter_dimension=1, tiled=True),
        lax.psum_scatter(total_out.reshape(1, -1), "dp", scatter_dimension=1, tiled=True),
        lax.psum_scatter(total_res.reshape(1, -1), "dp", scatter_dimension=1, tiled=True),
    )
    grad_merge = lax.psum_scatter(
        grad_merge_full.reshape(-1), ("section", "dp"), scatter_dimension=0, tiled=True
    )
    grad_taps, grad_bias_in, grad_bias_out = lax.psum(
        (grad_taps, grad_bias_in, grad_bias_out), "dp"
    )
    grad_input = jnp.stack(
        [
            jnp.where(
                is_encoder, input_grads[batches - position], input_grads[batches - 1 - position]
            )
            for position in range(batches)
        ]
    )[None]
    return (
        activations,
        grad_input,
        grad_taps[None],
        grad_gain[None],
        grad_shift[None],
        grad_bias_in[None],
        grad_bias_out[None],
        grad_in,
        grad_out,
        grad_res,
        grad_merge,
    )


def solution(mesh):
    in_specs = (
        P(None, "dp", None, None),
        P(None, "dp", None, None),
        P("dp", None),
        P("section", None, None),
        P("section", None),
        P("section", None),
        P("section", None),
        P("section", None),
        P("section", "dp"),
        P("section", "dp"),
        P("section", "dp"),
        P(("section", "dp")),
    )
    out_specs = (
        P("section", None, "dp", None, None),
        P("section", None, "dp", None, None),
        P("section", None, None),
        P("section", None),
        P("section", None),
        P("section", None),
        P("section", None),
        P("section", "dp"),
        P("section", "dp"),
        P("section", "dp"),
        P(("section", "dp")),
    )
    return jax.shard_map(
        on_device, mesh=mesh, in_specs=in_specs, out_specs=out_specs, check_vma=False
    )
```

profile of v0, /device:TPU:8, one launch (start us, length us, event | category | flops | bytes accessed | tf_op | source)
XLA Modules:
  0.0 2257.5 jit_solution(7815987832772200360)
XLA Ops:
  18.4 152.9 %all-reduce.24.cloned.1.call-done = bf16[320000]{0:T(1024)(128)(2,1)} async-done(((bf16[320000]{0:T(1024)(128)(2,1)}), bf16[320000]{0:T(1024)(128)(2,1)}) %all-reduce.24.cloned.1.call-update) | async-done | bytes 640016
  174.1 54.1 %reduce = bf16[1280000]{0:T(1024)(128)(2,1)S(1)} reduce(bf16[1,1280000]{1,0:T(2,128)(2,1)} %all-gather.2.cloned.1.call-done, bf16[]{:T(256)} %constant.188), dimensions={0}, to_apply=%all_gather.12.reduce_sub_computation | reduce | bytes 5120002 | tf_op jit(solution)/shard_map/all_gather | solution.py:92
  245.0 76.1 %all-reduce.30.cloned.1.call-done = (bf16[640000]{0:T(1024)(128)(2,1)}, bf16[640000]{0:T(1024)(128)(2,1)}) async-done(((bf16[640000]{0:T(1024)(128)(2,1)}, bf16[640000]{0:T(1024)(128)(2,1)}), (bf16[640000]{0:T(1024)(128)(2,1)}, bf16[640000]{0:T(1024)(128)(2,1)})) %all-reduce.30.cloned.1.call-update) | async-done | bytes 2560016
  329.3 7.3 reshape.335
  350.4 15.3 multiply_reduce_fusion.14
  365.7 34.3 %all-reduce.16 = (f32[400]{0:T(512)S(1)}, f32[]{:T(128)}, f32[400]{0:T(512)S(1)}) all-reduce(f32[400]{0:T(512)} %get-tuple-element.827, f32[]{:T(128)} %convert_reduce_fusion.12, f32[400]{0:T(512)} %get-tuple-element.826), channel_id=1, replica_groups=mesh['section'=2,'dp'=16] {'dp'}, use_global_device_ids=true, to_apply=%region_7.0 | all-reduce | flops 801 | bytes 6408 | tf_op jit(solution)/shard_map/psum | solution.py:160
  405.0 11.3 fusion.520
  428.4 13.9 fusion.1160
  467.5 10.7 collective-permute-done.4
  480.8 15.3 multiply_reduce_fusion.12
  496.1 37.3 %all-reduce.15 = (f32[400]{0:T(512)S(1)}, f32[400]{0:T(512)S(1)}) all-reduce(f32[400]{0:T(512)} %get-tuple-element.825, f32[400]{0:T(512)} %get-tuple-element.824), channel_id=1, replica_groups=mesh['section'=2,'dp'=16] {'dp'}, use_global_device_ids=true, to_apply=%region_16.0 | all-reduce | flops 800 | bytes 6400 | tf_op jit(solution)/shard_map/psum | solution.py:160
  538.5 11.3 fusion.525
  562.1 13.1 fusion.1161
  602.9 8.4 collective-permute-done.8
  613.9 14.8 multiply_reduce_fusion.10
  628.6 38.9 %all-reduce.14 = (f32[400]{0:T(512)S(1)}, f32[400]{0:T(512)S(1)}) all-reduce(f32[400]{0:T(512)S(1)} %get-tuple-element.823, f32[400]{0:T(512)S(1)} %get-tuple-element.822), channel_id=1, replica_groups=mesh['section'=2,'dp'=16] {'dp'}, use_global_device_ids=true, to_apply=%region_24.0 | all-reduce | flops 800 | bytes 6400 | tf_op jit(solution)/shard_map/psum | solution.py:160
  672.7 11.4 fusion.530
  696.1 13.1 fusion.1162
  736.7 8.5 collective-permute-done.12
  747.8 14.8 multiply_reduce_fusion.8
  762.6 38.8 %all-reduce.13 = (f32[400]{0:T(512)S(1)}, f32[400]{0:T(512)S(1)}) all-reduce(f32[400]{0:T(512)S(1)} %get-tuple-element.821, f32[400]{0:T(512)S(1)} %get-tuple-element.820), channel_id=1, replica_groups=mesh['section'=2,'dp'=16] {'dp'}, use_global_device_ids=true, to_apply=%region_32.0 | all-reduce | flops 800 | bytes 6400 | tf_op jit(solution)/shard_map/psum | solution.py:160
  806.5 11.4 fusion.535
  829.9 13.1 fusion.1163
  870.6 8.4 collective-permute-done.16
  881.6 13.2 multiply_reduce_fusion.6
  894.8 38.8 %all-reduce.12 = (f32[400]{0:T(512)S(1)}, f32[400]{0:T(512)S(1)}) all-reduce(f32[400]{0:T(512)S(1)} %get-tuple-element.819, f32[400]{0:T(512)S(1)} %get-tuple-element.818), channel_id=1, replica_groups=mesh['section'=2,'dp'=16] {'dp'}, use_global_device_ids=true, to_apply=%region_40.0 | all-reduce | flops 800 | bytes 6400 | tf_op jit(solution)/shard_map/psum | solution.py:160
  942.1 14.6 fusion.1164
  959.1 19.2 fusion.1186
  978.4 13.3 fusion.540
  991.7 26.5 %conditional.33 = (f32[4,160,400]{2,1,0:T(8,128)}, f32[1280000]{0:T(1024)}) conditional(s32[]{:T(128)} %convert_element_type.3001, bf16[4,4,160,400]{3,2,1,0:T(8,128)(2,1)} %param.61, (f32[2,80,1]{1,0,2:T(2,128)S(1)}, bf16[2,800,800]{2,1,0:T(8,128)(2,1)S(1)}, bf16[4,160,400]{2,1,0:T(8,128)(2,1)}) %tuple.734), branch_computations={%region_41.0_spmd, %region_42.0_spmd} | conditional | flops 819200320 | bytes 32769616 | solution.py:225
  1003.1 7.0 copy.92
  1010.2 8.0 reshape.297
  1020.5 51.8 %fusion.321 = (f32[4,160,1600]{2,1,0:T(8,128)}, f32[4,160,1600]{2,1,0:T(8,128)}, f32[4,160,1600]{2,1,0:T(8,128)}, f32[4,160,1600]{2,1,0:T(8,128)}, f32[4,160,1600]{2,1,0:T(8,128)S(1)}) fusion(f32[4,160,1600]{2,1,0:T(8,128)} %get-tuple-element.1115, f32[1600]{0:T(1024)S(1)} %copy-done.531, u8[160,1600]{1,0:T(8,128)(4,1)S(1)} %copy-done.535, ...), kind=kLoop, calls=%fused_computation.554 | loop fusion | flops 344064000 | bytes 43526400 | tf_op jit(solution)/shard_map/jvp()/erfc | solution.py:33
  1081.8 37.2 %all-reduce.11 = (f32[400]{0:T(512)}, f32[400]{0:T(512)}) all-reduce(f32[400]{0:T(512)} %get-tuple-element.857, f32[400]{0:T(512)} %get-tuple-element.856), channel_id=1, replica_groups=mesh['section'=2,'dp'=16] {'dp'}, use_global_device_ids=true, to_apply=%region_48.49 | all-reduce | flops 800 | bytes 6400 | tf_op jit(solution)/shard_map/psum | solution.py:249
  1125.4 7.5 collective-permute-start.21
  1149.0 14.0 fusion.1159
  1182.9 24.8 %conditional.36 = (f32[4,160,400]{2,1,0:T(8,128)S(1)}, f32[1280000]{0:T(1024)}) conditional(s32[]{:T(128)} %convert_element_type.3001, bf16[4,4,160,400]{3,2,1,0:T(8,128)(2,1)} %param.61, (bf16[4,160,400]{2,1,0:T(8,128)(2,1)}, bf16[2,80,800]{2,1,0:T(8,128)(2,1)S(1)}, f32[2,80,1]{1,0,2:T(2,128)S(1)}, bf16[2,800,800]{2,1,0:T(8,128)(2,1)}, ...), branch_computations={%region_51.52_spmd, %region_52.53_spmd} | conditional | flops 820480000 | bytes 35841296 | solution.py:225
  1192.6 7.1 copy.96
  1199.7 8.0 reshape.302
  1218.0 35.1 %all-reduce.10 = (f32[400]{0:T(512)S(1)}, f32[400]{0:T(512)S(1)}) all-reduce(f32[400]{0:T(512)S(1)} %get-tuple-element.855, f32[400]{0:T(512)S(1)} %get-tuple-element.854), channel_id=1, replica_groups=mesh['section'=2,'dp'=16] {'dp'}, use_global_device_ids=true, to_apply=%region_58.59 | all-reduce | flops 800 | bytes 6400 | tf_op jit(solution)/shard_map/psum | solution.py:249
  1282.9 12.7 fusion.1158
  1303.6 7.8 stack.889
  1321.4 24.8 %conditional.39 = (f32[4,160,400]{2,1,0:T(8,128)S(1)}, f32[1280000]{0:T(1024)}) conditional(s32[]{:T(128)} %convert_element_type.3001, bf16[4,4,160,400]{3,2,1,0:T(8,128)(2,1)S(1)} %copy-done.107, (bf16[4,160,400]{2,1,0:T(8,128)(2,1)}, bf16[2,80,800]{2,1,0:T(8,128)(2,1)S(1)}, f32[2,80,1]{1,0,2:T(2,128)S(1)}, bf16[2,800,800]{2,1,0:T(8,128)(2,1)S(1)}, ...), branch_computations={%region_61.62_spmd, %region_62.63_spmd} | conditional | flops 820480000 | bytes 35841296 | solution.py:225
  1331.0 7.1 copy.100
  1338.1 8.1 reshape.307
  1356.4 35.4 %all-reduce.9 = (f32[400]{0:T(512)S(1)}, f32[400]{0:T(512)S(1)}) all-reduce(f32[400]{0:T(512)S(1)} %get-tuple-element.853, f32[400]{0:T(512)S(1)} %get-tuple-element.852), channel_id=1, replica_groups=mesh['section'=2,'dp'=16] {'dp'}, use_global_device_ids=true, to_apply=%region_68.69 | all-reduce | flops 800 | bytes 6400 | tf_op jit(solution)/shard_map/psum | solution.py:249
  1423.1 12.7 fusion.1157
  1443.9 8.5 stack.939
  1463.4 24.7 %conditional.42 = (f32[4,160,400]{2,1,0:T(8,128)S(1)}, f32[1280000]{0:T(1024)}) conditional(s32[]{:T(128)} %convert_element_type.3001, bf16[4,4,160,400]{3,2,1,0:T(8,128)(2,1)S(1)} %copy-done.108, (bf16[4,160,400]{2,1,0:T(8,128)(2,1)}, bf16[2,80,800]{2,1,0:T(8,128)(2,1)S(1)}, f32[2,80,1]{1,0,2:T(2,128)S(1)}, bf16[2,800,800]{2,1,0:T(8,128)(2,1)S(1)}, ...), branch_computations={%region_71.72_spmd, %region_72.73_spmd} | conditional | flops 820480000 | bytes 35841296 | solution.py:225
  1473.0 7.1 copy.104
  1480.0 8.0 reshape.312
  1498.3 35.2 %all-reduce.8 = (f32[400]{0:T(512)S(1)}, f32[400]{0:T(512)S(1)}) all-reduce(f32[400]{0:T(512)S(1)} %get-tuple-element.851, f32[400]{0:T(512)S(1)} %get-tuple-element.850), channel_id=1, replica_groups=mesh['section'=2,'dp'=16] {'dp'}, use_global_device_ids=true, to_apply=%region_78.79 | all-reduce | flops 800 | bytes 6400 | tf_op jit(solution)/shard_map/psum | solution.py:249
  1564.9 12.7 fusion.1156
  1599.8 24.1 %conditional.45 = (f32[4,160,400]{2,1,0:T(8,128)S(1)}, f32[1280000]{0:T(1024)}) conditional(s32[]{:T(128)} %convert_element_type.3001, bf16[4,4,160,400]{3,2,1,0:T(8,128)(2,1)S(1)} %copy-done.109, (bf16[4,160,400]{2,1,0:T(8,128)(2,1)S(1)}, bf16[2,80,800]{2,1,0:T(8,128)(2,1)S(1)}, f32[2,80,1]{1,0,2:T(2,128)S(1)}, ...), branch_computations={%region_81.82_spmd, %region_82.83_spmd} | conditional | flops 820480000 | bytes 37889324 | solution.py:225
  1608.8 7.1 copy.108
  1615.8 8.0 reshape.317
  1630.7 6.6 convolution_bitcast_fusion.20
  1642.8 70.6 %all-reduce.7 = (f32[400]{0:T(512)S(1)}, f32[400]{0:T(512)S(1)}, f32[1,1600]{1,0:T(1,128)}, f32[1,400]{1,0:T(1,128)}) all-reduce(f32[400]{0:T(512)S(1)} %get-tuple-element.849, f32[400]{0:T(512)S(1)} %get-tuple-element.848, f32[1,1600]{1,0:T(1,128)S(1)} %broadcast_in_dim.137, ...), channel_id=1, replica_groups=mesh['section'=2,'dp'=16] {'dp'}, use_global_device_ids=true, to_apply=%region_88.89 | all-reduce | flops 2800 | bytes 22400 | tf_op jit(solution)/shard_map/psum | solution.py:249
  1741.8 9.9 fusion.384
  1764.6 8.1 reshape.337
  1775.8 13.3 fusion.1155
  1802.6 19.5 add_add_fusion
  1833.3 103.8 %all-reduce.26.cloned.1.call-done = f32[320000]{0:T(1024)} async-done(((f32[320000]{0:T(1024)}), f32[320000]{0:T(1024)}) %all-reduce.26.cloned.1.call-update) | async-done | bytes 1280016
  1938.5 306.6 %all-reduce.28.cloned.1.call-done = (f32[1,49,400]{2,0,1:T(1,128)}, f32[1,640000]{1,0:T(1,128)}, f32[1,640000]{1,0:T(1,128)}, f32[1,1280000]{1,0:T(1,128)}) async-done(((f32[1,49,400]{2,0,1:T(1,128)}, f32[1,640000]{1,0:T(1,128)}, f32[1,640000]{1,0:T(1,128)}, f32[1,1280000]{1,0:T(1,128)}), (f32[1,49,400]{2,0,1:T(1,128)}, f32[1,640000]{1,0:T(1,128)}, f32[1,640000]{1,0:T(1,128)}, ...) | async-done | bytes 10318416 | tf_op jit(solution)/shard_map/psum | solution.py:312
  (1708 shorter events, 671.7 us)
Async XLA Ops:
  8.0 163.2 %all-reduce.24.cloned.1.call-start = ((), (), s32[]{:S(2)}) async-start(), calls=%async_computation.1 | async-start | bytes 1282048
  10.3 163.8 %all-gather.2.cloned.1.call-start = ((), (), s32[]{:S(2)}) async-start(), calls=%async_computation | async-start | bytes 5440000 | tf_op jit(solution)/shard_map/all_gather | solution.py:92
  11.4 309.8 %all-reduce.30.cloned.1.call-start = ((), (), s32[]{:S(2)}) async-start(), calls=%async_computation.4 | async-start | bytes 5120000
  16.7 1920.4 %all-reduce.26.cloned.1.call-start = ((), (), s32[]{:S(2)}) async-start(), calls=%async_computation.2 | async-start | bytes 2564096
  174.1 686.3 %copy-start.16 = (bf16[800,400]{1,0:T(8,128)(2,1)}, bf16[800,400]{1,0:T(8,128)(2,1)S(1)}, u32[]{:S(2)}) copy-start(bf16[800,400]{1,0:T(8,128)(2,1)S(1)} %reshape.331) | copy-start | bytes 1920004
  236.1 111.6 %collective-permute-start = (bf16[3,160,400]{2,1,0:T(8,128)(2,1)}, bf16[3,160,400]{2,1,0:T(8,128)(2,1)}, u32[]{:S(2)}, u32[]{:S(2)}) collective-permute-start(bf16[3,160,400]{2,1,0:T(8,128)(2,1)} %get-tuple-element.1036), channel_id=1, source_target_pairs={{0,1},{1,2},{2,3},{3,4},{4,5},{5,6},{6,7},{7,8},{8,9},{9,10},{10,1... | collective-permute-start | bytes 1152008 | tf_op jit(solution)/shard_map/ppermute | solution.py:17
  239.4 108.3 %collective-permute-start.1 = (bf16[3,160,400]{2,1,0:T(8,128)(2,1)}, bf16[3,160,400]{2,1,0:T(8,128)(2,1)}, u32[]{:S(2)}, u32[]{:S(2)}) collective-permute-start(bf16[3,160,400]{2,1,0:T(8,128)(2,1)} %get-tuple-element.1037), channel_id=1, source_target_pairs={{1,0},{2,1},{3,2},{4,3},{5,4},{6,5},{7,6},{8,7},{9,8},{10,9},{11,1... | collective-permute-start | bytes 1152008 | tf_op jit(solution)/shard_map/ppermute | solution.py:19
  329.3 605.5 %copy-start.30 = (bf16[400,1600,1]{1,0,2:T(8,128)(2,1)}, bf16[400,1600,1]{1,0,2:T(8,128)(2,1)S(1)}, u32[]{:S(2)}) copy-start(bf16[400,1600,1]{1,0,2:T(8,128)(2,1)S(1)} %reshape.470) | copy-start | bytes 3840004
  338.6 89.5 %copy-start.56 = (bf16[4,160,400]{2,1,0:T(8,128)(2,1)}, bf16[4,160,400]{2,1,0:T(8,128)(2,1)S(1)}, u32[]{:S(2)}) copy-start(bf16[4,160,400]{2,1,0:T(8,128)(2,1)S(1)} %get-tuple-element.416) | copy-start | bytes 1536004
  339.7 86.0 %collective-permute-start.42 = (bf16[3,160,400]{2,1,0:T(8,128)(2,1)}, bf16[3,160,400]{2,1,0:T(8,128)(2,1)}, u32[]{:S(2)}, u32[]{:S(2)}) collective-permute-start(bf16[3,160,400]{2,1,0:T(8,128)(2,1)} %get-tuple-element.1026), channel_id=1, source_target_pairs={{0,1},{1,2},{2,3},{3,4},{4,5},{5,6},{6,7},{7,8},{8,9},{9,10},{10,1... | collective-permute-start | bytes 1152008 | tf_op jit(solution)/shard_map/ppermute | solution.py:17
  343.4 82.4 %collective-permute-start.43 = (bf16[3,160,400]{2,1,0:T(8,128)(2,1)}, bf16[3,160,400]{2,1,0:T(8,128)(2,1)}, u32[]{:S(2)}, u32[]{:S(2)}) collective-permute-start(bf16[3,160,400]{2,1,0:T(8,128)(2,1)} %get-tuple-element.1027), channel_id=1, source_target_pairs={{1,0},{2,1},{3,2},{4,3},{5,4},{6,5},{7,6},{8,7},{9,8},{10,9},{11,1... | collective-permute-start | bytes 1152008 | tf_op jit(solution)/shard_map/ppermute | solution.py:19
  416.4 25.9 %collective-permute-start.3 = (bf16[4,160,400]{2,1,0:T(8,128)(2,1)}, bf16[4,160,400]{2,1,0:T(8,128)(2,1)}, u32[]{:S(2)}, u32[]{:S(2)}) collective-permute-start(bf16[4,160,400]{2,1,0:T(8,128)(2,1)} %fusion.520), channel_id=1, source_target_pairs={{0,16},{1,17},{2,18},{3,19},{4,20},{5,21},{6,22},{7,23},{8,24},{9,... | collective-permute-start | bytes 1536008 | tf_op jit(solution)/shard_map/ppermute | solution.py:29
  423.7 18.6 collective-permute-start.2
  447.3 30.9 %collective-permute-start.4 = (bf16[3,160,400]{2,1,0:T(8,128)(2,1)}, bf16[3,160,400]{2,1,0:T(8,128)(2,1)}, u32[]{:S(2)}, u32[]{:S(2)}) collective-permute-start(bf16[3,160,400]{2,1,0:T(8,128)(2,1)} %get-tuple-element.1034), channel_id=1, source_target_pairs={{0,1},{1,2},{2,3},{3,4},{4,5},{5,6},{6,7},{7,8},{8,9},{9,10},{10,1... | collective-permute-start | bytes 1152008 | tf_op jit(solution)/shard_map/ppermute | solution.py:17
  449.2 29.0 %collective-permute-start.5 = (bf16[3,160,400]{2,1,0:T(8,128)(2,1)}, bf16[3,160,400]{2,1,0:T(8,128)(2,1)}, u32[]{:S(2)}, u32[]{:S(2)}) collective-permute-start(bf16[3,160,400]{2,1,0:T(8,128)(2,1)} %get-tuple-element.1035), channel_id=1, source_target_pairs={{1,0},{2,1},{3,2},{4,3},{5,4},{6,5},{7,6},{8,7},{9,8},{10,9},{11,1... | collective-permute-start | bytes 1152008 | tf_op jit(solution)/shard_map/ppermute | solution.py:19
  458.4 101.1 %copy-start.47 = (bf16[4,160,400]{2,1,0:T(8,128)(2,1)}, bf16[4,160,400]{2,1,0:T(8,128)(2,1)S(1)}, u32[]{:S(2)}) copy-start(bf16[4,160,400]{2,1,0:T(8,128)(2,1)S(1)} %get-tuple-element.411) | copy-start | bytes 1536004
  459.5 99.9 %collective-permute-start.36 = (bf16[3,160,400]{2,1,0:T(8,128)(2,1)}, bf16[3,160,400]{2,1,0:T(8,128)(2,1)}, u32[]{:S(2)}, u32[]{:S(2)}) collective-permute-start(bf16[3,160,400]{2,1,0:T(8,128)(2,1)} %get-tuple-element.1024), channel_id=1, source_target_pairs={{0,1},{1,2},{2,3},{3,4},{4,5},{5,6},{6,7},{7,8},{8,9},{9,10},{10,1... | collective-permute-start | bytes 1152008 | tf_op jit(solution)/shard_map/ppermute | solution.py:17
  461.7 97.7 %collective-permute-start.37 = (bf16[3,160,400]{2,1,0:T(8,128)(2,1)}, bf16[3,160,400]{2,1,0:T(8,128)(2,1)}, u32[]{:S(2)}, u32[]{:S(2)}) collective-permute-start(bf16[3,160,400]{2,1,0:T(8,128)(2,1)} %get-tuple-element.1025), channel_id=1, source_target_pairs={{1,0},{2,1},{3,2},{4,3},{5,4},{6,5},{7,6},{8,7},{9,8},{10,9},{11,1... | collective-permute-start | bytes 1152008 | tf_op jit(solution)/shard_map/ppermute | solution.py:19
  549.9 25.4 %collective-permute-start.7 = (bf16[4,160,400]{2,1,0:T(8,128)(2,1)}, bf16[4,160,400]{2,1,0:T(8,128)(2,1)}, u32[]{:S(2)}, u32[]{:S(2)}) collective-permute-start(bf16[4,160,400]{2,1,0:T(8,128)(2,1)} %fusion.525), channel_id=1, source_target_pairs={{0,16},{1,17},{2,18},{3,19},{4,20},{5,21},{6,22},{7,23},{8,24},{9,... | collective-permute-start | bytes 1536008 | tf_op jit(solution)/shard_map/ppermute | solution.py:29
  557.2 18.1 collective-permute-start.6
  581.5 29.7 %collective-permute-start.8 = (bf16[3,160,400]{2,1,0:T(8,128)(2,1)}, bf16[3,160,400]{2,1,0:T(8,128)(2,1)}, u32[]{:S(2)}, u32[]{:S(2)}) collective-permute-start(bf16[3,160,400]{2,1,0:T(8,128)(2,1)} %get-tuple-element.1032), channel_id=1, source_target_pairs={{0,1},{1,2},{2,3},{3,4},{4,5},{5,6},{6,7},{7,8},{8,9},{9,10},{10,1... | collective-permute-start | bytes 1152008 | tf_op jit(solution)/shard_map/ppermute | solution.py:17
  583.5 27.8 %collective-permute-start.9 = (bf16[3,160,400]{2,1,0:T(8,128)(2,1)}, bf16[3,160,400]{2,1,0:T(8,128)(2,1)}, u32[]{:S(2)}, u32[]{:S(2)}) collective-permute-start(bf16[3,160,400]{2,1,0:T(8,128)(2,1)} %get-tuple-element.1033), channel_id=1, source_target_pairs={{1,0},{2,1},{3,2},{4,3},{5,4},{6,5},{7,6},{8,7},{9,8},{10,9},{11,1... | collective-permute-start | bytes 1152008 | tf_op jit(solution)/shard_map/ppermute | solution.py:19
  593.8 99.6 %copy-start.49 = (bf16[4,160,400]{2,1,0:T(8,128)(2,1)}, bf16[4,160,400]{2,1,0:T(8,128)(2,1)S(1)}, u32[]{:S(2)}) copy-start(bf16[4,160,400]{2,1,0:T(8,128)(2,1)S(1)} %get-tuple-element.406) | copy-start | bytes 1536004
  594.9 98.5 %collective-permute-start.30 = (bf16[3,160,400]{2,1,0:T(8,128)(2,1)}, bf16[3,160,400]{2,1,0:T(8,128)(2,1)}, u32[]{:S(2)}, u32[]{:S(2)}) collective-permute-start(bf16[3,160,400]{2,1,0:T(8,128)(2,1)} %get-tuple-element.1022), channel_id=1, source_target_pairs={{0,1},{1,2},{2,3},{3,4},{4,5},{5,6},{6,7},{7,8},{8,9},{9,10},{10,1... | collective-permute-start | bytes 1152008 | tf_op jit(solution)/shard_map/ppermute | solution.py:17
  597.1 96.3 %collective-permute-start.31 = (bf16[3,160,400]{2,1,0:T(8,128)(2,1)}, bf16[3,160,400]{2,1,0:T(8,128)(2,1)}, u32[]{:S(2)}, u32[]{:S(2)}) collective-permute-start(bf16[3,160,400]{2,1,0:T(8,128)(2,1)} %get-tuple-element.1023), channel_id=1, source_target_pairs={{1,0},{2,1},{3,2},{4,3},{5,4},{6,5},{7,6},{8,7},{9,8},{10,9},{11,1... | collective-permute-start | bytes 1152008 | tf_op jit(solution)/shard_map/ppermute | solution.py:19
  684.0 25.2 %collective-permute-start.11 = (bf16[4,160,400]{2,1,0:T(8,128)(2,1)}, bf16[4,160,400]{2,1,0:T(8,128)(2,1)}, u32[]{:S(2)}, u32[]{:S(2)}) collective-permute-start(bf16[4,160,400]{2,1,0:T(8,128)(2,1)} %fusion.530), channel_id=1, source_target_pairs={{0,16},{1,17},{2,18},{3,19},{4,20},{5,21},{6,22},{7,23},{8,24},{9,... | collective-permute-start | bytes 1536008 | tf_op jit(solution)/shard_map/ppermute | solution.py:29
  691.4 17.9 collective-permute-start.10
  715.5 29.7 %collective-permute-start.12 = (bf16[3,160,400]{2,1,0:T(8,128)(2,1)}, bf16[3,160,400]{2,1,0:T(8,128)(2,1)}, u32[]{:S(2)}, u32[]{:S(2)}) collective-permute-start(bf16[3,160,400]{2,1,0:T(8,128)(2,1)} %get-tuple-element.1030), channel_id=1, source_target_pairs={{0,1},{1,2},{2,3},{3,4},{4,5},{5,6},{6,7},{7,8},{8,9},{9,10},{10,1... | collective-permute-start | bytes 1152008 | tf_op jit(solution)/shard_map/ppermute | solution.py:17
  717.4 27.8 %collective-permute-start.13 = (bf16[3,160,400]{2,1,0:T(8,128)(2,1)}, bf16[3,160,400]{2,1,0:T(8,128)(2,1)}, u32[]{:S(2)}, u32[]{:S(2)}) collective-permute-start(bf16[3,160,400]{2,1,0:T(8,128)(2,1)} %get-tuple-element.1031), channel_id=1, source_target_pairs={{1,0},{2,1},{3,2},{4,3},{5,4},{6,5},{7,6},{8,7},{9,8},{10,9},{11,1... | collective-permute-start | bytes 1152008 | tf_op jit(solution)/shard_map/ppermute | solution.py:19
  727.7 99.5 %copy-start.51 = (bf16[4,160,400]{2,1,0:T(8,128)(2,1)}, bf16[4,160,400]{2,1,0:T(8,128)(2,1)S(1)}, u32[]{:S(2)}) copy-start(bf16[4,160,400]{2,1,0:T(8,128)(2,1)S(1)} %get-tuple-element.401) | copy-start | bytes 1536004
  728.8 98.4 %collective-permute-start.24 = (bf16[3,160,400]{2,1,0:T(8,128)(2,1)}, bf16[3,160,400]{2,1,0:T(8,128)(2,1)}, u32[]{:S(2)}, u32[]{:S(2)}) collective-permute-start(bf16[3,160,400]{2,1,0:T(8,128)(2,1)} %get-tuple-element.1020), channel_id=1, source_target_pairs={{0,1},{1,2},{2,3},{3,4},{4,5},{5,6},{6,7},{7,8},{8,9},{9,10},{10,1... | collective-permute-start | bytes 1152008 | tf_op jit(solution)/shard_map/ppermute | solution.py:17
  731.0 96.2 %collective-permute-start.25 = (bf16[3,160,400]{2,1,0:T(8,128)(2,1)}, bf16[3,160,400]{2,1,0:T(8,128)(2,1)}, u32[]{:S(2)}, u32[]{:S(2)}) collective-permute-start(bf16[3,160,400]{2,1,0:T(8,128)(2,1)} %get-tuple-element.1021), channel_id=1, source_target_pairs={{1,0},{2,1},{3,2},{4,3},{5,4},{6,5},{7,6},{8,7},{9,8},{10,9},{11,1... | collective-permute-start | bytes 1152008 | tf_op jit(solution)/shard_map/ppermute | solution.py:19
  817.8 25.2 %collective-permute-start.15 = (bf16[4,160,400]{2,1,0:T(8,128)(2,1)}, bf16[4,160,400]{2,1,0:T(8,128)(2,1)}, u32[]{:S(2)}, u32[]{:S(2)}) collective-permute-start(bf16[4,160,400]{2,1,0:T(8,128)(2,1)} %fusion.535), channel_id=1, source_target_pairs={{0,16},{1,17},{2,18},{3,19},{4,20},{5,21},{6,22},{7,23},{8,24},{9,... | collective-permute-start | bytes 1536008 | tf_op jit(solution)/shard_map/ppermute | solution.py:29
  825.2 17.8 collective-permute-start.14
  849.3 29.7 %collective-permute-start.16 = (bf16[3,160,400]{2,1,0:T(8,128)(2,1)}, bf16[3,160,400]{2,1,0:T(8,128)(2,1)}, u32[]{:S(2)}, u32[]{:S(2)}) collective-permute-start(bf16[3,160,400]{2,1,0:T(8,128)(2,1)} %get-tuple-element.1028), channel_id=1, source_target_pairs={{0,1},{1,2},{2,3},{3,4},{4,5},{5,6},{6,7},{7,8},{8,9},{9,10},{10,1... | collective-permute-start | bytes 1152008 | tf_op jit(solution)/shard_map/ppermute | solution.py:17
  851.2 27.8 %collective-permute-start.17 = (bf16[3,160,400]{2,1,0:T(8,128)(2,1)}, bf16[3,160,400]{2,1,0:T(8,128)(2,1)}, u32[]{:S(2)}, u32[]{:S(2)}) collective-permute-start(bf16[3,160,400]{2,1,0:T(8,128)(2,1)} %get-tuple-element.1029), channel_id=1, source_target_pairs={{1,0},{2,1},{3,2},{4,3},{5,4},{6,5},{7,6},{8,7},{9,8},{10,9},{11,1... | collective-permute-start | bytes 1152008 | tf_op jit(solution)/shard_map/ppermute | solution.py:19
  862.6 75.9 %collective-permute-start.18 = (bf16[3,160,400]{2,1,0:T(8,128)(2,1)}, bf16[3,160,400]{2,1,0:T(8,128)(2,1)S(1)}, u32[]{:S(2)}, u32[]{:S(2)}) collective-permute-start(bf16[3,160,400]{2,1,0:T(8,128)(2,1)} %get-tuple-element.1018), channel_id=1, source_target_pairs={{0,1},{1,2},{2,3},{3,4},{4,5},{5,6},{6,7},{7,8},{8,9},{9,10},{10,1... | collective-permute-start | bytes 1152008 | tf_op jit(solution)/shard_map/ppermute | solution.py:17
  864.9 74.5 %collective-permute-start.19 = (bf16[3,160,400]{2,1,0:T(8,128)(2,1)}, bf16[3,160,400]{2,1,0:T(8,128)(2,1)}, u32[]{:S(2)}, u32[]{:S(2)}) collective-permute-start(bf16[3,160,400]{2,1,0:T(8,128)(2,1)} %get-tuple-element.1019), channel_id=1, source_target_pairs={{1,0},{2,1},{3,2},{4,3},{5,4},{6,5},{7,6},{8,7},{9,8},{10,9},{11,1... | collective-permute-start | bytes 1152008 | tf_op jit(solution)/shard_map/ppermute | solution.py:19
  1125.4 14.4 collective-permute-start.21
  1132.9 12.5 collective-permute-start.20
  1168.5 14.5 collective-permute-start.22
  1174.9 8.0 collective-permute-start.23
  1262.8 12.8 collective-permute-start.27
  1266.7 12.7 collective-permute-start.26
  1301.0 20.4 collective-permute-start.28
  1311.4 10.0 collective-permute-start.29
  1401.5 14.3 collective-permute-start.33
  1407.2 12.7 collective-permute-start.32
  1441.4 21.9 collective-permute-start.34
  1452.4 10.9 collective-permute-start.35
  1543.2 14.3 collective-permute-start.39
  1548.9 12.7 collective-permute-start.38
  1583.3 16.5 collective-permute-start.40
  1589.8 10.0 collective-permute-start.41
  1639.8 73.7 %copy-start.666 = (f32[400]{0:T(512)S(1)}, f32[400]{0:T(512)}, u32[]{:S(2)}) copy-start(f32[400]{0:T(512)} %get-tuple-element.913) | copy-start | bytes 4804
  1639.8 73.7 %copy-start.667 = (f32[400]{0:T(512)S(1)}, f32[400]{0:T(512)}, u32[]{:S(2)}) copy-start(f32[400]{0:T(512)} %get-tuple-element.914) | copy-start | bytes 4804
  1639.8 73.7 %copy-start.669 = (f32[400]{0:T(512)S(1)}, f32[400]{0:T(512)}, u32[]{:S(2)}) copy-start(f32[400]{0:T(512)} %copy-done.668) | copy-start | bytes 4804
  1639.8 73.6 %copy-start.671 = (f32[400]{0:T(512)S(1)}, f32[400]{0:T(512)}, u32[]{:S(2)}) copy-start(f32[400]{0:T(512)} %copy-done.670) | copy-start | bytes 4804
  1639.8 73.6 %copy-start.673 = (f32[400]{0:T(512)S(1)}, f32[400]{0:T(512)}, u32[]{:S(2)}) copy-start(f32[400]{0:T(512)} %copy-done.672) | copy-start | bytes 4804
  1639.8 74.2 %copy-start.1 = (bf16[10,163,400]{2,1,0:T(8,128)(2,1)S(1)}, bf16[10,163,400]{2,1,0:T(8,128)(2,1)}, u32[]{:S(2)}) copy-start(bf16[10,163,400]{2,1,0:T(8,128)(2,1)} %copy-done) | copy-start | bytes 3912004
  1639.8 74.2 %copy-start.545 = (f32[4,160]{1,0:T(4,128)S(1)}, f32[4,160]{1,0:T(4,128)}, u32[]{:S(2)}) copy-start(f32[4,160]{1,0:T(4,128)} %broadcast_divide_fusion) | copy-start | bytes 7684
  1735.8 37.2 %collective-permute-start.45 = (bf16[3,160,400]{2,1,0:T(8,128)(2,1)}, bf16[3,160,400]{2,1,0:T(8,128)(2,1)}, u32[]{:S(2)}, u32[]{:S(2)}) collective-permute-start(bf16[3,160,400]{2,1,0:T(8,128)(2,1)} %get-tuple-element.1004), channel_id=1, source_target_pairs={{1,0},{2,1},{3,2},{4,3},{5,4},{6,5},{7,6},{8,7},{9,8},{10,9},{11,1... | collective-permute-start | bytes 1152008 | tf_op jit(solution)/shard_map/ppermute | solution.py:19
  1737.7 35.3 %collective-permute-start.44 = (bf16[3,160,400]{2,1,0:T(8,128)(2,1)}, bf16[3,160,400]{2,1,0:T(8,128)(2,1)}, u32[]{:S(2)}, u32[]{:S(2)}) collective-permute-start(bf16[3,160,400]{2,1,0:T(8,128)(2,1)} %get-tuple-element.1005), channel_id=1, source_target_pairs={{0,1},{1,2},{2,3},{3,4},{4,5},{5,6},{6,7},{7,8},{8,9},{9,10},{10,1... | collective-permute-start | bytes 1152008 | tf_op jit(solution)/shard_map/ppermute | solution.py:17
  1802.5 442.6 %all-reduce.28.cloned.1.call-start = ((), (), s32[]{:S(2)}) async-start(), calls=%async_computation.3 | async-start | bytes 20680704 | tf_op jit(solution)/shard_map/psum | solution.py:312
  (675 other events, 5909.2 us)
Sparse Core Ops, SparseCore 0:
  14.7 156.5 all-reduce.23
  177.8 143.2 all-reduce.29
  1802.7 134.3 all-reduce.25
  1945.0 300.0 all-reduce.27
Sparse Core Ops, SparseCore 1:
  14.2 85.6 all-gather.1
where the time goes:
time: 2280 us; the launch traced here: 2260 us
  waiting for transfers between devices  704 us (31%)
  other arithmetic  496 us (22%)
  blocking collectives  402 us (18%)
  local copies, waits for them, and re-layouts  246 us (11%)
  matrix products  236 us (10%)
  starting transfers between devices  142 us (6%)
  between operations  28.1 us (1%)
    unnamed x8, waiting for transfers between devices  333 us
    psum x1, waiting for transfers between devices, on_device(): lax.psum((grad_taps, grad_bias_in, grad_bias_out), 'dp')  307 us
    psum x5, blocking collectives, on_device(): lax.psum((jnp.sum(normed_grad, axis=(0, 1)), jnp.sum(normed_grad * center...  213 us
    psum x5, blocking collectives, on_device(): lax.psum((jnp.sum(depth_out * ocean_cells, axis=(0, 1)), jnp.sum(depth_ou...  188 us
    ppermute x15, starting transfers between devices, extended(): lax.ppermute(head, axis, [((i + 1) % count, i) for i in range(ends)])  78.9 us
    reduce_sum x5, other arithmetic, on_device(): jnp.sum(depth_out * ocean_cells, axis=(0, 1))  73.4 us
    reduce_sum x20, other arithmetic, kernel_grad(): jnp.sum(window.astype(jnp.float32) * grad_float, axis=(0, 1))  72.2 us
    sub x5, other arithmetic, hidden_part(): depth_out - mean_value  67.9 us
  transfers between devices with their start and end apart: 51, of which 15 were waited for; matrix products, arithmetic and copies ran while one was open for 21% of the time, Pallas kernels for 0%

commit v1 on v0

v1 whole, which is shorter than its diff:
```python
import functools

import jax
import jax.numpy as jnp
import ml_dtypes
import numpy as np
from jax import lax
from jax.experimental import pallas as pl
from jax.experimental.pallas import tpu as pltpu
from jax.sharding import PartitionSpec as P

BF = jnp.bfloat16
F32 = jnp.float32
MESH = pl.DeviceIdType.MESH
ANY = pl.BlockSpec(memory_space=pl.ANY)
VM = pl.BlockSpec(memory_space=pltpu.VMEM)
DMA = pltpu.SemaphoreType.DMA
EPS = 1e-05
GROUPS = 16
MEGA = 1 << 20


def padded(width):
    return -(-(width // GROUPS) // 16) * 16


def selector(rows, cols, pairs):
    out = np.zeros((rows, cols), np.float32)
    for r, c in pairs:
        out[r, c] = 1
    return out.astype(ml_dtypes.bfloat16)


def matrices(channels):
    group, wide = channels // GROUPS, padded(channels)
    spread = selector(channels, GROUPS * wide, [(c, c // group * wide + c % group) for c in range(channels)])
    natural = selector(896, 224, [(i * 128 + q * 8 + p, (p + i) * 16 + q) for i in range(7) for q in range(16) for p in range(8)])

    def place(q, row):
        if row < 0:
            return 128 + q * 3 + row + 3
        return q * 8 + row if row < 8 else 176 + q * 3 + row - 8

    shifts = selector(896, 224, [(i * 128 + q * 8 + p, place(q, p + i - 3)) for i in range(7) for q in range(16) for p in range(8)])
    turn = selector(128, 128, [(q * 8 + p, p * 16 + q) for q in range(16) for p in range(8)])
    edges = selector(96, 128, [(48 * e + q * 3 + k, q * 8 + 5 * e + k) for e in range(2) for q in range(16) for k in range(3)])
    patch = selector(
        256, 256,
        [((i * 2 + j) * 64 + b * 4 + a, (2 * b + j) * 8 + 2 * a + i) for i in range(2) for j in range(2) for b in range(16) for a in range(4)],
    )
    return dict(
        spread=spread, gather=np.ascontiguousarray(spread.T), natural=natural, shifts=shifts, turn=turn,
        back=np.ascontiguousarray(turn.T), edges=edges, patch=patch, unpatch=np.ascontiguousarray(patch.T),
    )


def grow(value, sizes):
    return jnp.pad(value, [(0, n - o) for n, o in zip(sizes, value.shape)])


def pack_in(value, parts, c, h):
    value = value.reshape(parts, c // GROUPS, GROUPS, h // GROUPS)
    return grow(value, (parts, padded(c), GROUPS, padded(h))).reshape(parts, padded(c), -1)


def pack_down(value, parts, c, n):
    value = value.reshape(parts, 4, c // GROUPS, GROUPS, n // GROUPS)
    return grow(value, (parts, 4, padded(c), GROUPS, padded(n))).reshape(parts, 4 * padded(c), -1)


def pack_up(value, parts, c, n):
    value = value.reshape(parts, n // GROUPS, 2, 2 * GROUPS, c // GROUPS)
    value = grow(value, (parts, padded(n), 2, 2 * GROUPS, padded(c)))
    return value.transpose(0, 2, 1, 3, 4).reshape(parts, 2 * padded(n), -1)


def unpack_in(value, c, h):
    value = value.reshape(-1, padded(c), GROUPS, padded(h))
    return value[:, : c // GROUPS, :, : h // GROUPS].reshape(-1)


def unpack_down(value, c, n):
    value = value.reshape(-1, 4, padded(c), GROUPS, padded(n))
    return value[:, :, : c // GROUPS, :, : n // GROUPS].reshape(-1)


def unpack_up(value, c, n):
    value = value.reshape(-1, 2, padded(n), 2 * GROUPS, padded(c))
    return value.transpose(0, 2, 1, 3, 4)[:, : n // GROUPS, :, :, : c // GROUPS].reshape(-1)


def where_am_i():
    s, d = lax.axis_index("section"), lax.axis_index("dp")
    return s, d, d // 4, d % 4, 2 * (d // 4) + s


def greet(peers):
    barrier = pltpu.get_barrier_semaphore()
    for peer in peers:
        pl.semaphore_signal(barrier, inc=1, device_id=peer, device_id_type=MESH)
    pl.semaphore_wait(barrier, len(peers))


def greet_line(count):
    s, d, g, m, p = where_am_i()
    barrier = pltpu.get_barrier_semaphore()

    def one(k, carry):
        q = (p + k) % count
        pl.semaphore_signal(barrier, inc=1, device_id=(q % 2, 4 * (q // 2) + m), device_id_type=MESH)
        return carry

    lax.fori_loop(1, count, one, 0)
    pl.semaphore_wait(barrier, count - 1)


def greet_all(sections, dps):
    s, d, g, m, p = where_am_i()
    barrier = pltpu.get_barrier_semaphore()
    me, count = s * dps + d, sections * dps

    def one(k, carry):
        q = (me + k) % count
        pl.semaphore_signal(barrier, inc=1, device_id=(q // dps, q % dps), device_id_type=MESH)
        return carry

    lax.fori_loop(1, count, one, 0)
    pl.semaphore_wait(barrier, count - 1)


def remote(src, dst, send, recv, peer):
    return pltpu.make_async_remote_copy(src_ref=src, dst_ref=dst, send_sem=send, recv_sem=recv, device_id=peer, device_id_type=MESH)


def arrived(ref, sem):
    pltpu.make_async_copy(ref, ref, sem).wait()


def all_sum(mine, slots, send, recv, count):
    s, d, g, m, p = where_am_i()

    def copy(k):
        q = (p + k) % count
        return remote(mine, slots.at[p], send.at[k], recv.at[k], (q % 2, 4 * (q // 2) + m))

    lax.fori_loop(1, count, lambda k, c: (copy(k).start(), c)[1], 0)
    slots[p] = mine[...]

    def wait(k, carry):
        arrived(slots.at[(p + count - k) % count], recv.at[k])
        copy(k).wait_send()
        return carry

    lax.fori_loop(1, count, wait, 0)
    return lax.fori_loop(0, count, lambda k, total: total + slots[k], jnp.zeros(mine.shape, F32))


def swap_rows(packed, halo, send, recv, count):
    s, d, g, m, p = where_am_i()

    def peer(q):
        return (q % 2, 4 * (q // 2) + m)

    @pl.when(p > 0)
    def _():
        remote(packed.at[0], halo.at[1], send.at[0], recv.at[1], peer(p - 1)).start()

    @pl.when(p < count - 1)
    def _():
        remote(packed.at[1], halo.at[0], send.at[1], recv.at[0], peer(p + 1)).start()

    @pl.when(p > 0)
    def _():
        arrived(halo.at[0], recv.at[0])
        remote(packed.at[0], halo.at[1], send.at[0], recv.at[1], peer(p - 1)).wait_send()

    @pl.when(p < count - 1)
    def _():
        arrived(halo.at[1], recv.at[1])
        remote(packed.at[1], halo.at[0], send.at[1], recv.at[0], peer(p + 1)).wait_send()

    @pl.when(p == 0)
    def _():
        halo[0] = jnp.zeros(halo.shape[1:], BF)

    @pl.when(p == count - 1)
    def _():
        halo[1] = jnp.zeros(halo.shape[1:], BF)


def dot(a, b):
    return jnp.dot(a, b, preferred_element_type=F32)


def dot_nt(a, b):
    return lax.dot_general(a, b, (((1,), (1,)), ((), ())), preferred_element_type=F32)


def dot_tn(a, b):
    return lax.dot_general(a, b, (((0,), (0,)), ((), ())), preferred_element_type=F32)


def lanes4(mask, width):
    return jnp.concatenate([mask] * (width // 128), axis=1)


def rows8(value):
    return value.reshape(-1, 8, value.shape[-1]).sum(0)


def to_natural(cells, back, gather):
    turned = dot(dot(back, cells).astype(BF), gather).astype(BF)
    return turned.reshape(8, 16, turned.shape[-1])


def shifted(chunk, perm, S, c):
    moved = dot(perm, chunk)
    for lane in range(S.shape[1]):
        S[:, lane, pl.ds(3 + 16 * c, 16)] = moved[:, lane * 128 : lane * 128 + 128].reshape(7, 16, 8, 128)
    return moved


def wrap(S, cols):
    S[:, :, 0:3] = S[:, :, cols : cols + 3]
    S[:, :, cols + 3 : cols + 6] = S[:, :, 3:6]


def taps_to(kb, par, flip):
    for k in range(49):
        kb[k] = jnp.broadcast_to(par[(48 - k if flip else k) : (48 - k if flip else k) + 1], kb.shape[1:])


def conv_tail(S, kb, ocean, z, stats, slots, out, send, recv, count, cols):
    wide = kb.shape[2]
    tally = jnp.zeros((8, 128), F32)
    tally = lax.fori_loop(0, cols // 8, lambda b, t: t + ocean[pl.ds(b * 8, 8)].sum(0), tally)
    for lane in range(wide // 128):
        at = slice(lane * 128, lane * 128 + 128)

        def step(b, carry):
            first, second = carry
            acc = jnp.zeros((8, 8, 128), F32)
            for i in range(7):
                window = S[i, lane, pl.ds(b * 8, 14)]
                for j in range(7):
                    acc = acc + window[j : j + 8] * kb[7 * i + j, :, at][None]
            z[pl.ds(b * 8, 8), :, at] = acc
            kept = acc * ocean[pl.ds(b * 8, 8)]
            return first + kept.sum(0), second + (kept * acc).sum(0)

        zero = jnp.zeros((8, 128), F32)
        first, second = lax.fori_loop(0, cols // 8, step, (zero, zero))
        stats[0:1, at] = first.sum(0, keepdims=True)
        stats[1:2, at] = second.sum(0, keepdims=True)
        stats[2:3, at] = tally.sum(0, keepdims=True)
        stats[3:8, at] = jnp.zeros((5, 128), F32)
    out[...] = all_sum(stats, slots, send, recv, count)


def enc_conv_kernel(count, cols, x14, spread, natural, par, ocean, z, a, out, S, kb, stats, slots, send, recv):
    greet_line(count)
    taps_to(kb, par, False)

    def chunk(c, carry):
        block = x14[:, c]
        block = dot(block.reshape(-1, block.shape[-1]), spread[...]).astype(BF)
        moved = shifted(block, natural[...], S, c)
        a[pl.ds(pl.multiple_of(c * 128, 128), 128)] = moved[384:512].astype(BF)
        return carry

    lax.fori_loop(0, cols // 16, chunk, 0)
    wrap(S, cols)
    conv_tail(S, kb, ocean, z, stats, slots, out, send, recv, count, cols)


def dec_conv_kernel(count, cols, a, halo, shifts, par, ocean, z, out, S, kb, stats, slots, send, recv):
    greet_line(count)
    taps_to(kb, par, False)

    def chunk(c, carry):
        block = jnp.concatenate([a[pl.ds(pl.multiple_of(c * 128, 128), 128)], halo[0, c], halo[1, c]], axis=0)
        shifted(block, shifts[...], S, c)
        return carry

    lax.fori_loop(0, cols // 16, chunk, 0)
    wrap(S, cols)
    conv_tail(S, kb, ocean, z, stats, slots, out, send, recv, count, cols)


def norm_terms(st, par):
    counted = st[2:3]
    mean = st[0:1] / counted
    inverse = lax.rsqrt(st[1:2] / counted - mean * mean + EPS)
    return counted, mean, inverse, par[49:50], par[50:51]


def ff_kernel(z, st, par, bias, w1, w2, res, ocean, back, gather, n, g, gp, y, nat):
    counted, mean, inverse, gain, shift = norm_terms(st, par)
    normed = ((z[...] - mean) * inverse * gain + shift).astype(BF)
    n[...] = normed
    acc = jnp.zeros(z.shape, F32)
    for h in range(0, w1.shape[1], 256):
        at = slice(h, h + 256)
        e = dot(normed, w1[:, at]) + bias[0:1, at]
        phi = 0.5 + 0.5 * lax.erf(e * np.float32(0.5**0.5))
        act = (e * phi).astype(BF)
        g[:, at] = act
        gp[:, at] = (phi + e * (np.float32((2 * np.pi) ** -0.5) * jnp.exp(-0.5 * e * e))).astype(BF)
        acc = acc + dot(act, w2[at])
    mask = lanes4(ocean[...], z.shape[1])
    out = (mask * (res[...].astype(F32) + (acc + par[51:52]))).astype(BF)
    y[...] = out
    for k in range(2):
        nat[:, k] = to_natural(out[128 * k : 128 * k + 128], back[...], gather[...])


def mid_kernel(count, skip, down, up_w, merge, coarse, patch, unpatch, edges, pieces, deep, up, h, a, halo, packed, send, recv):
    s, d, g, m, p = where_am_i()
    barrier = pltpu.get_barrier_semaphore()

    def peer(q):
        return (q % 2, 4 * (q // 2) + m)

    @pl.when(p > 0)
    def _():
        pl.semaphore_signal(barrier, inc=1, device_id=peer(p - 1), device_id_type=MESH)

    @pl.when(p < count - 1)
    def _():
        pl.semaphore_signal(barrier, inc=1, device_id=peer(p + 1), device_id_type=MESH)

    pl.semaphore_wait(barrier, jnp.where(p > 0, 1, 0) + jnp.where(p < count - 1, 1, 0))
    wide = skip.shape[1]
    blocks = skip.shape[0] // 256
    for b in range(blocks):
        moved = dot(patch[...], skip[256 * b : 256 * b + 256]).astype(BF)
        for k in range(4):
            pieces[k, 64 * b : 64 * b + 64] = moved[64 * k : 64 * k + 64]
    value = sum(dot(pieces[k], down[wide * k : wide * k + wide]) for k in range(4))
    deep_value = (lanes4(coarse[...], value.shape[1]) * value).astype(BF)
    deep[...] = deep_value
    rows = up_w.shape[0] * up_w.shape[2]
    lifted = [dot(deep_value, up_w[:, i].reshape(rows, -1)).astype(BF) for i in range(2)]
    for b in range(blocks):
        stacked = jnp.concatenate(
            [lifted[i][64 * b : 64 * b + 64, wide * j : wide * j + wide] for i in range(2) for j in range(2)], axis=0
        )
        up[256 * b : 256 * b + 256] = dot(unpatch[...], stacked).astype(BF)
    for b in range(blocks):
        at = slice(256 * b, 256 * b + 256)
        joined = dot(up[at], merge[0]) + dot(skip[at], merge[1])
        h[at] = joined
        low = joined.astype(BF)
        a[at] = low
        for k in range(2):
            ends = dot(edges[...], low[128 * k : 128 * k + 128]).astype(BF)
            packed[0, 2 * b + k] = ends[:48]
            packed[1, 2 * b + k] = ends[48:]
    swap_rows(packed, halo, send, recv, count)


def back_ff_kernel(
    count, natural_grad, top, z, st, par, w1, w2, n, g, gp, ocean, spread, turn, edges,
    dym, dw1, dw2, small, dz, halo, dn, dr, packed, stats, slots, send, recv, hsend, hrecv,
):
    greet_line(count)
    wide = z.shape[1]
    chunks = z.shape[0] // 128
    counted, mean, inverse, gain, shift = norm_terms(st, par)

    def begin(c, total):
        at = pl.ds(pl.multiple_of(c * 128, 128), 128)
        if natural_grad:
            block = top[:, c]
            block = dot(block.reshape(-1, block.shape[-1]), spread[...]).astype(BF)
            grad = dot(turn[...], block)
        else:
            grad = top[at]
        grad = grad * lanes4(ocean[at], wide)
        dym[at] = grad
        low = grad.astype(BF)
        dr[at] = low
        return total + rows8(low.astype(F32))

    total = lax.fori_loop(0, chunks, begin, jnp.zeros((8, wide), F32))
    small[2:3] = total.sum(0, keepdims=True)
    small[3:8] = jnp.zeros((5, wide), F32)
    for h in range(0, w1.shape[1], 256):
        at = slice(h, h + 256)
        dg = dot_nt(dr[...], w2[at])
        de = (dg * gp[:, at].astype(F32)).astype(BF)
        row, col = 3 + h // wide, h % wide
        small[row : row + 1, col : col + 256] = de.astype(F32).sum(0, keepdims=True)
        dw1[:, at] = dot_tn(n[...], de).astype(BF)
        dw2[at] = dot_tn(g[:, at], dr[...]).astype(BF)
        part = dot_nt(de, w1[:, at])
        if h == 0:
            dn[...] = part
        else:
            dn[...] += part

    def sums(c, carry):
        at = pl.ds(pl.multiple_of(c * 128, 128), 128)
        grad = dn[at]
        return carry[0] + rows8(grad), carry[1] + rows8(grad * ((z[at] - mean) * inverse))

    zero = jnp.zeros((8, wide), F32)
    plain, scaled = lax.fori_loop(0, chunks, sums, (zero, zero))
    small[0:1] = plain.sum(0, keepdims=True)
    small[1:2] = scaled.sum(0, keepdims=True)
    stats[...] = small[...]
    summed = all_sum(stats, slots, send, recv, count)
    first = -inverse * gain * summed[0:1] / counted
    second = -inverse * inverse * gain * summed[1:2] / counted

    def end(c, carry):
        at = pl.ds(pl.multiple_of(c * 128, 128), 128)
        grad = inverse * gain * dn[at] + lanes4(ocean[at], wide) * (first + second * (z[at] - mean))
        low = grad.astype(BF)
        dz[at] = low
        ends = dot(edges[...], low).astype(BF)
        packed[0, c] = ends[:48]
        packed[1, c] = ends[48:]
        return carry

    lax.fori_loop(0, chunks, end, 0)
    swap_rows(packed, halo, hsend, hrecv, count)


def back_conv_kernel(cols, natural_out, dz, halo, shifts, par, dym, a, back, gather, dh, dk, S, kb, acc_dk):
    taps_to(kb, par, True)
    wide = dz.shape[1]

    def chunk(c, carry):
        block = jnp.concatenate([dz[pl.ds(pl.multiple_of(c * 128, 128), 128)], halo[0, c], halo[1, c]], axis=0)
        shifted(block, shifts[...], S, c)
        return carry

    lax.fori_loop(0, cols // 16, chunk, 0)
    wrap(S, cols)
    acc_dk[...] = jnp.zeros(acc_dk.shape, F32)
    for lane in range(wide // 128):
        at = slice(lane * 128, lane * 128 + 128)

        def step(b, carry):
            cells = pl.ds(pl.multiple_of(b * 64, 64), 64)
            acc = dym[cells, at].reshape(8, 8, 128)
            field = a[cells, at].astype(F32).reshape(8, 8, 128)
            for i in range(7):
                window = S[i, lane, pl.ds(b * 8, 14)]
                for j in range(7):
                    acc = acc + window[j : j + 8] * kb[7 * i + j, :, at][None]
                    acc_dk[7 * i + j, :, at] += (window[j : j + 8] * field).sum(0)
            dh[cells, at] = acc.reshape(64, 128).astype(BF)
            return carry

        lax.fori_loop(0, cols // 8, step, 0)
    for k in range(49):
        dk[48 - k : 49 - k] = acc_dk[k].sum(0, keepdims=True)
    dk[49:56] = jnp.zeros((7, wide), F32)
    if natural_out is not None:

        def out(c, carry):
            cells = dh[pl.ds(pl.multiple_of(c * 128, 128), 128)]
            natural_out[:, c] = to_natural(cells, back[...], gather[...])
            return carry

        lax.fori_loop(0, cols // 16, out, 0)


def back_mid_kernel(dh, up, skip, deep, pieces, down, up_w, merge, coarse, patch, unpatch, back, gather,
                    dmerge, dup_w, ddown, dy, nat, dskip, dups, spreads):
    wide = dh.shape[1]
    blocks = dh.shape[0] // 256
    dmerge[0] = dot_tn(up[...], dh[...]).astype(BF)
    dmerge[1] = dot_tn(skip[...], dh[...]).astype(BF)
    for b in range(blocks):
        at = slice(256 * b, 256 * b + 256)
        low = dot_nt(dh[at], merge[1]).astype(BF)
        dskip[at] = low
        for k in range(2):
            nat[:, 2 * b + k] = to_natural(low[128 * k : 128 * k + 128], back[...], gather[...])
        lifted = dot_nt(dh[at], merge[0]).astype(BF)
        moved = dot(patch[...], lifted).astype(BF)
        for k in range(4):
            dups[k // 2, 64 * b : 64 * b + 64, wide * (k % 2) : wide * (k % 2) + wide] = moved[64 * k : 64 * k + 64]
    rows = up_w.shape[0] * up_w.shape[2]
    ddeep = dot_nt(dups[0], up_w[:, 0].reshape(rows, -1)) + dot_nt(dups[1], up_w[:, 1].reshape(rows, -1))
    for i in range(2):
        grad = dot_tn(deep[...], dups[i]).astype(BF)
        dup_w[:, i] = grad.reshape(up_w.shape[0], up_w.shape[2], -1)
    masked = (lanes4(coarse[...], ddeep.shape[1]) * ddeep).astype(BF)
    for k in range(4):
        ddown[wide * k : wide * k + wide] = dot_tn(pieces[k], masked).astype(BF)
        spreads[k] = dot_nt(masked, down[wide * k : wide * k + wide])
    for b in range(blocks):
        value = jnp.concatenate([spreads[k, 64 * b : 64 * b + 64] for k in range(4)], axis=0)
        high = value.astype(BF)
        rest = (value - high.astype(F32)).astype(BF)
        at = slice(256 * b, 256 * b + 256)
        dy[at] = dskip[at].astype(F32) + (dot(unpatch[...], high) + dot(unpatch[...], rest))


def share_kernel(sections, dps, x, cot, land, par, bias, zero, x14, cot8, land2, par2, bias2, xs, xr, hs, hr, cs, cr, ls, lr, ps, pr):
    s, d, g, m, p = where_am_i()
    count = 2 * (dps // 4)
    greet_all(sections, dps)
    pos, j = d // 2, d % 2

    def move(started, cond, src, dst, send, recv, peer):
        self = (peer[0] == s) & (peer[1] == d)
        far = remote(src, dst, send, recv, peer)
        pl.when(cond & jnp.logical_not(self))(lambda: far.start())
        pl.when(cond & self)(lambda: pltpu.make_async_copy(src, dst, recv).start())
        started.append((cond & jnp.logical_not(self), far))

    started = []
    yes = d >= 0
    for k in range(2):
        mb = 2 * k + s
        to = (pos % 2, 4 * (pos // 2) + mb)
        move(started, yes, x.at[mb], x14.at[pl.ds(3 + 4 * j, 4)], xs.at[k], xr.at[j], to)
        move(started, yes, cot.at[mb], cot8.at[pl.ds(4 * j, 4)], cs.at[k], cr.at[j], to)
        move(started, yes, land, land2.at[j], ls.at[k], lr.at[j], to)
        above, below = pos - 1, pos + 1
        move(started, (j == 0) & (pos > 0), x.at[mb, pl.ds(0, 3)], x14.at[pl.ds(11, 3)], hs.at[k], hr.at[1], (above % 2, 4 * (above // 2) + mb))
        move(started, (j == 1) & (pos < count - 1), x.at[mb, pl.ds(1, 3)], x14.at[pl.ds(0, 3)], hs.at[k], hr.at[0], (below % 2, 4 * (below // 2) + mb))
    pl.when(p == 0)(lambda: pltpu.make_async_copy(zero, x14.at[pl.ds(0, 3)], hr.at[0]).start())
    pl.when(p == count - 1)(lambda: pltpu.make_async_copy(zero, x14.at[pl.ds(11, 3)], hr.at[1]).start())
    other = (1 - s, d)
    far = [remote(par, par2.at[s], ps.at[0], pr.at[0], other), remote(bias, bias2.at[s], ps.at[1], pr.at[1], other)]
    near = [pltpu.make_async_copy(par, par2.at[s], ps.at[2]), pltpu.make_async_copy(bias, bias2.at[s], ps.at[3])]
    for c in far + near:
        c.start()
    for jj in range(2):
        arrived(x14.at[pl.ds(3 + 4 * jj, 4)], xr.at[jj])
        arrived(cot8.at[pl.ds(4 * jj, 4)], cr.at[jj])
        arrived(land2.at[jj], lr.at[jj])
    arrived(x14.at[pl.ds(0, 3)], hr.at[0])
    arrived(x14.at[pl.ds(11, 3)], hr.at[1])
    arrived(par2.at[1 - s], pr.at[0])
    arrived(bias2.at[1 - s], pr.at[1])
    for c in far:
        c.wait_send()
    for c in near:
        c.wait()
    for cond, c in started:
        pl.when(cond)(lambda c=c: c.wait_send())


def gather_kernel(*refs):
    ins, outs = refs[:4], refs[4:8]
    own, zs, zr, as_, ar, bs, br, cs, cr = refs[8:]
    s, d, g, m, p = where_am_i()
    greet_all(2, 16)
    zc, others = d // 4, []
    local, far_z = [], []
    for k in range(4):
        local.append(pltpu.make_async_copy(ins[k], outs[k].at[s, zc, m], own.at[k]))
        local[-1].start()
        for step in range(1, 4):
            peer = (s, 4 * ((zc + step) % 4) + m)
            far_z.append(remote(ins[k], outs[k].at[s, zc, m], zs.at[k, step], zr.at[k, step], peer))
            far_z[-1].start()
    first, second, last = [], [], []

    def hand_over(k, col, index):
        c = remote(outs[k].at[s, :, col], outs[k].at[s, :, col], cs.at[k, index], cr.at[k, index], (1 - s, d))
        c.start()
        last.append(c)

    for k in range(4):
        bit = 1 if k < 2 else 2
        local[k].wait()
        for step in range(1, 4):
            arrived(outs[k].at[s, (zc + 4 - step) % 4, m], zr.at[k, step])
        first.append(remote(outs[k].at[s, :, m], outs[k].at[s, :, m], as_.at[k], ar.at[k], (s, d ^ bit)))
        first[-1].start()
        second.append(remote(outs[k].at[s, :, m], outs[k].at[s, :, m], bs.at[k, 0], br.at[k, 0], (s, d ^ (3 - bit))))
        second[-1].start()
        hand_over(k, m, 0)
    for k in range(4):
        bit = 1 if k < 2 else 2
        arrived(outs[k].at[s, :, m ^ bit], ar.at[k])
        second.append(remote(outs[k].at[s, :, m ^ bit], outs[k].at[s, :, m ^ bit], bs.at[k, 1], br.at[k, 1], (s, d ^ (3 - bit))))
        second[-1].start()
        hand_over(k, m ^ bit, 1)
    for k in range(4):
        bit = 1 if k < 2 else 2
        arrived(outs[k].at[s, :, m ^ (3 - bit)], br.at[k, 0])
        hand_over(k, m ^ (3 - bit), 2)
        arrived(outs[k].at[s, :, m ^ 3], br.at[k, 1])
        hand_over(k, m ^ 3, 3)
    for k in range(4):
        bit = 1 if k < 2 else 2
        for index, col in enumerate((m, m ^ bit, m ^ (3 - bit), m ^ 3)):
            arrived(outs[k].at[1 - s, :, col], cr.at[k, index])
    for c in far_z + first + second + last:
        c.wait_send()


def deliver_kernel(dps, a0, a1, g0, g1, act, gi, send, recv):
    s, d, g, m, p = where_am_i()
    greet_all(2, dps)
    started = []
    for sec in range(2):
        for q, (src, dst) in enumerate((((a0, a1)[sec], act), ((g0, g1)[sec], gi))):
            for j in range(2):
                dp = 4 * g + 2 * s + j
                self = (s == sec) & (d == dp)
                part = src.at[pl.ds(4 * j, 4)]
                far = remote(part, dst.at[m], send.at[sec, q, j], recv.at[q, m], (sec, dp))
                pl.when(jnp.logical_not(self))(lambda far=far: far.start())
                pl.when(self)(lambda part=part, dst=dst, q=q: pltpu.make_async_copy(part, dst.at[m], recv.at[q, m]).start())
                started.append((jnp.logical_not(self), far))
    for q, dst in enumerate((act, gi)):
        for mb in range(4):
            arrived(dst.at[mb], recv.at[q, mb])
    for cond, far in started:
        pl.when(cond)(lambda far=far: far.wait_send())


def reduce_kernel(*refs):
    enc, dec, merge, small = refs[:3], refs[3:6], refs[6], refs[7]
    outs, small_out = refs[8:12], refs[12]
    own, core, plane1, plane2, line = refs[13:17], refs[17:21], refs[21:25], refs[25:29], refs[29:33]
    tiny, ls, cs, cr, as_, ar, bs, br, zs, zr, ts, tr = refs[33:]
    s, d, g, m, p = where_am_i()
    greet_all(2, 16)
    other = (1 - s, d)
    for k in range(4):
        for sec in range(2):

            @pl.when(s == sec)
            def _(k=k, sec=sec):
                mine = (enc, dec)[sec][k] if k < 3 else merge.at[sec]
                theirs = (enc, dec)[1 - sec][k] if k < 3 else merge.at[1 - sec]
                pltpu.make_async_copy(mine, own[k], ls.at[k]).start()
                remote(theirs, core[k], cs.at[k], cr.at[k], other).start()

    def theirs_of(k):
        return enc[k] if k < 3 else merge.at[0]

    t0 = remote(small.at[1 - s], tiny.at[0], ts.at[0], tr.at[0], other)
    t0.start()
    arrived(tiny.at[0], tr.at[0])
    t0.wait_send()
    tiny[1] = small[s] + tiny[0]
    sent = []
    for step in range(1, 4):
        sent.append(remote(tiny.at[1], tiny.at[1 + step], ts.at[step], tr.at[step], (s, 4 * ((g + step) % 4) + m)))
        sent[-1].start()
    for step in range(1, 4):
        arrived(tiny.at[1 + step], tr.at[step])
    for c in sent:
        c.wait_send()
    tiny[5] = tiny[1] + tiny[2] + tiny[3] + tiny[4]
    sent = []
    for step in range(1, 4):
        sent.append(remote(tiny.at[5], tiny.at[5 + step], ts.at[3 + step], tr.at[3 + step], (s, d ^ step)))
        sent[-1].start()
    for step in range(1, 4):
        arrived(tiny.at[5 + step], tr.at[3 + step])
    for c in sent:
        c.wait_send()
    small_out[...] = tiny[5] + tiny[6] + tiny[7] + tiny[8]

    sent = []
    for k in range(4):
        bit = 1 if k < 2 else 2
        pltpu.make_async_copy(own[k], own[k], ls.at[k]).wait()
        arrived(core[k], cr.at[k])

        def add(b, carry, k=k):
            own[k][b // 4, b % 4] = (own[k][b // 4, b % 4].astype(F32) + core[k][b // 4, b % 4].astype(F32)).astype(BF)
            return carry

        lax.fori_loop(0, 16, add, 0)
        for index, col in enumerate((m ^ bit, m ^ 3)):
            sent.append(remote(own[k].at[:, col], plane1[k].at[:, index], as_.at[k, index], ar.at[k, index], (s, d ^ bit)))
            sent[-1].start()
    for k in range(4):
        bit = 1 if k < 2 else 2
        rest = m ^ (3 - bit)
        arrived(plane1[k].at[:, 1], ar.at[k, 1])
        for z in range(4):
            own[k][z, rest] = (own[k][z, rest].astype(F32) + plane1[k][z, 1].astype(F32)).astype(BF)
        sent.append(remote(own[k].at[:, rest], plane2[k], bs.at[k], br.at[k], (s, d ^ (3 - bit))))
        sent[-1].start()
    for k in range(4):
        arrived(plane1[k].at[:, 0], ar.at[k, 0])
        arrived(plane2[k], br.at[k])
        for z in range(4):
            own[k][z, m] = (own[k][z, m].astype(F32) + plane1[k][z, 0].astype(F32) + plane2[k][z].astype(F32)).astype(BF)
        for step in range(1, 4):
            to = (g + step) % 4
            sent.append(remote(own[k].at[to, m], line[k].at[step - 1], zs.at[k, step], zr.at[k, step], (s, 4 * to + m)))
            sent[-1].start()
    for k in range(4):
        for step in range(1, 4):
            arrived(line[k].at[step - 1], zr.at[k, step])
        outs[k][...] = own[k][g, m].astype(F32) + line[k][0].astype(F32) + line[k][1].astype(F32) + line[k][2].astype(F32)
    for c in sent:
        c.wait_send()
    for k in range(4):
        remote(theirs_of(k), core[k], cs.at[k], cr.at[k], other).wait_send()


def call(name, body, outs, ins=None, out_specs=None, scratch=(), cid=None, limit=56, **more):
    params = dict(vmem_limit_bytes=limit * MEGA)
    if cid is not None:
        params.update(collective_id=cid, has_side_effects=True)
    shapes = [jax.ShapeDtypeStruct(s, t) for s, t in outs]
    return pl.pallas_call(
        body, out_shape=shapes, name=name, compiler_params=pltpu.CompilerParams(**params), scratch_shapes=list(scratch),
        out_specs=out_specs or [VM] * len(outs), **({"in_specs": ins} if ins else {}), **more,
    )


def on_device(sections, dps, inputs, cotangent, land, kernel, bn_gain, bn_bias, bias_in, bias_out, w_in, w_out, resample, merge):
    batches, height, cols, c = inputs.shape
    hid = bias_in.shape[1]
    n = resample.shape[1] * dps // (4 * c)
    cw, hw, nw = (GROUPS * padded(v) for v in (c, hid, n))
    cells, deep_cells = cols * 8, cols * 2
    count = 2 * (dps // 4)
    assert batches == 4 and height == 4 and dps % 4 == 0 and sections == 2 and cols % 32 == 0
    s = lax.axis_index("section")
    mats = {k: jnp.asarray(v) for k, v in matrices(c).items()}
    tiles = cols // 16

    rows = jnp.concatenate([kernel[0], bn_gain, bn_bias, bias_out], axis=0)
    par = grow(grow(rows.reshape(-1, GROUPS, c // GROUPS), (52, GROUPS, padded(c))).reshape(52, cw), (56, cw))
    bias = grow(grow(bias_in.reshape(GROUPS, -1), (GROUPS, padded(hid))).reshape(1, hw), (8, hw))
    x = inputs.reshape(batches, height, tiles, 16, c)
    cot = cotangent.reshape(batches, height, tiles, 16, c)
    land_cols = -(-cols // 128) * 128
    x14, cot8, land2, par2, bias2 = call(
        "share", functools.partial(share_kernel, sections, dps),
        [((14, tiles, 16, c), BF), ((8, tiles, 16, c), BF), ((2, 8, land_cols), jnp.int32), ((2, 56, cw), F32), ((2, 8, hw), F32)],
        [ANY] * 6, [ANY] * 5, [DMA((k,)) for k in (2, 2, 2, 2, 2, 2, 2, 2, 4, 2)], 1,
    )(x, cot, grow(land, (8, land_cols)), par, bias, jnp.zeros((3, tiles, 16, c), BF))

    def mine(parts, w1, w2, rd, ru):
        return (
            pack_in(w1, parts, c, hid), pack_in(w2, parts, hid, c),
            pack_down(rd, parts, c, n), pack_up(ru, parts, c, n),
        )

    if dps == GROUPS:
        w1, w2, rd, ru = mine(1, *(v.astype(BF) for v in (w_in, w_out, resample, resample)))
        mm = pack_in(merge.astype(BF), 1, c, c)
        shards = [w1[0], w2[0], jnp.where(s == 0, rd, ru)[0], mm[0]]
        full = call(
            "gather", gather_kernel, [((2, 4, 4) + v.shape, BF) for v in shards], [ANY] * 4, [ANY] * 4,
            [DMA((4,)), DMA((4, 4)), DMA((4, 4)), DMA((4,)), DMA((4,)), DMA((4, 2)), DMA((4, 2)), DMA((4, 4)), DMA((4, 4))], 2,
        )(*shards)
        W1, W2, R, M = (v.reshape((2, GROUPS) + v.shape[3:]) for v in full)
        R0, R1 = R[0], R[1]
    else:
        both = ("section", "dp")
        flat = [lax.all_gather(v.astype(BF).reshape(-1), both, axis=0, tiled=True) for v in (w_in, w_out, resample, merge)]
        halves = [v.reshape(2, -1) for v in flat]
        packs = [mine(GROUPS, halves[0][k], halves[1][k], halves[2][k], halves[2][k]) for k in range(2)]
        W1, W2 = (jnp.stack([packs[0][k], packs[1][k]]) for k in range(2))
        R0, R1 = packs[0][2], packs[1][3]
        M = jnp.stack([pack_in(halves[3][k], GROUPS, c, c) for k in range(2)])
    W1, W2, M = W1.reshape(2, cw, hw), W2.reshape(2, hw, cw), M.reshape(2, cw, cw)
    R0 = R0.reshape(4 * cw, nw)
    R1 = R1.reshape(GROUPS, 2, padded(n), 2 * cw)

    wet = land2[:, :height, :cols].reshape(8, cols)
    ocean = jnp.broadcast_to(wet.T.reshape(cells, 1), (cells, 128)).astype(F32)
    shallow = jnp.min(wet.reshape(4, 2, cols // 2, 2), axis=(1, 3))
    coarse = jnp.broadcast_to(shallow.T.reshape(deep_cells, 1), (deep_cells, 128)).astype(F32)
    ocean3 = ocean.reshape(cols, 8, 128)

    field = lambda t: ((cells, cw), t)
    exchange = [pltpu.VMEM((8, cw), F32), pltpu.VMEM((count, 8, cw), F32), DMA((count,)), DMA((count,))]
    shift_space = [pltpu.VMEM((7, cw // 128, cols + 6, 8, 128), F32), pltpu.VMEM((49, 8, cw), F32)]
    conv_out = [((cols, 8, cw), F32)]
    st_out = [((8, cw), F32)]

    def feed_forward(name, z, st, sec, res):
        full = lambda *shape: pl.BlockSpec(shape, lambda i: (0,) * len(shape))
        row = lambda w: pl.BlockSpec((256, w), lambda i: (i, 0))
        return call(
            name, ff_kernel, [field(BF), ((cells, hw), BF), ((cells, hw), BF), field(BF), ((8, tiles, 16, c), BF)],
            [row(cw), full(8, cw), full(56, cw), full(8, hw), full(cw, hw), full(hw, cw), row(cw), row(128), full(128, 128), full(cw, c)],
            [row(cw), row(hw), row(hw), row(cw), pl.BlockSpec((8, 2, 16, c), lambda i: (0, i, 0, 0))], grid=(cells // 256,),
        )(z.reshape(cells, cw), st, par2[sec], bias2[sec], W1[sec], W2[sec], res, ocean, mats["back"], mats["gather"])

    def backward(name, cid, natural_grad, top, z, st, sec, kept):
        nn, gg, gp = kept
        return call(
            name, functools.partial(back_ff_kernel, count, natural_grad),
            [field(F32), ((cw, hw), BF), ((hw, cw), BF), ((8, cw), F32), field(BF), ((2, tiles, 48, cw), BF)],
            scratch=[pltpu.VMEM((cells, cw), F32), pltpu.VMEM((cells, cw), BF), pltpu.VMEM((2, tiles, 48, cw), BF)] + exchange + [DMA((2,)), DMA((2,))],
            cid=cid, limit=60,
        )(top, z.reshape(cells, cw), st, par2[sec], W1[sec], W2[sec], nn, gg, gp, ocean, mats["spread"], mats["turn"], mats["edges"])

    def backward_conv(name, dz, halo, sec, dym, a, with_natural):
        def body(dz, halo, shifts, par, dym, a, back, gather, dh, dk, *rest):
            nat = rest[0] if with_natural else None
            back_conv_kernel(cols, nat, dz, halo, shifts, par, dym, a, back, gather, dh, dk, *rest[1 if with_natural else 0 :])

        return call(
            name, body, [field(BF), ((56, cw), F32)] + ([((8, tiles, 16, c), BF)] if with_natural else []),
            scratch=shift_space + [pltpu.VMEM((49, 8, cw), F32)],
        )(dz, halo, mats["shifts"], par2[sec], dym, a, mats["back"], mats["gather"])

    z0, a0, st0 = call(
        "enc_conv", functools.partial(enc_conv_kernel, count, cols), conv_out + [field(BF)] + st_out,
        scratch=shift_space + exchange, cid=3,
    )(x14, mats["spread"], mats["natural"], par2[0], ocean3)
    *kept0, skip, nat_act0 = feed_forward("enc_ff", z0, st0, 0, a0)
    pieces, deep, up, h, a1, halo1 = call(
        "mid", functools.partial(mid_kernel, count),
        [((4, deep_cells, cw), BF), ((deep_cells, nw), BF), field(BF), field(F32), field(BF), ((2, tiles, 48, cw), BF)],
        scratch=[pltpu.VMEM((2, tiles, 48, cw), BF), DMA((2,)), DMA((2,))], cid=4,
    )(skip, R0, R1, M, coarse, mats["patch"], mats["unpatch"], mats["edges"])
    z1, st1 = call(
        "dec_conv", functools.partial(dec_conv_kernel, count, cols), conv_out + st_out, scratch=shift_space + exchange, cid=5,
    )(a1, halo1, mats["shifts"], par2[1], ocean3)
    *kept1, _, nat_act1 = feed_forward("dec_ff", z1, st1, 1, h)

    dym1, dw1_1, dw2_1, small1, dz1, dhalo1 = backward("dec_back", 6, True, cot8, z1, st1, 1, kept1)
    dh1, dk1 = backward_conv("dec_back_conv", dz1, dhalo1, 1, dym1, a1, False)
    dm, dr1, dr0, dy0, nat_g1 = call(
        "back_mid", back_mid_kernel,
        [((2, cw, cw), BF), ((GROUPS, 2, padded(n), 2 * cw), BF), ((4 * cw, nw), BF), field(F32), ((8, tiles, 16, c), BF)],
        scratch=[pltpu.VMEM((cells, cw), BF), pltpu.VMEM((2, deep_cells, 2 * cw), BF), pltpu.VMEM((4, deep_cells, cw), F32)], limit=60,
    )(dh1, up, skip, deep, pieces, R0, R1, M, coarse, mats["patch"], mats["unpatch"], mats["back"], mats["gather"])
    dym0, dw1_0, dw2_0, small0, dz0, dhalo0 = backward("enc_back", 7, False, dy0, z0, st0, 0, kept0)
    _, dk0, nat_g0 = backward_conv("enc_back_conv", dz0, dhalo0, 0, dym0, a0, True)

    act, gi = call(
        "deliver", functools.partial(deliver_kernel, dps), [((4, 4, tiles, 16, c), BF)] * 2, [ANY] * 4, [ANY] * 2,
        [DMA((2, 2, 2)), DMA((2, 4))], 8,
    )(nat_act0, nat_act1, nat_g0, nat_g1)
    activations = act.reshape(1, batches, height, cols, c)
    grad_input = gi.astype(F32).reshape(1, batches, height, cols, c)
    tiny = jnp.stack([jnp.concatenate([dk, small], axis=0) for dk, small in ((dk0, small0), (dk1, small1))])
    shapes = [(padded(c), hw), (padded(hid), cw), (4 * padded(c), nw), (padded(c), cw)]
    if dps == GROUPS:
        view = lambda v, shape: v.reshape((4, 4) + shape)
        grids = lambda dw1, dw2, dr: [view(v, shape) for v, shape in zip((dw1, dw2, dr), shapes)]
        banks = [[pltpu.VMEM(lead + shape, BF) for shape in shapes] for lead in ((4, 4), (4, 4), (4, 2), (4,), (3,))]
        g1, g2, gr, gm, tiny = call(
            "reduce", reduce_kernel, [(shape, F32) for shape in shapes] + [((64, cw), F32)], [ANY] * 7 + [VM], None,
            sum(banks, []) + [pltpu.VMEM((9, 64, cw), F32)]
            + [DMA((4,)), DMA((4,)), DMA((4,)), DMA((4, 2)), DMA((4, 2)), DMA((4,)), DMA((4,)), DMA((4, 4)), DMA((4, 4)), DMA((7,)), DMA((7,))],
            9, 60,
        )(*grids(dw1_0, dw2_0, dr0), *grids(dw1_1, dw2_1, dr1), dm.reshape((2, 4, 4) + shapes[3]), tiny)
        gw1, gw2, gmm = unpack_in(g1, c, hid), unpack_in(g2, hid, c), unpack_in(gm, c, c)
        gres = jnp.where(s == 0, unpack_down(gr, c, n), unpack_up(gr, c, n))
    else:
        both = ("section", "dp")
        scatter = lambda v: lax.psum_scatter(v.astype(F32).reshape(-1), both, scatter_dimension=0, tiled=True)
        gw1 = scatter(jnp.stack([unpack_in(v, c, hid) for v in (dw1_0, dw1_1)]))
        gw2 = scatter(jnp.stack([unpack_in(v, hid, c) for v in (dw2_0, dw2_1)]))
        gres = scatter(jnp.stack([unpack_down(dr0, c, n), unpack_up(dr1, c, n)]))
        gmm = scatter(jnp.stack([unpack_in(dm[k], c, c) for k in range(2)]))
        tiny = lax.psum(tiny, both)[s]
    narrow = lambda v: v.reshape(-1, GROUPS, padded(c))[:, :, : c // GROUPS].reshape(-1, c)
    fine = narrow(tiny[:59])
    grad_bias_in = tiny[59:63].reshape(-1)[:hw].reshape(GROUPS, -1)[:, : hid // GROUPS].reshape(1, hid)
    return (
        activations, grad_input, fine[None, :49], fine[57:58], fine[56:57], grad_bias_in, fine[58:59],
        gw1[None], gw2[None], gres[None], gmm,
    )


def solution(mesh):
    sections, dps = mesh.shape["section"], mesh.shape["dp"]
    flat, both = P("section", "dp"), P(("section", "dp"))
    per = P("section", None)
    rows = P(None, "dp", None, None)
    taps = P("section", None, None)
    fields = P("section", None, "dp", None, None)
    return jax.shard_map(
        functools.partial(on_device, sections, dps), mesh=mesh,
        in_specs=(rows, rows, P("dp", None), taps, per, per, per, per, flat, flat, flat, both),
        out_specs=(fields, fields, taps, per, per, per, per, flat, flat, flat, both), check_vma=False,
    )
```

time: 2280 us -> 733 us (0.32)
  waiting for transfers between devices: 704 us -> 0 us
  Pallas kernels: 0 us -> 654 us
  other arithmetic: 496 us -> 17.7 us
  blocking collectives: 402 us -> 0 us
  matrix products: 236 us -> 0 us
  local copies, waits for them, and re-layouts: 246 us -> 51.5 us
  starting transfers between devices: 142 us -> 0 us
  between operations: 28.1 us -> 1.64 us
    pallas_call x0 -> x14, Pallas kernels: none -> 654 us  [the longest x1 138 us: on_device(): call('reduce', reduce_kernel, [(shape, F32) for shape in shapes] + [((64,...]
    psum x10 -> x0, blocking collectives: 402 us -> none  [the longest x5 213 us: on_device(): lax.psum((jnp.sum(normed_grad, axis=(0, 1)), jnp.sum(normed_grad * center...]
    unnamed x8 -> x0, waiting for transfers between devices: 333 us -> none
    psum x1 -> x0, waiting for transfers between devices: 307 us -> none  [on_device(): lax.psum((grad_taps, grad_bias_in, grad_bias_out), 'dp')]
    dot_general x49 -> x0, matrix products: 236 us -> none  [the longest x5 58.7 us: on_device(): jnp.einsum('hwe,ec->hwc', activated, matrix_out, preferred_element_type=j...]
    reduce_sum x31 -> x0, other arithmetic: 151 us -> none  [the longest x5 73.4 us: on_device(): jnp.sum(depth_out * ocean_cells, axis=(0, 1))]
    ppermute x46 -> x0, starting transfers between devices: 142 us -> none  [the longest x15 78.9 us: extended(): lax.ppermute(head, axis, [((i + 1) % count, i) for i in range(ends)])]
    add x14 -> x0, other arithmetic: 94.9 us -> none  [the longest x5 65.2 us: on_device(): ocean_grad + depthwise_back(grad_padded, kernel_taps, height, across)]
  transfers between devices with their start and end apart: 51 -> 0, of which waited for: 15 -> 0; matrix products, arithmetic and copies ran while one was open for 21% -> 0% of each run, Pallas kernels for 0% -> 0%
where the time goes in v1:
time: 733 us; the launch traced here: 725 us
  Pallas kernels  654 us (89%)
  local copies, waits for them, and re-layouts  51.5 us (7%)
  other arithmetic  17.7 us (2%)
    pallas_call x1, Pallas kernels, on_device(): call('reduce', reduce_kernel, [(shape, F32) for shape in shapes] + [((64,...  138 us
    pallas_call x1, Pallas kernels, on_device(): call('gather', gather_kernel, [((2, 4, 4) + v.shape, BF) for v in shards]...  103 us
    pallas_call x2, Pallas kernels, backward(): call(name, functools.partial(back_ff_kernel, count, natural_grad), [field...  79.5 us
    pallas_call x1, Pallas kernels, on_device(): call('deliver', functools.partial(deliver_kernel, dps), [((4, 4, tiles, 1...  61.2 us
    pallas_call x2, Pallas kernels, backward_conv(): call(name, body, [field(BF), ((56, cw), F32)] + ([((8, tiles, 16, c), BF)...  58.5 us
    pallas_call x1, Pallas kernels, on_device(): call('share', functools.partial(share_kernel, sections, dps), [((14, tile...  51.1 us
    pallas_call x1, Pallas kernels, on_device(): call('enc_conv', functools.partial(enc_conv_kernel, count, cols), conv_ou...  50.4 us
    pallas_call x2, Pallas kernels, feed_forward(): call(name, ff_kernel, [field(BF), ((cells, hw), BF), ((cells, hw), BF), f...  36.2 us

profile of v1, /device:TPU:8, one launch (start us, length us, event | category | flops | bytes accessed | tf_op | source)
XLA Modules:
  0.0 724.9 jit_solution(15131053275802238501)
XLA Ops:
  0.7 0.5 broadcast.62
  1.2 1.3 reduce.26
  2.5 1.3 reduce.25
  3.9 1.3 reduce.24
  5.2 1.3 pad.40.land
  6.5 0.7 reduce.4
  7.4 0.8 convert_element_type.54
  8.2 0.6 pad.44.bias
  9.1 0.8 squeeze_reshape.11.refs_3_
  9.9 1.3 convert_reduce_fusion.2
  11.6 0.8 squeeze_reshape.9.refs_0_
  12.5 1.3 convert_reduce_fusion.1
  13.8 0.8 convert_reduce_fusion
  15.8 0.7 pad.42.par
  16.5 0.9 reshape.202
  17.9 0.8 copy.73.refs_1_
  18.6 1.2 reshape.203
  20.3 2.0 reshape.205
  22.5 1.4 copy.71
  24.3 0.7 broadcast_select_fusion.1.refs_2_
  25.1 0.8 broadcast_in_dim.19.zero
  25.9 51.1 %share.1 = (bf16[14,10,16,400]{3,2,1,0:T(8,128)(2,1)}, bf16[8,10,16,400]{3,2,1,0:T(8,128)(2,1)}, s32[2,8,256]{2,1,0:T(8,128)}, f32[2,56,512]{2,1,0:T(8,128)}, f32[2,8,1792]{2,1,0:T(8,128)}) custom-call(bf16[4,4,10,16,400]{4,3,2,1,0:T(8,128)(2,1)} %bitcast.98, bf16[4,4,10,16,400]{4,3,2,1,0:T(8,128)(2,1)} %bitcast.99, s32[8,256]{1,0:T(8,128)} %pad.40.land, ...), custom_call_target="tpu_custom_call" | custom-call | tf_op jit(solution)/shard_map/share/pallas_call | solution.py:738
  77.0 0.7 fusion.3
  78.0 1.5 slice_bitcast_fusion.2
  79.5 1.7 slice_bitcast_fusion
  81.6 0.8 broadcast_in_dim.22.coarse
  82.4 1.1 broadcast_in_dim.20.ocean
  83.5 1.1 broadcast_in_dim.21.ocean
  84.6 50.4 %enc_conv.1 = (f32[160,8,512]{2,1,0:T(8,128)}, bf16[1280,512]{1,0:T(8,128)(2,1)}, f32[8,512]{1,0:T(8,128)}) custom-call(bf16[14,10,16,400]{3,2,1,0:T(8,128)(2,1)} %get-tuple-element.68.x14, bf16[400,512]{1,0:T(8,128)(2,1)} %constant.33.clone.spread, bf16[896,224]{1,0:T(8,128)(2,1)} %constant.35.clone.natural, f32[56,512]{1,0:T(8,128)} %get-tuple-element.168.par, ...), custom_call_target="tpu_custom_call" | custom-call | tf_op jit(solution)/shard_map/enc_conv/pallas_call | solution.py:812
  135.0 103.0 %gather.6 = (bf16[2,4,4,32,1792]{4,3,2,1,0:T(8,128)(2,1)}, bf16[2,4,4,112,512]{4,3,2,1,0:T(8,128)(2,1)}, bf16[2,4,4,128,1024]{4,3,2,1,0:T(8,128)(2,1)}, bf16[2,4,4,32,512]{4,3,2,1,0:T(8,128)(2,1)}) custom-call(bf16[32,1792]{1,0:T(8,128)(2,1)} %squeeze_reshape.9.refs_0_, bf16[112,512]{1,0:T(8,128)(2,1)} %copy.73.refs_1_, ...), custom_call_target="tpu_custom_call" | custom-call | tf_op jit(solution)/shard_map/gather/pallas_call | solution.py:754
  238.0 4.4 fusion.2
  242.4 2.1 fusion.1
  244.5 1.8 copy-done
  246.2 3.7 fusion
  250.0 18.0 %enc_ff.1 = (bf16[1280,512]{1,0:T(8,128)(2,1)}, bf16[1280,1792]{1,0:T(8,128)(2,1)}, bf16[1280,1792]{1,0:T(8,128)(2,1)}, bf16[1280,512]{1,0:T(8,128)(2,1)}, bf16[8,10,16,400]{3,2,1,0:T(8,128)(2,1)}) custom-call(f32[1280,512]{1,0:T(8,128)} %bitcast.87, f32[8,512]{1,0:T(8,128)} %get-tuple-element.72.st, f32[56,512]{1,0:T(8,128)} %get-tuple-element.168.par, ...), custom_call_target="tpu_custom_call" | custom-call | tf_op jit(solution)/shard_map/enc_ff/pallas_call | solution.py:787
  267.9 21.6 %mid.1 = (bf16[4,320,512]{2,1,0:T(8,128)(2,1)}, bf16[320,1024]{1,0:T(8,128)(2,1)}, bf16[1280,512]{1,0:T(8,128)(2,1)}, f32[1280,512]{1,0:T(8,128)}, bf16[1280,512...) custom-call(bf16[1280,512]{1,0:T(8,128)(2,1)} %get-tuple-element.78.skip, bf16[2048,1024]{1,0:T(8,128)(2,1)} %bitcast.77, ...), custom_call_target="tpu_custom_call" | custom-call | tf_op jit(solution)/shard_map/mid/pallas_call | solution.py:817
  289.6 32.3 %dec_conv.1 = (f32[160,8,512]{2,1,0:T(8,128)}, f32[8,512]{1,0:T(8,128)}) custom-call(bf16[1280,512]{1,0:T(8,128)(2,1)} %get-tuple-element.81.a, bf16[2,10,48,512]{3,2,1,0:T(8,128)(2,1)} %get-tuple-element.82.halo, bf16[896,224]{1,0:T(8,128)(2,1)} %constant.36.clone.shifts, f32[56,512]{1,0:T(8,128)} %get-tuple-element.167.par, ...), custom_call_target="tpu_custom_call" | custom-call | tf_op jit(solution)/shard_map/dec_conv/pallas_call | solution.py:822
  321.9 18.2 %dec_ff.1 = (bf16[1280,512]{1,0:T(8,128)(2,1)}, bf16[1280,1792]{1,0:T(8,128)(2,1)}, bf16[1280,1792]{1,0:T(8,128)(2,1)}, bf16[1280,512]{1,0:T(8,128)(2,1)}, bf16[8,10,16,400]{3,2,1,0:T(8,128)(2,1)}) custom-call(f32[1280,512]{1,0:T(8,128)} %bitcast.89, f32[8,512]{1,0:T(8,128)} %get-tuple-element.84.st, f32[56,512]{1,0:T(8,128)} %get-tuple-element.167.par, ...), custom_call_target="tpu_custom_call" | custom-call | tf_op jit(solution)/shard_map/dec_ff/pallas_call | solution.py:787
  340.1 41.3 %dec_back.1 = (f32[1280,512]{1,0:T(8,128)}, bf16[512,1792]{1,0:T(8,128)(2,1)}, bf16[1792,512]{1,0:T(8,128)(2,1)}, f32[8,512]{1,0:T(8,128)}, bf16[1280,512]{1,0:T(8,128)(2,1)}, /*index=5*/bf16[2,10,48,512]{3,2,1,0:T(8,128)(2,1)}) custom-call(bf16[8,10,16,400]{3,2,1,0:T(8,128)(2,1)} %get-tuple-element.87.top, f32[1280,512]{1,0:T(8,128)} %bitcast.90, ...), custom_call_target="tpu_custom_call" | custom-call | tf_op jit(solution)/shard_map/dec_back/pallas_call | solution.py:795
  381.4 27.3 %dec_back_conv.1 = (bf16[1280,512]{1,0:T(8,128)(2,1)}, f32[56,512]{1,0:T(8,128)}) custom-call(bf16[1280,512]{1,0:T(8,128)(2,1)} %get-tuple-element.91.dz, bf16[2,10,48,512]{3,2,1,0:T(8,128)(2,1)} %get-tuple-element.92.halo, bf16[896,224]{1,0:T(8,128)(2,1)} %constant.36.clone.shifts, f32[56,512]{1,0:T(8,128)} %get-tuple-element.167.par, ...), custom_call_target="tpu_custom_call" | custom-call | tf_op jit(solution)/shard_map/dec_back_conv/pallas_call | solution.py:807
  408.7 22.4 %back_mid.1 = (bf16[2,512,512]{2,1,0:T(8,128)(2,1)}, bf16[16,2,64,1024]{3,2,1,0:T(8,128)(2,1)}, bf16[2048,1024]{1,0:T(8,128)(2,1)}, f32[1280,512]{1,0:T(8,128)}, bf16[8,10,16,400]{3,2,1,0:T(8,128)(2,1)}) custom-call(bf16[1280,512]{1,0:T(8,128)(2,1)} %get-tuple-element.94.dh, bf16[1280,512]{1,0:T(8,128)(2,1)} %get-tuple-element.95.up, ...), custom_call_target="tpu_custom_call" | custom-call | tf_op jit(solution)/shard_map/back_mid/pallas_call | solution.py:829
  431.1 38.3 %enc_back.1 = (f32[1280,512]{1,0:T(8,128)}, bf16[512,1792]{1,0:T(8,128)(2,1)}, bf16[1792,512]{1,0:T(8,128)(2,1)}, f32[8,512]{1,0:T(8,128)}, bf16[1280,512]{1,0:T(8,128)(2,1)}, /*index=5*/bf16[2,10,48,512]{3,2,1,0:T(8,128)(2,1)}) custom-call(f32[1280,512]{1,0:T(8,128)} %get-tuple-element.98.top, f32[1280,512]{1,0:T(8,128)} %bitcast.88, ...), custom_call_target="tpu_custom_call" | custom-call | tf_op jit(solution)/shard_map/enc_back/pallas_call | solution.py:795
  469.4 31.1 %enc_back_conv.1 = (bf16[1280,512]{1,0:T(8,128)(2,1)}, f32[56,512]{1,0:T(8,128)}, bf16[8,10,16,400]{3,2,1,0:T(8,128)(2,1)}) custom-call(bf16[1280,512]{1,0:T(8,128)(2,1)} %get-tuple-element.102.dz, bf16[2,10,48,512]{3,2,1,0:T(8,128)(2,1)} %get-tuple-element.103.halo, bf16[896,224]{1,0:T(8,128)(2,1)} %constant.36.clone.shifts, ...), custom_call_target="tpu_custom_call" | custom-call | tf_op jit(solution)/shard_map/enc_back_conv/pallas_call | solution.py:807
  500.6 61.2 %deliver.1 = (bf16[4,4,10,16,400]{4,3,2,1,0:T(8,128)(2,1)}, bf16[4,4,10,16,400]{4,3,2,1,0:T(8,128)(2,1)}) custom-call(bf16[8,10,16,400]{3,2,1,0:T(8,128)(2,1)} %get-tuple-element.77.a0, bf16[8,10,16,400]{3,2,1,0:T(8,128)(2,1)} %get-tuple-element.86.a1, bf16[8,10,16,400]{3,2,1,0:T(8,128)(2,1)} %get-tuple-element.105.g0, ...), custom_call_target="tpu_custom_call" | custom-call | tf_op jit(solution)/shard_map/deliver/pallas_call | solution.py:837
  561.9 0.7 pad_maximum_fusion.refs_7_
  562.6 137.8 %reduce.27 = (f32[32,1792]{1,0:T(8,128)}, f32[112,512]{1,0:T(8,128)}, f32[128,1024]{1,0:T(8,128)}, f32[32,512]{1,0:T(8,128)}, f32[64,512]{1,0:T(8,128)}) custom-call(bf16[4,4,32,1792]{3,2,1,0:T(8,128)(2,1)} %bitcast.104, bf16[4,4,112,512]{3,2,1,0:T(8,128)(2,1)} %bitcast.105, bf16[4,4,128,1024]{3,2,1,0:T(8,128)(2,1)} %bitcast.96, ...), custom_call_target="tpu_custom_call" | custom-call | tf_op jit(solution)/shard_map/reduce/pallas_call | solution.py:849
  700.4 0.8 slice_bitcast_fusion.4
  701.3 0.7 reshape.222
  702.0 1.1 reshape.223
  703.1 1.0 broadcast_in_dim_reshape.6
  704.1 1.1 copy.76
  705.4 0.8 reshape.230
  706.9 0.7 slice.124
  707.5 0.7 slice.119
  708.2 0.7 slice.117
  708.9 0.8 copy.80
  710.2 1.0 reshape.226
  711.2 0.6 reshape.227
  712.3 1.4 broadcast_in_dim_reshape.7
  713.7 1.7 copy.79
  715.4 1.5 reshape.228
  716.9 1.1 broadcast_select_fusion
  718.0 5.0 convert.1
  722.9 1.5 copy.84
  (66 shorter events, 6.3 us)
Async XLA Ops:
  0.6 13.2 %copy-start.4 = (f32[1,80000]{1,0:T(1,128)S(1)}, f32[1,80000]{1,0:T(1,128)}, u32[]{:S(2)}) copy-start(f32[1,80000]{1,0:T(1,128)} %param.31) | copy-start | bytes 960004
  0.7 14.0 %copy-start.8 = (f32[1,49,400]{2,0,1:T(1,128)S(1)}, f32[1,49,400]{2,0,1:T(1,128)}, u32[]{:S(2)}) copy-start(f32[1,49,400]{2,0,1:T(1,128)} %param.24) | copy-start | bytes 235204
  238.0 4.4 copy-start.1
  238.0 8.2 %copy-start = (bf16[2,4,4,128,1024]{4,3,2,1,0:T(8,128)(2,1)S(1)}, bf16[2,4,4,128,1024]{4,3,2,1,0:T(8,128)(2,1)}, u32[]{:S(2)}) copy-start(bf16[2,4,4,128,1024]{4,3,2,1,0:T(8,128)(2,1)} %get-tuple-element.79) | copy-start | bytes 25165828
  500.5 61.3 %copy-start.6 = (f32[56,512]{1,0:T(8,128)S(1)}, f32[56,512]{1,0:T(8,128)}, u32[]{:S(2)}) copy-start(f32[56,512]{1,0:T(8,128)} %get-tuple-element.118) | copy-start | bytes 344068
  500.5 61.3 %copy-start.7 = (f32[56,512]{1,0:T(8,128)S(1)}, f32[56,512]{1,0:T(8,128)}, u32[]{:S(2)}) copy-start(f32[56,512]{1,0:T(8,128)} %get-tuple-element.116) | copy-start | bytes 344068
  500.6 61.3 %copy-start.10 = (f32[8,512]{1,0:T(8,128)S(1)}, f32[8,512]{1,0:T(8,128)}, u32[]{:S(2)}) copy-start(f32[8,512]{1,0:T(8,128)} %get-tuple-element.119) | copy-start | bytes 49156
  500.6 61.3 %copy-start.11 = (f32[8,512]{1,0:T(8,128)S(1)}, f32[8,512]{1,0:T(8,128)}, u32[]{:S(2)}) copy-start(f32[8,512]{1,0:T(8,128)} %get-tuple-element.117) | copy-start | bytes 49156
  700.4 4.8 copy-start.9
  700.4 5.8 copy-start.5
  704.1 5.6 copy-start.3
  718.0 5.0 copy-start.2

commit v2 on v1

v2 whole, which is shorter than its diff:
```python
import functools

import jax
import jax.numpy as jnp
import ml_dtypes
import numpy as np
from jax import lax
from jax.experimental import pallas as pl
from jax.experimental.pallas import tpu as pltpu
from jax.sharding import PartitionSpec as P

BF = jnp.bfloat16
F32 = jnp.float32
MESH = pl.DeviceIdType.MESH
ANY = pl.BlockSpec(memory_space=pl.ANY)
VM = pl.BlockSpec(memory_space=pltpu.VMEM)
DMA = pltpu.SemaphoreType.DMA
EPS = 1e-05
GROUPS = 16
MEGA = 1 << 20


def padded(width):
    return -(-(width // GROUPS) // 16) * 16


def selector(rows, cols, pairs):
    out = np.zeros((rows, cols), np.float32)
    for r, c in pairs:
        out[r, c] = 1
    return out.astype(ml_dtypes.bfloat16)


def matrices(channels):
    group, wide = channels // GROUPS, padded(channels)
    spread = selector(channels, GROUPS * wide, [(c, c // group * wide + c % group) for c in range(channels)])
    natural = selector(896, 224, [(i * 128 + q * 8 + p, (p + i) * 16 + q) for i in range(7) for q in range(16) for p in range(8)])

    def place(q, row):
        if row < 0:
            return 128 + q * 3 + row + 3
        return q * 8 + row if row < 8 else 176 + q * 3 + row - 8

    shifts = selector(896, 224, [(i * 128 + q * 8 + p, place(q, p + i - 3)) for i in range(7) for q in range(16) for p in range(8)])
    turn = selector(128, 128, [(q * 8 + p, p * 16 + q) for q in range(16) for p in range(8)])
    edges = selector(96, 128, [(48 * e + q * 3 + k, q * 8 + 5 * e + k) for e in range(2) for q in range(16) for k in range(3)])
    patch = selector(
        256, 256,
        [((i * 2 + j) * 64 + b * 4 + a, (2 * b + j) * 8 + 2 * a + i) for i in range(2) for j in range(2) for b in range(16) for a in range(4)],
    )
    pick = selector(128, 16, [(q * 8 + p, p // 4 * 8 + p % 4) for q in range(16) for p in range(8)])
    return dict(
        pick=pick, spread=spread, gather=np.ascontiguousarray(spread.T), natural=natural, shifts=shifts, turn=turn,
        back=np.ascontiguousarray(turn.T), edges=edges, patch=patch, unpatch=np.ascontiguousarray(patch.T),
    )


def grow(value, sizes):
    return jnp.pad(value, [(0, n - o) for n, o in zip(sizes, value.shape)])


def pack_in(value, parts, c, h):
    value = value.reshape(parts, c // GROUPS, GROUPS, h // GROUPS)
    return grow(value, (parts, padded(c), GROUPS, padded(h))).reshape(parts, padded(c), -1)


def pack_down(value, parts, c, n):
    value = value.reshape(parts, 4, c // GROUPS, GROUPS, n // GROUPS)
    return grow(value, (parts, 4, padded(c), GROUPS, padded(n))).reshape(parts, 4 * padded(c), -1)


def pack_up(value, parts, c, n):
    value = value.reshape(parts, n // GROUPS, 2, 2 * GROUPS, c // GROUPS)
    value = grow(value, (parts, padded(n), 2, 2 * GROUPS, padded(c)))
    return value.transpose(0, 2, 1, 3, 4).reshape(parts, 2 * padded(n), -1)


def unpack_in(value, c, h):
    value = value.reshape(-1, padded(c), GROUPS, padded(h))
    return value[:, : c // GROUPS, :, : h // GROUPS].reshape(-1)


def unpack_down(value, c, n):
    value = value.reshape(-1, 4, padded(c), GROUPS, padded(n))
    return value[:, :, : c // GROUPS, :, : n // GROUPS].reshape(-1)


def unpack_up(value, c, n):
    value = value.reshape(-1, 2, padded(n), 2 * GROUPS, padded(c))
    return value.transpose(0, 2, 1, 3, 4)[:, : n // GROUPS, :, :, : c // GROUPS].reshape(-1)


def device(p, m):
    g = p // 2
    return (p + g) % 2, 4 * g + m


def where_am_i():
    s, d = lax.axis_index("section"), lax.axis_index("dp")
    g = d // 4
    return s, d, g, d % 4, 2 * g + (s + g) % 2


def greet_near(count):
    s, d, g, m, p = where_am_i()
    barrier = pltpu.get_barrier_semaphore()

    def one(k, carry):
        q = (p + k) % count
        pl.semaphore_signal(barrier, inc=1, device_id=device(q, m), device_id_type=MESH)
        return carry

    lax.fori_loop(1, count, one, 0)
    for k in range(1, 4):
        for sec in range(2):
            pl.semaphore_signal(barrier, inc=1, device_id=(sec, 4 * g + (m + k) % 4), device_id_type=MESH)
    pl.semaphore_wait(barrier, count + 5)


def remote(src, dst, send, recv, peer):
    return pltpu.make_async_remote_copy(src_ref=src, dst_ref=dst, send_sem=send, recv_sem=recv, device_id=peer, device_id_type=MESH)


def arrived(ref, sem):
    pltpu.make_async_copy(ref, ref, sem).wait()


def all_sum(mine, slots, send, recv, count):
    s, d, g, m, p = where_am_i()
    groups = count // 2
    over = remote(mine, slots.at[groups], send.at[0], recv.at[0], (1 - s, d))
    over.start()
    arrived(slots.at[groups], recv.at[0])
    slots[g] = mine[...] + slots[groups]
    over.wait_send()

    def copy(k):
        return remote(slots.at[g], slots.at[g], send.at[k], recv.at[k], (s, 4 * ((g + k) % groups) + m))

    lax.fori_loop(1, groups, lambda k, c: (copy(k).start(), c)[1], 0)

    def wait(k, carry):
        arrived(slots.at[(g + groups - k) % groups], recv.at[k])
        copy(k).wait_send()
        return carry

    lax.fori_loop(1, groups, wait, 0)
    return lax.fori_loop(0, groups, lambda k, total: total + slots[k], jnp.zeros(mine.shape, F32))


def swap_rows(packed, halo, send, recv, count):
    s, d, g, m, p = where_am_i()

    def peer(q):
        return device(q, m)

    @pl.when(p > 0)
    def _():
        remote(packed.at[0], halo.at[1], send.at[0], recv.at[1], peer(p - 1)).start()

    @pl.when(p < count - 1)
    def _():
        remote(packed.at[1], halo.at[0], send.at[1], recv.at[0], peer(p + 1)).start()

    @pl.when(p > 0)
    def _():
        arrived(halo.at[0], recv.at[0])
        remote(packed.at[0], halo.at[1], send.at[0], recv.at[1], peer(p - 1)).wait_send()

    @pl.when(p < count - 1)
    def _():
        arrived(halo.at[1], recv.at[1])
        remote(packed.at[1], halo.at[0], send.at[1], recv.at[0], peer(p + 1)).wait_send()

    @pl.when(p == 0)
    def _():
        halo[0] = jnp.zeros(halo.shape[1:], BF)

    @pl.when(p == count - 1)
    def _():
        halo[1] = jnp.zeros(halo.shape[1:], BF)


def dot(a, b):
    return jnp.dot(a, b, preferred_element_type=F32)


def dot_nt(a, b):
    return lax.dot_general(a, b, (((1,), (1,)), ((), ())), preferred_element_type=F32)


def dot_tn(a, b):
    return lax.dot_general(a, b, (((0,), (0,)), ((), ())), preferred_element_type=F32)


def lanes4(mask, width):
    return jnp.concatenate([mask] * (width // 128), axis=1)


def rows8(value):
    return value.reshape(-1, 8, value.shape[-1]).sum(0)


def to_natural(cells, back, gather):
    turned = dot(dot(back, cells).astype(BF), gather).astype(BF)
    return turned.reshape(8, 16, turned.shape[-1])


def shifted(chunk, perm, S, c):
    moved = dot(perm, chunk)
    for lane in range(S.shape[1]):
        S[:, lane, pl.ds(3 + 16 * c, 16)] = moved[:, lane * 128 : lane * 128 + 128].reshape(7, 16, 8, 128)
    return moved


def wrap(S, cols):
    S[:, :, 0:3] = S[:, :, cols : cols + 3]
    S[:, :, cols + 3 : cols + 6] = S[:, :, 3:6]


def taps_to(kb, par, flip):
    for k in range(49):
        kb[k] = jnp.broadcast_to(par[(48 - k if flip else k) : (48 - k if flip else k) + 1], kb.shape[1:])


def norm_terms(st, par):
    counted = st[2:3]
    mean = st[0:1] / counted
    inverse = lax.rsqrt(st[1:2] / counted - mean * mean + EPS)
    return counted, mean, inverse, par[49:50], par[50:51]


def back_ff_kernel(sec, count, ns, hook):
    greet_near(count)
    hook(0)
    z, w1, w2, dn, dr, small, ocean, edges = ns.z, ns.w1, ns.w2, ns.dn, ns.dr, ns.small, ns.ocean, ns.edges
    wide = z.shape[1]
    chunks = z.shape[0] // 128
    counted, mean, inverse, gain, shift = norm_terms(ns.st, ns.par[sec])

    def begin(c, total):
        at = pl.ds(pl.multiple_of(c * 128, 128), 128)
        if sec == 1:
            block = ns.top[:, c]
            block = dot(block.reshape(-1, block.shape[-1]), ns.spread[...]).astype(BF)
            grad = dot(ns.turn[...], block)
        else:
            grad = ns.top[at]
        grad = grad * lanes4(ocean[at], wide)
        ns.dym[at] = grad
        low = grad.astype(BF)
        dr[at] = low
        return total + rows8(low.astype(F32))

    total = lax.fori_loop(0, chunks, begin, jnp.zeros((8, wide), F32))
    small[2:3] = total.sum(0, keepdims=True)
    small[3:8] = jnp.zeros((5, wide), F32)
    for h in range(0, w1.shape[1], 256):
        at = slice(h, h + 256)
        dg = dot_nt(dr[...], w2[at])
        de = (dg * ns.gp[:, at].astype(F32)).astype(BF)
        row, col = 3 + h // wide, h % wide
        small[row : row + 1, col : col + 256] = de.astype(F32).sum(0, keepdims=True)
        ns.dw1[:, at] = dot_tn(ns.n[...], de).astype(BF)
        ns.dw2[at] = dot_tn(ns.g[:, at], dr[...]).astype(BF)
        part = dot_nt(de, w1[:, at])
        if h == 0:
            dn[...] = part
        else:
            dn[...] += part
        if h == 512:
            hook(1)

    def sums(c, carry):
        at = pl.ds(pl.multiple_of(c * 128, 128), 128)
        grad = dn[at]
        return carry[0] + rows8(grad), carry[1] + rows8(grad * ((z[at] - mean) * inverse))

    zero = jnp.zeros((8, wide), F32)
    plain, scaled = lax.fori_loop(0, chunks, sums, (zero, zero))
    small[0:1] = plain.sum(0, keepdims=True)
    small[1:2] = scaled.sum(0, keepdims=True)
    ns.stats[...] = small[...]
    summed = all_sum(ns.stats, ns.slots, ns.send, ns.recv, count)
    first = -inverse * gain * summed[0:1] / counted
    second = -inverse * inverse * gain * summed[1:2] / counted
    hook(2)

    def end(c, carry):
        at = pl.ds(pl.multiple_of(c * 128, 128), 128)
        grad = inverse * gain * dn[at] + lanes4(ocean[at], wide) * (first + second * (z[at] - mean))
        low = grad.astype(BF)
        ns.dz[at] = low
        ends = dot(edges[...], low).astype(BF)
        ns.packed[0, c] = ends[:48]
        ns.packed[1, c] = ends[48:]
        return carry

    lax.fori_loop(0, chunks, end, 0)
    swap_rows(ns.packed, ns.halo, ns.hsend, ns.hrecv, count)
    hook(3)


def back_conv_kernel(sec, count, cols, ns, hook):
    greet_near(count)
    hook(0)
    taps_to(ns.kb, ns.par[sec], True)
    wide = ns.dz.shape[1]
    S, kb, acc_dk = ns.S, ns.kb, ns.acc_dk

    def chunk(c, carry):
        block = jnp.concatenate([ns.dz[pl.ds(pl.multiple_of(c * 128, 128), 128)], ns.halo[0, c], ns.halo[1, c]], axis=0)
        shifted(block, ns.perm[...], S, c)
        return carry

    lax.fori_loop(0, cols // 16, chunk, 0)
    wrap(S, cols)
    acc_dk[...] = jnp.zeros(acc_dk.shape, F32)
    for lane in range(wide // 128):
        at = slice(lane * 128, lane * 128 + 128)

        def step(b, carry):
            cells = pl.ds(pl.multiple_of(b * 64, 64), 64)
            acc = ns.dym[cells, at].reshape(8, 8, 128)
            field = ns.a[cells, at].astype(F32).reshape(8, 8, 128)
            for i in range(7):
                window = S[i, lane, pl.ds(b * 8, 14)]
                for j in range(7):
                    acc = acc + window[j : j + 8] * kb[7 * i + j, :, at][None]
                    acc_dk[7 * i + j, :, at] += (window[j : j + 8] * field).sum(0)
            ns.dh[cells, at] = acc.reshape(64, 128).astype(BF)
            return carry

        lax.fori_loop(0, cols // 8, step, 0)
        if lane in (1, 2):
            hook(lane)
    for k in range(49):
        ns.dk[48 - k : 49 - k] = acc_dk[k].sum(0, keepdims=True)
    ns.dk[49:56] = jnp.zeros((7, wide), F32)
    if sec == 0:

        def out(c, carry):
            cells = ns.dh[pl.ds(pl.multiple_of(c * 128, 128), 128)]
            ns.nat[:, c] = to_natural(cells, ns.back[...], ns.gather[...])
            return carry

        lax.fori_loop(0, cols // 16, out, 0)
    hook(3)


def back_mid_kernel(count, ns, hook):
    greet_near(count)
    hook(0)
    dh, up, skip, deep, pieces, down, up_w, merge = ns.dh, ns.up, ns.skip, ns.deep, ns.pieces, ns.down, ns.up_w, ns.merge
    dskip, dups, spreads = ns.dskip, ns.dups, ns.spreads
    wide = dh.shape[1]
    blocks = dh.shape[0] // 256
    ns.dmerge[0] = dot_tn(up[...], dh[...]).astype(BF)
    ns.dmerge[1] = dot_tn(skip[...], dh[...]).astype(BF)
    for b in range(blocks):
        at = slice(256 * b, 256 * b + 256)
        low = dot_nt(dh[at], merge[1]).astype(BF)
        dskip[at] = low
        for k in range(2):
            ns.nat[:, 2 * b + k] = to_natural(low[128 * k : 128 * k + 128], ns.back[...], ns.gather[...])
        lifted = dot_nt(dh[at], merge[0]).astype(BF)
        moved = dot(ns.patch[...], lifted).astype(BF)
        for k in range(4):
            dups[k // 2, 64 * b : 64 * b + 64, wide * (k % 2) : wide * (k % 2) + wide] = moved[64 * k : 64 * k + 64]
    hook(1)
    rows = up_w.shape[0] * up_w.shape[2]
    ddeep = dot_nt(dups[0], up_w[:, 0].reshape(rows, -1)) + dot_nt(dups[1], up_w[:, 1].reshape(rows, -1))
    for i in range(2):
        grad = dot_tn(deep[...], dups[i]).astype(BF)
        ns.dup_w[:, i] = grad.reshape(up_w.shape[0], up_w.shape[2], -1)
    masked = (lanes4(ns.coarse[...], ddeep.shape[1]) * ddeep).astype(BF)
    hook(2)
    for k in range(4):
        ns.ddown[wide * k : wide * k + wide] = dot_tn(pieces[k], masked).astype(BF)
        spreads[k] = dot_nt(masked, down[wide * k : wide * k + wide])
    for b in range(blocks):
        value = jnp.concatenate([spreads[k, 64 * b : 64 * b + 64] for k in range(4)], axis=0)
        high = value.astype(BF)
        rest = (value - high.astype(F32)).astype(BF)
        at = slice(256 * b, 256 * b + 256)
        ns.dy[at] = dskip[at].astype(F32) + (dot(ns.unpatch[...], high) + dot(ns.unpatch[...], rest))
    hook(3)


class Job:
    def __init__(self, name):
        self.name, self.ins, self.outs, self.scratch, self.alias = name, {}, {}, {}, {}

    def add(self, kind, name, value):
        getattr(self, kind)[self.name + name] = value

    def ref(self, ns, name):
        return getattr(ns, self.name + name)

    def steps(self, ns):
        return [lambda: None] * 4


def start_either(self, src, dst, send, recv, peer):
    pl.when(jnp.logical_not(self))(lambda: remote(src, dst, send, recv, peer).start())
    pl.when(self)(lambda: pltpu.make_async_copy(src, dst, recv).start())


class Deliver(Job):
    def __init__(self, name, sec, natural, before=None):
        super().__init__(name)
        self.sec = sec
        rows, tiles, q, c = natural.shape
        self.add("ins", "nat", (natural, ANY))
        self.add("outs", "out", ((4, 4, tiles, q, c), BF, ANY))
        self.add("outs", "bounce", ((rows, tiles, q, c), BF, ANY))
        self.add("scratch", "s", DMA((2, 2)))
        self.add("scratch", "r", DMA((4,)))
        self.add("scratch", "b", DMA((2,)))
        if before is not None:
            self.add("ins", "before", (before, ANY))
            self.alias = {name + "before": name + "out"}

    def steps(self, ns):
        return deliver(self.sec, *(self.ref(ns, k) for k in ("nat", "out", "bounce", "s", "r", "b")))


def deliver(sec, nat, out, bounce, send, recv, b):
    s, d, g, m, p = where_am_i()

    def target(which, j):
        dp = 4 * g + 2 * ((p + which) % 2) + j
        part = (nat, bounce)[which].at[pl.ds(4 * j, 4)]
        return dp == d, part, out.at[m], send.at[which, j], recv.at[m], (s, dp)

    def over():
        return remote(nat, bounce, b.at[0], b.at[1], (1 - s, d))

    def sends(which):
        for j in range(2):
            start_either(*target(which, j))

    def begin():
        pl.when(s != sec)(lambda: over().start())
        pl.when(s == sec)(lambda: sends(0))

    def middle():
        @pl.when(s == sec)
        def _():
            arrived(bounce, b.at[1])
            sends(1)

    def end():
        @pl.when(s == sec)
        def _():
            for mb in range(4):
                arrived(out.at[mb], recv.at[mb])
            for which in range(2):
                for j in range(2):
                    self_, *rest = target(which, j)
                    pl.when(jnp.logical_not(self_))(lambda rest=rest: remote(*rest).wait_send())

        pl.when(s != sec)(lambda: over().wait_send())

    return [begin, middle, lambda: None, end]


def collect(field, out, first, send, recv):
    s, d, g, m, p = where_am_i()
    core, dp = device(d // 2, 0)
    j = d % 2

    def parts(step):
        mb = (m + step) % 4
        return field.at[mb], out.at[pl.ds(first + 4 * j, 4)], send.at[step], recv.at[j], (s, dp + mb)

    def begin():
        @pl.when(s == core)
        def _():
            for step in range(1, 4):
                remote(*parts(step)).start()
            src, dst, _, sem, _ = parts(0)
            pltpu.make_async_copy(src, dst, sem).start()

    def end():
        for jj in range(2):
            arrived(out.at[pl.ds(first + 4 * jj, 4)], recv.at[jj])

        @pl.when(s == core)
        def _():
            for step in range(1, 4):
                remote(*parts(step)).wait_send()

    return begin, end


def half(ref, c):
    rows, lanes = ref.shape[-2:]
    lead = (slice(None),) * (len(ref.shape) - 2)
    if rows % 32 == 0:
        return ref.at[lead + (pl.ds(pl.multiple_of(c * (rows // 2), 16), rows // 2),)]
    return ref.at[lead + (slice(None), pl.ds(pl.multiple_of(c * (lanes // 2), 128), lanes // 2))]


def half_shape(shape):
    rows, lanes = shape[-2:]
    return shape[:-2] + ((rows // 2, lanes) if rows % 32 == 0 else (rows, lanes // 2))


class PlaneSum(Job):
    def __init__(self, name, parts):
        super().__init__(name)
        self.parts, n = parts, len(parts)
        for k, v in enumerate(parts):
            array = v[0] if isinstance(v, tuple) else v
            self.add("ins", f"in{k}", (array, ANY))
            shape = half_shape(array.shape[-2:])
            for bank, lead in (("own", (4, 4)), ("core", (4, 4)), ("one", (4, 2)), ("two", (4,))):
                self.add("scratch", f"{bank}{k}", pltpu.VMEM(lead + shape, BF))
            self.add("outs", f"out{k}", ((4,) + shape, BF, VM))
        for k, width in (("l", 1), ("cs", 1), ("cr", 1), ("as", 2), ("ar", 2), ("bs", 1), ("br", 1)):
            self.add("scratch", k, DMA((n, width)))

    def steps(self, ns):
        s, d, g, m, p = where_am_i()
        sem = {k: self.ref(ns, k) for k in ("l", "cs", "cr", "as", "ar", "bs", "br")}
        bank = lambda kind, k: self.ref(ns, f"{kind}{k}")
        bit, every = 1 + s, range(len(self.parts))

        def source(k, c):
            v, ref = self.parts[k], self.ref(ns, f"in{k}")
            return half(ref.at[v[1]] if isinstance(v, tuple) else ref, c)

        def near(k):
            return pltpu.make_async_copy(source(k, s), bank("own", k), sem["l"].at[k, 0])

        def over(k):
            return remote(source(k, 1 - s), bank("core", k), sem["cs"].at[k, 0], sem["cr"].at[k, 0], (1 - s, d))

        def first(k, index):
            col = (m ^ bit, m ^ 3)[index]
            return remote(bank("own", k).at[:, col], bank("one", k).at[:, index], sem["as"].at[k, index], sem["ar"].at[k, index], (s, d ^ bit))

        def second(k):
            return remote(bank("own", k).at[:, m ^ (3 - bit)], bank("two", k), sem["bs"].at[k, 0], sem["br"].at[k, 0], (s, d ^ (3 - bit)))

        def h0():
            for k in every:
                over(k).start()
                near(k).start()

        def h1():
            for k in every:
                own, core = bank("own", k), bank("core", k)
                near(k).wait()
                arrived(core, sem["cr"].at[k, 0])

                def add(b, carry, own=own, core=core):
                    own[b // 4, b % 4] = (own[b // 4, b % 4].astype(F32) + core[b // 4, b % 4].astype(F32)).astype(BF)
                    return carry

                lax.fori_loop(0, 16, add, 0)
                first(k, 1).start()
                first(k, 0).start()

        def h2():
            for k in every:
                own, one, rest = bank("own", k), bank("one", k), m ^ (3 - bit)
                arrived(one.at[:, 1], sem["ar"].at[k, 1])
                for z in range(4):
                    own[z, rest] = (own[z, rest].astype(F32) + one[z, 1].astype(F32)).astype(BF)
                second(k).start()

        def h3():
            for k in every:
                own, one, two, out = (bank(n, k) for n in ("own", "one", "two", "out"))
                arrived(one.at[:, 0], sem["ar"].at[k, 0])
                arrived(two, sem["br"].at[k, 0])
                for z in range(4):
                    out[z] = (own[z, m].astype(F32) + one[z, 0].astype(F32) + two[z].astype(F32)).astype(BF)
                first(k, 0).wait_send()
                first(k, 1).wait_send()
                second(k).wait_send()
                over(k).wait_send()

        return [h0, h1, h2, h3]


class LineSum(Job):
    def __init__(self, name, columns):
        super().__init__(name)
        self.secs = [sec for _, sec in columns]
        n = len(columns)
        for k, (v, _) in enumerate(columns):
            self.add("ins", f"in{k}", (v, ANY))
            self.add("outs", f"out{k}", ((2,) + v.shape[1:], F32, VM))
            self.add("scratch", f"line{k}", pltpu.VMEM(v.shape, BF))
            self.add("scratch", f"mine{k}", pltpu.VMEM(v.shape[1:], F32))
        for k, width in (("s", 4), ("r", 4), ("c", 2)):
            self.add("scratch", k, DMA((n, width)))

    def steps(self, ns):
        s, d, g, m, p = where_am_i()
        send, recv, sem = self.ref(ns, "s"), self.ref(ns, "r"), self.ref(ns, "c")
        every = list(enumerate(self.secs))

        def near(k):
            return pltpu.make_async_copy(self.ref(ns, f"in{k}").at[g], self.ref(ns, f"line{k}").at[0], send.at[k, 0])

        def far(k, step):
            to = (g + step) % 4
            return remote(self.ref(ns, f"in{k}").at[to], self.ref(ns, f"line{k}").at[step], send.at[k, step], recv.at[k, step], (s, 4 * to + m))

        def give(k):
            return remote(self.ref(ns, f"mine{k}"), self.ref(ns, f"out{k}").at[s], sem.at[k, 0], sem.at[k, 1], (1 - s, d))

        def begin():
            for k, _ in every:
                near(k).start()
                for step in range(1, 4):
                    far(k, step).start()

        def end():
            for k, sec in every:
                line, mine, out = (self.ref(ns, f"{n}{k}") for n in ("line", "mine", "out"))
                near(k).wait()
                for step in range(1, 4):
                    arrived(line.at[step], recv.at[k, step])
                    far(k, step).wait_send()
                mine[...] = sum(line[z].astype(F32) for z in range(4))
                pl.when(s != sec)(give(k).start)

                @pl.when(s == sec)
                def _(out=out, mine=mine):
                    out[s] = mine[...]

            for k, sec in every:
                pl.when(s != sec)(give(k).wait_send)
                pl.when(s == sec)(lambda k=k: arrived(self.ref(ns, f"out{k}").at[1 - s], sem.at[k, 1]))

        return [begin, lambda: None, lambda: None, end]


def collect_land(land, out, send, recv):
    s, d, g, m, p = where_am_i()
    core, dp = device(d // 2, 0)

    def part(step):
        return remote(land, out.at[d % 2], send.at[step], recv.at[d % 2], (s, dp + (m + step) % 4))

    def begin():
        @pl.when(s == core)
        def _():
            for step in range(1, 4):
                part(step).start()
            pltpu.make_async_copy(land, out.at[d % 2], recv.at[d % 2]).start()

    def end():
        for jj in range(2):
            arrived(out.at[jj], recv.at[jj])

        @pl.when(s == core)
        def _():
            for step in range(1, 4):
                part(step).wait_send()

    return begin, end


def last_kernel(count, ns, hook):
    s, d, g, m, p = where_am_i()
    greet_near(count)
    hook(0)
    tiny, small, ts, tr = ns.tiny, ns.small, ns.ts, ns.tr
    over = remote(small.at[1 - s], tiny.at[0], ts.at[0], tr.at[0], (1 - s, d))
    over.start()
    arrived(tiny.at[0], tr.at[0])
    over.wait_send()
    tiny[1] = small[s] + tiny[0]
    for base, peer in ((1, lambda step: (s, 4 * ((g + step) % 4) + m)), (5, lambda step: (s, d ^ step))):
        sent = [remote(tiny.at[base], tiny.at[base + step], ts.at[base + step], tr.at[base + step], peer(step)) for step in range(1, 4)]
        for c in sent:
            c.start()
        for step in range(1, 4):
            arrived(tiny.at[base + step], tr.at[base + step])
        for c in sent:
            c.wait_send()
        total = tiny[base] + tiny[base + 1] + tiny[base + 2] + tiny[base + 3]
        if base == 1:
            tiny[5] = total
        else:
            ns.total[...] = total
    hook(1)
    hook(2)
    hook(3)


class Gather:
    def __init__(self, shard, full, send, recv):
        self.shard, self.full, self.send, self.recv = shard, full, send, recv
        self.s, self.d, self.g, self.m, _ = where_am_i()
        self.bit = 1 + self.s

    def block(self, col, c):
        return half(self.full.at[:, col], c)

    def near(self):
        return pltpu.make_async_copy(half(self.shard, self.s), half(self.full.at[self.g, self.m], self.s), self.send.at[0])

    def line(self, step):
        src, dst = half(self.shard, self.s), half(self.full.at[self.g, self.m], self.s)
        return remote(src, dst, self.send.at[step], self.recv.at[step], (self.s, 4 * ((self.g + step) % 4) + self.m))

    def column(self, slot, col, peer):
        block = self.block(col, self.s)
        return remote(block, block, self.send.at[slot], self.recv.at[slot], peer)

    def first(self):
        return self.column(4, self.m, (self.s, self.d ^ self.bit))

    def second(self, index):
        return self.column(5 + index, (self.m, self.m ^ self.bit)[index], (self.s, self.d ^ (3 - self.bit)))

    def cols(self, way):
        return (self.m, self.m ^ way, self.m ^ (3 - way), self.m ^ 3)

    def hand(self, index):
        return self.column(7 + index, self.cols(self.bit)[index], (1 - self.s, self.d))

    def start(self):
        self.near().start()
        for step in range(1, 4):
            self.line(step).start()

    def plane(self):
        self.near().wait()
        for step in range(1, 4):
            arrived(half(self.full.at[(self.g + 4 - step) % 4, self.m], self.s), self.recv.at[step])
        self.first().start()
        self.second(0).start()
        self.hand(0).start()

    def onward(self):
        arrived(self.block(self.m ^ self.bit, self.s), self.recv.at[4])
        self.second(1).start()
        self.hand(1).start()

    def over(self):
        for index in range(2):
            arrived(self.block((self.m ^ (3 - self.bit), self.m ^ 3)[index], self.s), self.recv.at[5 + index])
            self.hand(2 + index).start()

    def whole(self):
        for index, col in enumerate(self.cols(3 - self.bit)):
            arrived(self.block(col, 1 - self.s), self.recv.at[7 + index])

    def finish(self):
        for step in range(1, 4):
            self.line(step).wait_send()
        self.first().wait_send()
        for index in range(2):
            self.second(index).wait_send()
        for index in range(4):
            self.hand(index).wait_send()


class Load:
    def __init__(self, src, full, sem):
        self.copy = lambda: pltpu.make_async_copy(src, full, sem.at[0])

    def start(self):
        self.copy().start()

    def whole(self):
        self.copy().wait()

    def plane(self):
        pass

    onward = over = finish = plane


def masks(land, ocean, coarse, pick, patch):
    rows, across = land.shape[0] * land.shape[1], land.shape[2]
    flat = land[...].reshape(rows, across).astype(F32).astype(BF)
    spread = dot(pick, flat)
    at = lax.broadcasted_iota(jnp.int32, spread.shape, 1) - lax.broadcasted_iota(jnp.int32, spread.shape, 0) // 8
    ones = jnp.ones((across, 128), BF)

    def chunk(c, carry):
        ocean[pl.ds(pl.multiple_of(c * 128, 128), 128)] = dot(jnp.where(at == 16 * c, spread, 0.0).astype(BF), ones)
        return carry

    lax.fori_loop(0, ocean.shape[0] // 128, chunk, 0)
    for b in range(ocean.shape[0] // 256):
        moved = dot(patch, ocean[256 * b : 256 * b + 256].astype(BF))
        coarse[64 * b : 64 * b + 64] = moved[:64] * moved[64:128] * moved[128:192] * moved[192:]


def conv_phase(sec, cols, ns, hook):
    S, kb, ocean, z, stats = ns.S, ns.kb, ns.ocean, ns.z, ns.stats
    taps_to(kb, ns.par[sec], False)
    lanes = S.shape[1]
    wide = kb.shape[2]

    def count_cells(b, t):
        return t + ocean[pl.ds(pl.multiple_of(b * 64, 64), 64)].reshape(8, 8, 128).sum(0)

    tally = lax.fori_loop(0, cols // 8, count_cells, jnp.zeros((8, 128), F32))
    for group in range(wide // 128 // lanes):
        part = slice(group * lanes * 128, (group + 1) * lanes * 128)

        def chunk(c, carry):
            cells = pl.ds(pl.multiple_of(c * 128, 128), 128)
            if sec == 0:
                block = ns.x14[:, c]
                block = dot(block.reshape(-1, block.shape[-1]), ns.spread[:, part]).astype(BF)
                moved = shifted(block, ns.natural[...], S, c)
                ns.a0[cells, part] = moved[384:512].astype(BF)
            else:
                shifted(jnp.concatenate([ns.a1[cells, part], ns.halo[0, c, :, part], ns.halo[1, c, :, part]], axis=0), ns.shifts[...], S, c)
            return carry

        lax.fori_loop(0, cols // 16, chunk, 0)
        wrap(S, cols)
        hook()
        for lane in range(lanes):
            at = slice((group * lanes + lane) * 128, (group * lanes + lane + 1) * 128)

            def step(b, carry):
                first, second = carry
                acc = jnp.zeros((8, 8, 128), F32)
                for i in range(7):
                    window = S[i, lane, pl.ds(b * 8, 14)]
                    for j in range(7):
                        acc = acc + window[j : j + 8] * kb[7 * i + j, :, at][None]
                z[pl.ds(b * 8, 8), :, at] = acc
                kept = acc * ocean[pl.ds(pl.multiple_of(b * 64, 64), 64)].reshape(8, 8, 128)
                return first + kept.sum(0), second + (kept * acc).sum(0)

            zero = jnp.zeros((8, 128), F32)
            first, second = lax.fori_loop(0, cols // 8, step, (zero, zero))
            stats[0:1, at] = first.sum(0, keepdims=True)
            stats[1:2, at] = second.sum(0, keepdims=True)
            stats[2:3, at] = tally.sum(0, keepdims=True)
            stats[3:8, at] = jnp.zeros((5, 128), F32)
            hook()


def ff_phase(sec, ns, st, w1, w2, res, y, nat, kept, hook):
    par = ns.par[sec]
    counted, mean, inverse, gain, shift = norm_terms(st, par)
    wide = ns.z.shape[2]
    steps = ns.z.shape[0] // 32
    stage, sems = (ns.n_st, ns.g_st, ns.gp_st), ns.ff_sem
    w1, w2 = w1.reshape(wide, -1), w2.reshape(-1, wide)
    hidden = w1.shape[1]

    def outs(b, slot):
        at = pl.ds(pl.multiple_of(b * 256, 256), 256)
        return [pltpu.make_async_copy(src.at[slot], dst.at[at], sems.at[k, slot]) for k, (src, dst) in enumerate(zip(stage, kept))]

    def block(b, carry):
        slot = b % 2

        @pl.when(b >= 2)
        def _():
            for copy in outs(b - 2, slot):
                copy.wait()

        z = ns.z[pl.ds(b * 32, 32)].reshape(256, wide)
        at = pl.ds(pl.multiple_of(b * 256, 256), 256)
        normed = ((z - mean) * inverse * gain + shift).astype(BF)
        ns.n_st[slot] = normed
        acc = jnp.zeros((256, wide), F32)
        for h in range(0, hidden, 256):
            cut = slice(h, h + 256)
            e = dot(normed, w1[:, cut]) + ns.bias[sec, 0:1, cut]
            phi = 0.5 + 0.5 * lax.erf(e * np.float32(0.5**0.5))
            act = (e * phi).astype(BF)
            ns.g_st[slot, :, cut] = act
            ns.gp_st[slot, :, cut] = (phi + e * (np.float32((2 * np.pi) ** -0.5) * jnp.exp(-0.5 * e * e))).astype(BF)
            acc = acc + dot(act, w2[cut])
        out = (lanes4(ns.ocean[at], wide) * (res[at].astype(F32) + (acc + par[51:52]))).astype(BF)
        if y is not None:
            y[at] = out
        for k in range(2):
            nat[:, 2 * b + k] = to_natural(out[128 * k : 128 * k + 128], ns.back[...], ns.gather[...])
        for copy in outs(b, slot):
            copy.start()
        for k in range(steps):
            pl.when(b == k)(functools.partial(hook, k))
        return carry

    lax.fori_loop(0, steps, block, 0)
    for b in (steps - 2, steps - 1):
        for copy in outs(b, b % 2):
            copy.wait()


def forward_kernel(fast, count, cols, ns):
    s, d, g, m, p = where_am_i()
    greet_near(count)
    x14 = ns.x14
    x_begin, x_end = collect(ns.x, x14, 3, ns.xs, ns.xr)
    land_begin, land_end = collect_land(ns.land, ns.land2, ns.ls, ns.lr)
    x_begin()
    land_begin()
    pairs = [(ns.mine, ns.par), (ns.mine_bias, ns.bias)] + [(getattr(ns, f"mine{k}"), getattr(ns, f"shard{k}")) for k in range(4) if fast]
    far = [remote(src, dst.at[s], ns.ps.at[k, 0], ns.pr.at[k], (1 - s, d)) for k, (src, dst) in enumerate(pairs)]
    near = [pltpu.make_async_copy(src, dst.at[s], ns.ps.at[k, 1]) for k, (src, dst) in enumerate(pairs)]
    for c in far + near:
        c.start()
    fulls = dict(w1_0=ns.w1_0, w2_0=ns.w2_0, r0=ns.r0, m0=ns.m0, m1=ns.m1, r1=ns.r1, w1_1=ns.w1_1, w2_1=ns.w2_1)
    which = dict(w1_0=(0, 0), w2_0=(1, 0), r0=(2, 0), r1=(2, 1), m0=(3, 0), m1=(3, 1), w1_1=(0, 1), w2_1=(1, 1))
    mats = {}
    for k, (name, full) in enumerate(fulls.items()):
        if fast:
            index, sec = which[name]
            mats[name] = Gather(getattr(ns, f"shard{index}").at[sec], full, ns.gs.at[k], ns.gr.at[k])
        else:
            mats[name] = Load(getattr(ns, name + "_in"), full, ns.gs.at[k])
    saves = {name: lambda k=k, name=name, full=full: pltpu.make_async_copy(full, getattr(ns, name + "_out"), ns.save.at[k]) for k, (name, full) in enumerate(fulls.items())}

    def do(step, *names):
        for name in names:
            getattr(mats[name], step)()

    def whole(*names):
        do("whole", *names)
        for name in names:
            saves[name]().start()

    if fast:
        for k in range(2, 6):
            near[k].wait()
            arrived(pairs[k][1].at[1 - s], ns.pr.at[k])
    do("start", "w1_0", "w2_0")
    do("start", "r0")
    land_end()
    masks(ns.land2, ns.ocean, ns.coarse, ns.pick[...], ns.patch[...])
    x_end()

    def edge(up):
        src, dst = (x14.at[pl.ds(3, 3)], x14.at[pl.ds(11, 3)]) if up else (x14.at[pl.ds(8, 3)], x14.at[pl.ds(0, 3)])
        return remote(src, dst, ns.hs.at[int(up)], ns.hr.at[int(up)], device(p - 1 if up else p + 1, m))

    pl.when(p > 0)(edge(True).start)
    pl.when(p < count - 1)(edge(False).start)
    do("plane", "w1_0", "w2_0")
    for k in range(2):
        near[k].wait()
        arrived(pairs[k][1].at[1 - s], ns.pr.at[k])

    @pl.when(p == 0)
    def _():
        x14[0:3] = jnp.zeros((3,) + x14.shape[1:], BF)

    @pl.when(p == count - 1)
    def _():
        x14[11:14] = jnp.zeros((3,) + x14.shape[1:], BF)

    pl.when(p > 0)(lambda: arrived(x14.at[pl.ds(0, 3)], ns.hr.at[0]))
    pl.when(p < count - 1)(lambda: arrived(x14.at[pl.ds(11, 3)], ns.hr.at[1]))

    def script(*actions):
        queue = list(actions)

        def hook(*_):
            if queue:
                queue.pop(0)()

        return hook

    cot_begin, cot_end = collect(ns.cot, ns.cot8, 0, ns.cs, ns.cr)
    act = deliver(0, ns.nat0, ns.act, ns.bounce, ns.ds_, ns.dr_, ns.db)

    conv_phase(0, cols, ns, script(
        lambda: (do("onward", "w1_0", "w2_0"), do("start", "m0", "m1", "r1")),
        lambda: do("plane", "r0"),
        lambda: do("over", "w1_0", "w2_0"),
        lambda: do("onward", "r0"),
        lambda: do("start", "w1_1", "w2_1"),
        lambda: do("plane", "m0", "m1", "r1"),
    ))
    ns.st0[...] = all_sum(ns.stats, ns.slots, ns.send, ns.recv, count)
    keep_z = pltpu.make_async_copy(ns.z, ns.z0, ns.keep.at[0])
    keep_z.start()
    whole("w1_0", "w2_0")
    ff0 = {0: lambda: do("over", "r0"), 1: lambda: do("onward", "m0", "m1", "r1"), 4: lambda: do("plane", "w1_1", "w2_1")}
    ff_phase(0, ns, ns.st0, ns.w1_0, ns.w2_0, ns.a0, ns.skip, ns.nat0, (ns.n0, ns.g0, ns.gp0), lambda k: ff0.get(k, lambda: None)())

    whole("r0")
    skip, pieces, wide = ns.skip, ns.pieces, ns.skip.shape[1]
    blocks = skip.shape[0] // 256
    down, up_w = ns.r0.reshape(4 * wide, -1), ns.r1.reshape(GROUPS, 2, ns.r1.shape[2] // 2, -1)
    merge = [v.reshape(wide, wide) for v in (ns.m0, ns.m1)]
    for b in range(blocks):
        moved = dot(ns.patch[...], skip[256 * b : 256 * b + 256]).astype(BF)
        for k in range(4):
            pieces[k, 64 * b : 64 * b + 64] = moved[64 * k : 64 * k + 64]
    value = sum(dot(pieces[k], down[wide * k : wide * k + wide]) for k in range(4))
    deep_value = (lanes4(ns.coarse[...], value.shape[1]) * value).astype(BF)
    ns.deep[...] = deep_value
    do("over", "m0", "m1", "r1")
    do("onward", "w1_1", "w2_1")
    act[0]()
    whole("m0", "m1", "r1")
    rows = up_w.shape[0] * up_w.shape[2]
    lifted = [dot(deep_value, up_w[:, i].reshape(rows, -1)).astype(BF) for i in range(2)]
    for b in range(blocks):
        at = slice(256 * b, 256 * b + 256)
        stacked = jnp.concatenate(
            [lifted[i][64 * b : 64 * b + 64, wide * j : wide * j + wide] for i in range(2) for j in range(2)], axis=0
        )
        ns.up[at] = dot(ns.unpatch[...], stacked).astype(BF)
        joined = dot(ns.up[at], merge[0][...]) + dot(skip[at], merge[1][...])
        ns.h[at] = joined
        low = joined.astype(BF)
        ns.a1[at] = low
        for k in range(2):
            ends = dot(ns.edges[...], low[128 * k : 128 * k + 128]).astype(BF)
            ns.packed[0, 2 * b + k] = ends[:48]
            ns.packed[1, 2 * b + k] = ends[48:]
    swap_rows(ns.packed, ns.halo, ns.es, ns.er, count)
    keep_z.wait()
    cot_begin()

    conv_phase(1, cols, ns, script(
        act[1],
        lambda: do("over", "w1_1", "w2_1"),
        lambda: whole("w1_1", "w2_1"),
    ))
    ns.st1[...] = all_sum(ns.stats, ns.slots1, ns.send1, ns.recv1, count)
    keep_z1 = pltpu.make_async_copy(ns.z, ns.z1, ns.keep.at[0])
    keep_z1.start()
    ff_phase(1, ns, ns.st1, ns.w1_1, ns.w2_1, ns.h, None, ns.nat1, (ns.n1, ns.g1, ns.gp1), lambda k: None)

    cot_end()
    act[3]()
    for name, save in saves.items():
        save().wait()
        do("finish", name)
    keep_z1.wait()
    for c in far:
        c.wait_send()
    pl.when(p > 0)(edge(True).wait_send)
    pl.when(p < count - 1)(edge(False).wait_send)


class Names:
    pass


def build(name, body, ins, outs, scratch=None, jobs=(), cid=None, limit=60, **more):
    ins, outs, scratch, alias = dict(ins), dict(outs), dict(scratch or {}), {}
    for job in jobs:
        ins.update(job.ins)
        outs.update(job.outs)
        scratch.update(job.scratch)
        alias.update(job.alias)
    ins = {k: v if isinstance(v, tuple) else (v, VM) for k, v in ins.items()}
    outs = {k: v if len(v) == 3 else v + (VM,) for k, v in outs.items()}
    names = list(ins) + list(outs) + list(scratch)

    def kernel(*refs):
        ns = Names()
        for k, ref in zip(names, refs):
            setattr(ns, k, ref)
        steps = [job.steps(ns) for job in jobs]

        def hook(k):
            for step in steps:
                step[k]()

        body(ns, hook)

    params = dict(vmem_limit_bytes=limit * MEGA)
    if cid is not None:
        params.update(collective_id=cid, has_side_effects=True)
    order_in, order_out = list(ins), list(outs)
    results = pl.pallas_call(
        kernel, name=name, out_shape=[jax.ShapeDtypeStruct(v[0], v[1]) for v in outs.values()],
        in_specs=[v[1] for v in ins.values()], out_specs=[v[2] for v in outs.values()], scratch_shapes=list(scratch.values()),
        input_output_aliases={order_in.index(a): order_out.index(b) for a, b in alias.items()},
        compiler_params=pltpu.CompilerParams(**params), **more,
    )(*[v[0] for v in ins.values()])
    out = Names()
    for k, v in zip(order_out, results):
        setattr(out, k, v)
    return out


def on_device(sections, dps, inputs, cotangent, land, kernel, bn_gain, bn_bias, bias_in, bias_out, w_in, w_out, resample, merge):
    batches, height, cols, c = inputs.shape
    hid = bias_in.shape[1]
    n = resample.shape[1] * dps // (4 * c)
    cw, hw, nw = (GROUPS * padded(v) for v in (c, hid, n))
    cells, deep_cells = cols * 8, cols * 2
    count = 2 * (dps // 4)
    fast = dps == GROUPS
    assert batches == 4 and height == 4 and dps % 4 == 0 and sections == 2 and cols % 32 == 0
    s = lax.axis_index("section")
    mats = {k: jnp.asarray(v) for k, v in matrices(c).items()}
    tiles = cols // 16
    both = ("section", "dp")

    def packs(parts, w1, w2, rd, ru):
        return pack_in(w1, parts, c, hid), pack_in(w2, parts, hid, c), pack_down(rd, parts, c, n), pack_up(ru, parts, c, n)

    shards = []
    if fast:
        w1, w2, rd, ru = packs(1, *(v.astype(BF) for v in (w_in, w_out, resample, resample)))
        shards = [w1[0], w2[0], jnp.where(s == 0, rd, ru)[0], pack_in(merge.astype(BF), 1, c, c)[0]]
    else:
        flat = [lax.all_gather(v.astype(BF).reshape(-1), both, axis=0, tiled=True) for v in (w_in, w_out, resample, merge)]
        halves = [v.reshape(2, -1) for v in flat]
        whole = [packs(GROUPS, halves[0][k], halves[1][k], halves[2][k], halves[2][k]) for k in range(2)]

    rows = jnp.concatenate([kernel[0], bn_gain, bn_bias, bias_out], axis=0)
    mine = grow(grow(rows.reshape(-1, GROUPS, c // GROUPS), (52, GROUPS, padded(c))).reshape(52, cw), (56, cw))
    mine_bias = grow(grow(bias_in.reshape(GROUPS, -1), (GROUPS, padded(hid))).reshape(1, hw), (8, hw))
    x = inputs.reshape(batches, height, tiles, 16, c)
    cot = cotangent.reshape(batches, height, tiles, 16, c)
    land_cols = -(-cols // 128) * 128
    at_any = lambda v: (v, ANY)
    field = lambda t: ((cells, cw), t)
    natural = ((8, tiles, 16, c), BF)
    edge_rows = ((2, tiles, 48, cw), BF)
    exchange = dict(stats=pltpu.VMEM((8, cw), F32), slots=pltpu.VMEM((count // 2 + 1, 8, cw), F32), send=DMA((count,)), recv=DMA((count,)))
    shift_space = dict(S=pltpu.VMEM((7, cw // 128, cols + 6, 8, 128), F32), kb=pltpu.VMEM((49, 8, cw), F32))
    conv_outs = dict(z=((cols, 8, cw), F32), st=((8, cw), F32))

    def only(ns, hook):
        greet_near(count)
        for k in range(4):
            hook(k)


    def backward(name, cid, jobs, sec, top, conv, w1, w2, kept):
        return build(
            name, functools.partial(back_ff_kernel, sec, count),
            dict(top=top, z=conv.z.reshape(cells, cw), st=conv.st, par=par, w1=w1, w2=w2, n=kept.n, g=kept.g, gp=kept.gp, ocean=ocean,
                 spread=mats["spread"], turn=mats["turn"], edges=mats["edges"]),
            dict(dym=field(F32), dw1=((cw, hw), BF), dw2=((hw, cw), BF), small=((8, cw), F32), dz=field(BF), halo=edge_rows),
            dict(dn=pltpu.VMEM((cells, cw), F32), dr=pltpu.VMEM((cells, cw), BF), packed=pltpu.VMEM(*edge_rows), hsend=DMA((2,)), hrecv=DMA((2,)), **exchange),
            jobs, cid,
        )

    def backward_conv(name, cid, jobs, sec, back, a):
        outs = dict(dh=field(BF), dk=((56, cw), F32))
        if sec == 0:
            outs["nat"] = natural
        return build(
            name, functools.partial(back_conv_kernel, sec, count, cols),
            dict(dz=back.dz, halo=back.halo, perm=mats["shifts"], par=par, dym=back.dym, a=a, back=mats["back"], gather=mats["gather"]),
            outs, dict(acc_dk=pltpu.VMEM((49, 8, cw), F32), **shift_space), jobs, cid,
        )

    shapes = [(padded(c), hw), (padded(hid), cw), (4 * padded(c), nw), (padded(c), cw)]
    names = dict(w1_0=0, w2_0=1, r0=2, m0=3, m1=3, r1=2, w1_1=0, w2_1=1)
    ins = dict(x=x, land=grow(land, (8, land_cols)), mine=mine, mine_bias=mine_bias, cot=cot)
    if fast:
        ins.update({f"mine{k}": v for k, v in enumerate(shards)})
    else:
        given = dict(w1_0=whole[0][0], w2_0=whole[0][1], r0=whole[0][2], r1=whole[1][3], w1_1=whole[1][0], w2_1=whole[1][1])
        given.update(m0=pack_in(halves[3][0], GROUPS, c, c), m1=pack_in(halves[3][1], GROUPS, c, c))
        ins.update({k + "_in": v.reshape((4, 4) + shapes[names[k]]) for k, v in given.items()})
    ins = {k: at_any(v) for k, v in ins.items()}
    ins.update({k: mats[k] for k in ("spread", "gather", "natural", "shifts", "patch", "unpatch", "edges", "back", "pick")})
    outs = dict(
        par=((2, 56, cw), F32), bias=((2, 8, hw), F32), ocean=((cells, 128), F32), coarse=((deep_cells, 128), F32),
        st0=((8, cw), F32), st1=((8, cw), F32), a0=field(BF), a1=field(BF), skip=field(BF), up=field(BF),
        pieces=((4, deep_cells, cw), BF), deep=((deep_cells, nw), BF), nat1=natural,
        z0=((cols, 8, cw), F32, ANY), z1=((cols, 8, cw), F32, ANY), cot8=natural + (ANY,), act=((4, 4, tiles, 16, c), BF, ANY),
    )
    for k in range(2):
        outs.update({f"n{k}": field(BF) + (ANY,), f"g{k}": ((cells, hw), BF, ANY), f"gp{k}": ((cells, hw), BF, ANY)})
    outs.update({k + "_out": ((4, 4) + shapes[v], BF, ANY) for k, v in names.items()})
    scratch = dict(
        x14=pltpu.VMEM((14, tiles, 16, c), BF), land2=pltpu.VMEM((2, 8, land_cols), jnp.int32),
        S=pltpu.VMEM((7, 2, cols + 6, 8, 128), F32), kb=pltpu.VMEM((49, 8, cw), F32), z=pltpu.VMEM((cols, 8, cw), F32),
        h=pltpu.VMEM((cells, cw), F32), n_st=pltpu.VMEM((2, 256, cw), BF), g_st=pltpu.VMEM((2, 256, hw), BF), gp_st=pltpu.VMEM((2, 256, hw), BF),
        nat0=pltpu.VMEM(*natural), bounce=pltpu.VMEM(*natural), halo=pltpu.VMEM(*edge_rows), packed=pltpu.VMEM(*edge_rows),
        stats=pltpu.VMEM((8, cw), F32), slots=pltpu.VMEM((count // 2 + 1, 8, cw), F32), slots1=pltpu.VMEM((count // 2 + 1, 8, cw), F32),
        send=DMA((count,)), recv=DMA((count,)), send1=DMA((count,)), recv1=DMA((count,)),
        xs=DMA((4,)), xr=DMA((2,)), ls=DMA((4,)), lr=DMA((2,)), hs=DMA((2,)), hr=DMA((2,)), ps=DMA((6, 2)), pr=DMA((6,)), cs=DMA((4,)), cr=DMA((2,)),
        ds_=DMA((2, 2)), dr_=DMA((4,)), db=DMA((2,)), es=DMA((2,)), er=DMA((2,)), gs=DMA((8, 12)), gr=DMA((8, 12)), save=DMA((8,)), keep=DMA((2,)),
        ff_sem=DMA((3, 2)),
    )
    scratch.update({k: pltpu.VMEM((4, 4) + shapes[v], BF) for k, v in names.items()})
    if fast:
        scratch.update({f"shard{k}": pltpu.VMEM((2,) + shapes[k], BF) for k in range(4)})
    fw = build("forward", lambda ns, hook: forward_kernel(fast, count, cols, ns), ins, outs, scratch, (), 1, 63)
    par, ocean, coarse, bias = fw.par, fw.ocean, fw.coarse, fw.bias
    w1_0, w2_0, w1_1, w2_1 = (v.reshape(r) for v, r in zip((fw.w1_0_out, fw.w2_0_out, fw.w1_1_out, fw.w2_1_out), ((cw, hw), (hw, cw)) * 2))
    r0, r1 = fw.r0_out.reshape(4 * cw, nw), fw.r1_out.reshape(GROUPS, 2, padded(n), 2 * cw)
    mm = jnp.stack([fw.m0_out.reshape(cw, cw), fw.m1_out.reshape(cw, cw)])

    class Kept:
        def __init__(self, k):
            self.z, self.st, self.n, self.g, self.gp, self.a = (getattr(fw, f"{v}{k}") for v in ("z", "st", "n", "g", "gp", "a"))

    conv0, conv1 = Kept(0), Kept(1)
    ff0, ff1 = conv0, conv1

    view = lambda v, k: v.reshape((4, 4) + shapes[k])
    back1 = backward("dec_back", 6, [Deliver("act", 1, fw.nat1, fw.act)], 1, fw.cot8, conv1, w1_1, w2_1, ff1)
    jobs = [PlaneSum("ps", [view(back1.dw1, 0), view(back1.dw2, 1)])] if fast else []
    bconv1 = backward_conv("dec_back_conv", 7, jobs, 1, back1, conv1.a)
    jobs = [LineSum("ls", [(bconv1.psout0, 1), (bconv1.psout1, 1)])] if fast else []
    bmid = build(
        "back_mid", functools.partial(back_mid_kernel, count),
        dict(dh=bconv1.dh, up=fw.up, skip=fw.skip, deep=fw.deep, pieces=fw.pieces, down=r0, up_w=r1, merge=mm, coarse=coarse,
             patch=mats["patch"], unpatch=mats["unpatch"], back=mats["back"], gather=mats["gather"]),
        dict(dmerge=((2, cw, cw), BF), dup_w=((GROUPS, 2, padded(n), 2 * cw), BF), ddown=((4 * cw, nw), BF), dy=field(F32), nat=natural),
        dict(dskip=pltpu.VMEM((cells, cw), BF), dups=pltpu.VMEM((2, deep_cells, 2 * cw), BF), spreads=pltpu.VMEM((4, deep_cells, cw), F32)), jobs, 8,
    )
    jobs = []
    if fast:
        dm = bmid.dmerge.reshape((2, 4, 4) + shapes[3])
        jobs = [PlaneSum("ps", [view(bmid.ddown, 2), view(bmid.dup_w, 2), (dm, 0), (dm, 1)])]
    back0 = backward("enc_back", 9, jobs, 0, bmid.dy, conv0, w1_0, w2_0, ff0)
    jobs = [Deliver("gi", 1, bmid.nat)]
    if fast:
        jobs += [PlaneSum("ps", [view(back0.dw1, 0), view(back0.dw2, 1)]), LineSum("ls", [(getattr(back0, f"psout{k}"), k % 2) for k in range(4)])]
    bconv0 = backward_conv("enc_back_conv", 10, jobs, 0, back0, conv0.a)

    tiny = jnp.stack([jnp.concatenate([dk, small], axis=0) for dk, small in ((bconv0.dk, back0.small), (bconv1.dk, back1.small))])
    jobs = [Deliver("gi", 0, bconv0.nat, bconv0.giout)]
    if fast:
        jobs += [LineSum("ls", [(bconv0.psout0, 0), (bconv0.psout1, 0)])]
        last = build(
            "last", functools.partial(last_kernel, count), dict(small=tiny), dict(total=((64, cw), F32)),
            dict(tiny=pltpu.VMEM((9, 64, cw), F32), ts=DMA((9,)), tr=DMA((9,))), jobs, 11,
        )
        tiny = last.total
        rows_of = lambda v: v.reshape(-1, v.shape[-1])
        gw1 = unpack_in(rows_of(jnp.where(s == 0, last.lsout0, bmid.lsout0)), c, hid)
        gw2 = unpack_in(jnp.where(s == 0, last.lsout1, bmid.lsout1).transpose(1, 0, 2).reshape(padded(hid), cw), hid, c)
        gres = jnp.where(s == 0, unpack_down(rows_of(bconv0.lsout0), c, n), unpack_up(rows_of(bconv0.lsout1), c, n))
        gmm = unpack_in(rows_of(jnp.where(s == 0, bconv0.lsout2, bconv0.lsout3)), c, c)
    else:
        last = build("last", only, {}, {}, {}, jobs, 11)
        scatter = lambda v: lax.psum_scatter(v.astype(F32).reshape(-1), both, scatter_dimension=0, tiled=True)
        gw1 = scatter(jnp.stack([unpack_in(v, c, hid) for v in (back0.dw1, back1.dw1)]))
        gw2 = scatter(jnp.stack([unpack_in(v, hid, c) for v in (back0.dw2, back1.dw2)]))
        gres = scatter(jnp.stack([unpack_down(bmid.ddown, c, n), unpack_up(bmid.dup_w, c, n)]))
        gmm = scatter(jnp.stack([unpack_in(bmid.dmerge[k], c, c) for k in range(2)]))
        tiny = lax.psum(tiny, both)[s]
    activations = back1.actout.reshape(1, batches, height, cols, c)
    grad_input = last.giout.astype(F32).reshape(1, batches, height, cols, c)
    narrow = lambda v: v.reshape(-1, GROUPS, padded(c))[:, :, : c // GROUPS].reshape(-1, c)
    fine = narrow(tiny[:59])
    grad_bias_in = tiny[59:63].reshape(-1)[:hw].reshape(GROUPS, -1)[:, : hid // GROUPS].reshape(1, hid)
    return (
        activations, grad_input, fine[None, :49], fine[57:58], fine[56:57], grad_bias_in, fine[58:59],
        gw1[None], gw2[None], gres[None], gmm,
    )


def solution(mesh):
    sections, dps = mesh.shape["section"], mesh.shape["dp"]
    flat, both = P("section", "dp"), P(("section", "dp"))
    per = P("section", None)
    rows = P(None, "dp", None, None)
    taps = P("section", None, None)
    fields = P("section", None, "dp", None, None)
    return jax.shard_map(
        functools.partial(on_device, sections, dps), mesh=mesh,
        in_specs=(rows, rows, P("dp", None), taps, per, per, per, per, flat, flat, flat, both),
        out_specs=(fields, fields, taps, per, per, per, per, flat, flat, flat, both), check_vma=False,
    )
```

time: 733 us -> 517 us (0.71)
  Pallas kernels: 654 us -> 458 us
  local copies, waits for them, and re-layouts: 51.5 us -> 31.8 us
    pallas_call x14 -> x7, Pallas kernels: 654 us -> 458 us  [build(): pl.pallas_call(kernel, name=name, out_shape=[jax.ShapeDtypeStruct(v[0], v...]
    slice x3 -> x0, local copies, waits for them, and re-layouts: 10.2 us -> none  [the longest x1 4.35 us: feed_forward(): W1[sec]]
where the time goes in v2:
time: 517 us; the launch traced here: 510 us
  Pallas kernels  458 us (89%)
  local copies, waits for them, and re-layouts  31.8 us (6%)
  other arithmetic  18.9 us (4%)
    pallas_call x7, Pallas kernels, build(): pl.pallas_call(kernel, name=name, out_shape=[jax.ShapeDtypeStruct(v[0], v...  458 us

profile of v2, /device:TPU:8, one launch (start us, length us, event | category | flops | bytes accessed | tf_op | source)
XLA Modules:
  0.0 510.0 jit_solution(8814088806832978248)
XLA Ops:
  0.7 0.5 broadcast.57
  1.2 1.3 reduce.25
  2.5 1.3 reduce.24
  3.9 1.3 reduce.23
  5.2 1.3 pad.40.refs_1_
  6.5 0.7 reduce.3
  7.4 0.8 convert_element_type.35
  8.2 0.6 pad.44.refs_3_
  8.8 0.2 reshape.180
  9.1 0.8 squeeze_reshape.11.refs_8_
  9.9 1.3 convert_reduce_fusion.2
  11.2 0.4 reshape.174
  11.6 0.8 squeeze_reshape.9.refs_5_
  12.5 1.3 convert_reduce_fusion.1
  13.8 0.8 convert_reduce_fusion
  14.6 0.1 copy.49
  14.8 0.2 concatenate.27
  15.0 0.2 concatenate.26
  15.2 0.2 concatenate.25
  15.4 0.3 select_maximum_fusion
  15.8 0.7 pad.42.refs_2_
  16.5 0.9 reshape.175
  17.4 0.4 copy.64
  17.9 0.8 copy.57.refs_6_
  18.6 1.2 reshape.176
  19.9 0.3 reshape.177
  20.3 2.0 reshape.178
  22.2 0.3 pad_bitcast_fusion
  22.5 1.2 copy.55
  23.7 0.2 reshape.179
  23.9 0.1 copy.56
  24.1 0.7 broadcast_select_fusion.1.refs_7_
  24.8 162.9 %forward.1 = (f32[2,56,512]{2,1,0:T(8,128)}, f32[2,8,1792]{2,1,0:T(8,128)}, f32[1280,128]{1,0:T(8,128)}, f32[320,128]{1,0:T(8,128)}, f32[8,512]{1,0:T(8,128)}, /...) custom-call(bf16[4,4,10,16,400]{4,3,2,1,0:T(8,128)(2,1)} %bitcast.80, ...), custom_call_target="tpu_custom_call" | custom-call | tf_op jit(solution)/shard_map/forward/pallas_call | solution.py:1082
  187.7 43.4 %dec_back.1 = (f32[1280,512]{1,0:T(8,128)}, bf16[512,1792]{1,0:T(8,128)(2,1)}, bf16[1792,512]{1,0:T(8,128)(2,1)}, f32[8,512]{1,0:T(8,128)}, bf16[1280,512]{1,0:T...) custom-call(bf16[8,10,16,400]{3,2,1,0:T(8,128)(2,1)} %get-tuple-elem, ...), custom_call_target="tpu_custom_call", output_to_operand_aliasing={{6}: (14, {})} | custom-call | tf_op jit(solution)/shard_map/dec_back/pallas_call | solution.py:1082
  231.1 39.1 %dec_back_conv.1 = (bf16[1280,512]{1,0:T(8,128)(2,1)}, f32[56,512]{1,0:T(8,128)}, bf16[4,16,1792]{2,1,0:T(8,128)(2,1)}, bf16[4,112,256]{2,1,0:T(8,128)(2,1)}) custom-call(bf16[1280,512]{1,0:T(8,128)(2,1)} %get-tuple-element.95.refs_0_, bf16[2,10,48,512]{3,2,1,0:T(8,128)(2,1)} %get-tuple-element.96.refs_1_, bf16[896,224]{1,0:T(8,128)(2,1)} %constant.36.clone.refs_12_.refs_2_, ...), custom_call_target="tpu_custom_call" | custom-call | tf_op jit(solution)/shard_map/dec_back_conv/pallas_call | solution.py:1082
  270.3 1.1 pad_maximum_fusion.refs_7_
  271.3 28.0 %back_mid.1 = (bf16[2,512,512]{2,1,0:T(8,128)(2,1)}, bf16[16,2,64,1024]{3,2,1,0:T(8,128)(2,1)}, bf16[2048,1024]{1,0:T(8,128)(2,1)}, f32[1280,512]{1,0:T(8,128)},...) custom-call(bf16[1280,512]{1,0:T(8,128)(2,1)} %get-tuple-element.101.refs_0_, ...), custom_call_target="tpu_custom_call" | custom-call | tf_op jit(solution)/shard_map/back_mid/pallas_call | solution.py:1082
  299.3 69.9 %enc_back.1 = (f32[1280,512]{1,0:T(8,128)}, bf16[512,1792]{1,0:T(8,128)(2,1)}, bf16[1792,512]{1,0:T(8,128)(2,1)}, f32[8,512]{1,0:T(8,128)}, bf16[1280,512]{1,0:T...) custom-call(f32[1280,512]{1,0:T(8,128)} %get-tuple-element.113.refs_, ...), custom_call_target="tpu_custom_call" | custom-call | tf_op jit(solution)/shard_map/enc_back/pallas_call | solution.py:1082
  369.3 51.2 %enc_back_conv.1 = (bf16[1280,512]{1,0:T(8,128)(2,1)}, f32[56,512]{1,0:T(8,128)}, bf16[8,10,16,400]{3,2,1,0:T(8,128)(2,1)}, bf16[4,4,10,16,400]{4,3,2,1,0:T(8,12...) custom-call(bf16[1280,512]{1,0:T(8,128)(2,1)} %get-tuple-element.124, ...), custom_call_target="tpu_custom_call" | custom-call | tf_op jit(solution)/shard_map/enc_back_conv/pallas_call | solution.py:1082
  420.6 0.9 maximum_bitcast_fusion
  421.5 0.7 pad_maximum_fusion.1.refs_0_
  422.2 63.2 %last.1 = (f32[64,512]{1,0:T(8,128)}, bf16[4,4,10,16,400]{4,3,2,1,0:T(8,128)(2,1)}, bf16[8,10,16,400]{3,2,1,0:T(8,128)(2,1)}, f32[2,16,1792]{2,1,0:T(8,128)}, f32[2,112,256]{2,1,0:T(8,128)}) custom-call(f32[2,64,512]{2,1,0:T(8,128)} %pad_maximum_fusion.1.refs_0_, ...), custom_call_target="tpu_custom_call", output_to_operand_aliasing={{1}: (2, {})} | custom-call | tf_op jit(solution)/shard_map/last/pallas_call | solution.py:1082
  485.4 1.0 select_bitcast_fusion
  486.4 1.0 broadcast_select_fusion.2
  487.4 0.7 slice_bitcast_fusion
  488.3 0.7 reshape.202
  488.9 0.2 reshape_reshape.15
  489.1 1.0 broadcast_in_dim_reshape.6
  490.5 0.8 reshape.205
  491.4 0.5 slice_reduce_fusion
  491.9 0.7 slice.64
  492.6 0.7 slice.59
  493.3 0.7 slice.57
  494.0 0.8 copy.63
  494.7 0.4 copy.60
  495.2 1.4 broadcast_in_dim_reshape.7
  496.6 0.3 reshape_reshape.17
  496.9 1.0 reshape.203
  497.9 0.3 copy.61
  498.3 2.6 copy.62
  500.9 3.1 reshape.204
  503.9 1.1 broadcast_select_fusion
  505.0 3.1 convert.1
  508.1 1.5 copy.69
  (51 shorter events, 1.1 us)
Async XLA Ops:
  0.6 13.2 %copy-start.6 = (f32[1,80000]{1,0:T(1,128)S(1)}, f32[1,80000]{1,0:T(1,128)}, u32[]{:S(2)}) copy-start(f32[1,80000]{1,0:T(1,128)} %param.32) | copy-start | bytes 960004
  0.7 14.0 %copy-start.11 = (f32[1,49,400]{2,0,1:T(1,128)S(1)}, f32[1,49,400]{2,0,1:T(1,128)}, u32[]{:S(2)}) copy-start(f32[1,49,400]{2,0,1:T(1,128)} %param.25) | copy-start | bytes 235204
  231.1 39.2 %copy-start.4 = (bf16[4,4,32,512]{3,2,1,0:T(8,128)(2,1)S(1)}, bf16[4,4,32,512]{3,2,1,0:T(8,128)(2,1)}, u32[]{:S(2)}) copy-start(bf16[4,4,32,512]{3,2,1,0:T(8,128)(2,1)} %get-tuple-element.108) | copy-start | bytes 1572868
  231.1 39.2 %copy-start.5 = (bf16[4,4,32,512]{3,2,1,0:T(8,128)(2,1)S(1)}, bf16[4,4,32,512]{3,2,1,0:T(8,128)(2,1)}, u32[]{:S(2)}) copy-start(bf16[4,4,32,512]{3,2,1,0:T(8,128)(2,1)} %get-tuple-element.109) | copy-start | bytes 1572868
  369.3 51.3 %copy-start.10 = (f32[56,512]{1,0:T(8,128)S(1)}, f32[56,512]{1,0:T(8,128)}, u32[]{:S(2)}) copy-start(f32[56,512]{1,0:T(8,128)} %get-tuple-element.137) | copy-start | bytes 344068
  369.3 51.3 %copy-start.14 = (f32[8,512]{1,0:T(8,128)S(1)}, f32[8,512]{1,0:T(8,128)}, u32[]{:S(2)}) copy-start(f32[8,512]{1,0:T(8,128)} %get-tuple-element.138) | copy-start | bytes 49156
  369.3 51.3 %copy-start.15 = (f32[8,512]{1,0:T(8,128)S(1)}, f32[8,512]{1,0:T(8,128)}, u32[]{:S(2)}) copy-start(f32[8,512]{1,0:T(8,128)} %get-tuple-element.136) | copy-start | bytes 49156
  422.2 63.2 %copy-start.8 = (f32[2,112,256]{2,1,0:T(8,128)S(1)}, f32[2,112,256]{2,1,0:T(8,128)}, u32[]{:S(2)}) copy-start(f32[2,112,256]{2,1,0:T(8,128)} %get-tuple-element.148) | copy-start | bytes 688132
  422.2 64.2 %copy-start.7 = (f32[2,16,1792]{2,1,0:T(8,128)S(1)}, f32[2,16,1792]{2,1,0:T(8,128)}, u32[]{:S(2)}) copy-start(f32[2,16,1792]{2,1,0:T(8,128)} %get-tuple-element.146) | copy-start | bytes 688132
  485.4 4.9 copy-start.12
  485.4 4.9 copy-start.13
  486.4 4.9 copy-start.9
  491.4 5.1 %copy-start.3 = (f32[2,64,1024]{2,1,0:T(8,128)S(1)}, f32[2,64,1024]{2,1,0:T(8,128)}, u32[]{:S(2)}) copy-start(f32[2,64,1024]{2,1,0:T(8,128)} %get-tuple-element.149) | copy-start | bytes 1572868
  496.6 1.3 copy-start.2
  500.9 4.1 copy-start.1
  505.0 3.1 copy-start

commit v3 on v2

--- a/solution.py
+++ b/solution.py
@@ -230,199 +230,9 @@
     return counted, mean, inverse, par[49:50], par[50:51]
 
 
-def back_ff_kernel(sec, count, ns, hook):
-    greet_near(count)
-    hook(0)
-    z, w1, w2, dn, dr, small, ocean, edges = ns.z, ns.w1, ns.w2, ns.dn, ns.dr, ns.small, ns.ocean, ns.edges
-    wide = z.shape[1]
-    chunks = z.shape[0] // 128
-    counted, mean, inverse, gain, shift = norm_terms(ns.st, ns.par[sec])
-
-    def begin(c, total):
-        at = pl.ds(pl.multiple_of(c * 128, 128), 128)
-        if sec == 1:
-            block = ns.top[:, c]
-            block = dot(block.reshape(-1, block.shape[-1]), ns.spread[...]).astype(BF)
-            grad = dot(ns.turn[...], block)
-        else:
-            grad = ns.top[at]
-        grad = grad * lanes4(ocean[at], wide)
-        ns.dym[at] = grad
-        low = grad.astype(BF)
-        dr[at] = low
-        return total + rows8(low.astype(F32))
-
-    total = lax.fori_loop(0, chunks, begin, jnp.zeros((8, wide), F32))
-    small[2:3] = total.sum(0, keepdims=True)
-    small[3:8] = jnp.zeros((5, wide), F32)
-    for h in range(0, w1.shape[1], 256):
-        at = slice(h, h + 256)
-        dg = dot_nt(dr[...], w2[at])
-        de = (dg * ns.gp[:, at].astype(F32)).astype(BF)
-        row, col = 3 + h // wide, h % wide
-        small[row : row + 1, col : col + 256] = de.astype(F32).sum(0, keepdims=True)
-        ns.dw1[:, at] = dot_tn(ns.n[...], de).astype(BF)
-        ns.dw2[at] = dot_tn(ns.g[:, at], dr[...]).astype(BF)
-        part = dot_nt(de, w1[:, at])
-        if h == 0:
-            dn[...] = part
-        else:
-            dn[...] += part
-        if h == 512:
-            hook(1)
-
-    def sums(c, carry):
-        at = pl.ds(pl.multiple_of(c * 128, 128), 128)
-        grad = dn[at]
-        return carry[0] + rows8(grad), carry[1] + rows8(grad * ((z[at] - mean) * inverse))
-
-    zero = jnp.zeros((8, wide), F32)
-    plain, scaled = lax.fori_loop(0, chunks, sums, (zero, zero))
-    small[0:1] = plain.sum(0, keepdims=True)
-    small[1:2] = scaled.sum(0, keepdims=True)
-    ns.stats[...] = small[...]
-    summed = all_sum(ns.stats, ns.slots, ns.send, ns.recv, count)
-    first = -inverse * gain * summed[0:1] / counted
-    second = -inverse * inverse * gain * summed[1:2] / counted
-    hook(2)
-
-    def end(c, carry):
-        at = pl.ds(pl.multiple_of(c * 128, 128), 128)
-        grad = inverse * gain * dn[at] + lanes4(ocean[at], wide) * (first + second * (z[at] - mean))
-        low = grad.astype(BF)
-        ns.dz[at] = low
-        ends = dot(edges[...], low).astype(BF)
-        ns.packed[0, c] = ends[:48]
-        ns.packed[1, c] = ends[48:]
-        return carry
-
-    lax.fori_loop(0, chunks, end, 0)
-    swap_rows(ns.packed, ns.halo, ns.hsend, ns.hrecv, count)
-    hook(3)
-
-
-def back_conv_kernel(sec, count, cols, ns, hook):
-    greet_near(count)
-    hook(0)
-    taps_to(ns.kb, ns.par[sec], True)
-    wide = ns.dz.shape[1]
-    S, kb, acc_dk = ns.S, ns.kb, ns.acc_dk
-
-    def chunk(c, carry):
-        block = jnp.concatenate([ns.dz[pl.ds(pl.multiple_of(c * 128, 128), 128)], ns.halo[0, c], ns.halo[1, c]], axis=0)
-        shifted(block, ns.perm[...], S, c)
-        return carry
-
-    lax.fori_loop(0, cols // 16, chunk, 0)
-    wrap(S, cols)
-    acc_dk[...] = jnp.zeros(acc_dk.shape, F32)
-    for lane in range(wide // 128):
-        at = slice(lane * 128, lane * 128 + 128)
-
-        def step(b, carry):
-            cells = pl.ds(pl.multiple_of(b * 64, 64), 64)
-            acc = ns.dym[cells, at].reshape(8, 8, 128)
-            field = ns.a[cells, at].astype(F32).reshape(8, 8, 128)
-            for i in range(7):
-                window = S[i, lane, pl.ds(b * 8, 14)]
-                for j in range(7):
-                    acc = acc + window[j : j + 8] * kb[7 * i + j, :, at][None]
-                    acc_dk[7 * i + j, :, at] += (window[j : j + 8] * field).sum(0)
-            ns.dh[cells, at] = acc.reshape(64, 128).astype(BF)
-            return carry
-
-        lax.fori_loop(0, cols // 8, step, 0)
-        if lane in (1, 2):
-            hook(lane)
-    for k in range(49):
-        ns.dk[48 - k : 49 - k] = acc_dk[k].sum(0, keepdims=True)
-    ns.dk[49:56] = jnp.zeros((7, wide), F32)
-    if sec == 0:
-
-        def out(c, carry):
-            cells = ns.dh[pl.ds(pl.multiple_of(c * 128, 128), 128)]
-            ns.nat[:, c] = to_natural(cells, ns.back[...], ns.gather[...])
-            return carry
-
-        lax.fori_loop(0, cols // 16, out, 0)
-    hook(3)
-
-
-def back_mid_kernel(count, ns, hook):
-    greet_near(count)
-    hook(0)
-    dh, up, skip, deep, pieces, down, up_w, merge = ns.dh, ns.up, ns.skip, ns.deep, ns.pieces, ns.down, ns.up_w, ns.merge
-    dskip, dups, spreads = ns.dskip, ns.dups, ns.spreads
-    wide = dh.shape[1]
-    blocks = dh.shape[0] // 256
-    ns.dmerge[0] = dot_tn(up[...], dh[...]).astype(BF)
-    ns.dmerge[1] = dot_tn(skip[...], dh[...]).astype(BF)
-    for b in range(blocks):
-        at = slice(256 * b, 256 * b + 256)
-        low = dot_nt(dh[at], merge[1]).astype(BF)
-        dskip[at] = low
-        for k in range(2):
-            ns.nat[:, 2 * b + k] = to_natural(low[128 * k : 128 * k + 128], ns.back[...], ns.gather[...])
-        lifted = dot_nt(dh[at], merge[0]).astype(BF)
-        moved = dot(ns.patch[...], lifted).astype(BF)
-        for k in range(4):
-            dups[k // 2, 64 * b : 64 * b + 64, wide * (k % 2) : wide * (k % 2) + wide] = moved[64 * k : 64 * k + 64]
-    hook(1)
-    rows = up_w.shape[0] * up_w.shape[2]
-    ddeep = dot_nt(dups[0], up_w[:, 0].reshape(rows, -1)) + dot_nt(dups[1], up_w[:, 1].reshape(rows, -1))
-    for i in range(2):
-        grad = dot_tn(deep[...], dups[i]).astype(BF)
-        ns.dup_w[:, i] = grad.reshape(up_w.shape[0], up_w.shape[2], -1)
-    masked = (lanes4(ns.coarse[...], ddeep.shape[1]) * ddeep).astype(BF)
-    hook(2)
-    for k in range(4):
-        ns.ddown[wide * k : wide * k + wide] = dot_tn(pieces[k], masked).astype(BF)
-        spreads[k] = dot_nt(masked, down[wide * k : wide * k + wide])
-    for b in range(blocks):
-        value = jnp.concatenate([spreads[k, 64 * b : 64 * b + 64] for k in range(4)], axis=0)
-        high = value.astype(BF)
-        rest = (value - high.astype(F32)).astype(BF)
-        at = slice(256 * b, 256 * b + 256)
-        ns.dy[at] = dskip[at].astype(F32) + (dot(ns.unpatch[...], high) + dot(ns.unpatch[...], rest))
-    hook(3)
-
-
-class Job:
-    def __init__(self, name):
-        self.name, self.ins, self.outs, self.scratch, self.alias = name, {}, {}, {}, {}
-
-    def add(self, kind, name, value):
-        getattr(self, kind)[self.name + name] = value
-
-    def ref(self, ns, name):
-        return getattr(ns, self.name + name)
-
-    def steps(self, ns):
-        return [lambda: None] * 4
-
-
 def start_either(self, src, dst, send, recv, peer):
     pl.when(jnp.logical_not(self))(lambda: remote(src, dst, send, recv, peer).start())
     pl.when(self)(lambda: pltpu.make_async_copy(src, dst, recv).start())
-
-
-class Deliver(Job):
-    def __init__(self, name, sec, natural, before=None):
-        super().__init__(name)
-        self.sec = sec
-        rows, tiles, q, c = natural.shape
-        self.add("ins", "nat", (natural, ANY))
-        self.add("outs", "out", ((4, 4, tiles, q, c), BF, ANY))
-        self.add("outs", "bounce", ((rows, tiles, q, c), BF, ANY))
-        self.add("scratch", "s", DMA((2, 2)))
-        self.add("scratch", "r", DMA((4,)))
-        self.add("scratch", "b", DMA((2,)))
-        if before is not None:
-            self.add("ins", "before", (before, ANY))
-            self.alias = {name + "before": name + "out"}
-
-    def steps(self, ns):
-        return deliver(self.sec, *(self.ref(ns, k) for k in ("nat", "out", "bounce", "s", "r", "b")))
 
 
 def deliver(sec, nat, out, bounce, send, recv, b):
@@ -507,140 +317,6 @@
     return shape[:-2] + ((rows // 2, lanes) if rows % 32 == 0 else (rows, lanes // 2))
 
 
-class PlaneSum(Job):
-    def __init__(self, name, parts):
-        super().__init__(name)
-        self.parts, n = parts, len(parts)
-        for k, v in enumerate(parts):
-            array = v[0] if isinstance(v, tuple) else v
-            self.add("ins", f"in{k}", (array, ANY))
-            shape = half_shape(array.shape[-2:])
-            for bank, lead in (("own", (4, 4)), ("core", (4, 4)), ("one", (4, 2)), ("two", (4,))):
-                self.add("scratch", f"{bank}{k}", pltpu.VMEM(lead + shape, BF))
-            self.add("outs", f"out{k}", ((4,) + shape, BF, VM))
-        for k, width in (("l", 1), ("cs", 1), ("cr", 1), ("as", 2), ("ar", 2), ("bs", 1), ("br", 1)):
-            self.add("scratch", k, DMA((n, width)))
-
-    def steps(self, ns):
-        s, d, g, m, p = where_am_i()
-        sem = {k: self.ref(ns, k) for k in ("l", "cs", "cr", "as", "ar", "bs", "br")}
-        bank = lambda kind, k: self.ref(ns, f"{kind}{k}")
-        bit, every = 1 + s, range(len(self.parts))
-
-        def source(k, c):
-            v, ref = self.parts[k], self.ref(ns, f"in{k}")
-            return half(ref.at[v[1]] if isinstance(v, tuple) else ref, c)
-
-        def near(k):
-            return pltpu.make_async_copy(source(k, s), bank("own", k), sem["l"].at[k, 0])
-
-        def over(k):
-            return remote(source(k, 1 - s), bank("core", k), sem["cs"].at[k, 0], sem["cr"].at[k, 0], (1 - s, d))
-
-        def first(k, index):
-            col = (m ^ bit, m ^ 3)[index]
-            return remote(bank("own", k).at[:, col], bank("one", k).at[:, index], sem["as"].at[k, index], sem["ar"].at[k, index], (s, d ^ bit))
-
-        def second(k):
-            return remote(bank("own", k).at[:, m ^ (3 - bit)], bank("two", k), sem["bs"].at[k, 0], sem["br"].at[k, 0], (s, d ^ (3 - bit)))
-
-        def h0():
-            for k in every:
-                over(k).start()
-                near(k).start()
-
-        def h1():
-            for k in every:
-                own, core = bank("own", k), bank("core", k)
-                near(k).wait()
-                arrived(core, sem["cr"].at[k, 0])
-
-                def add(b, carry, own=own, core=core):
-                    own[b // 4, b % 4] = (own[b // 4, b % 4].astype(F32) + core[b // 4, b % 4].astype(F32)).astype(BF)
-                    return carry
-
-                lax.fori_loop(0, 16, add, 0)
-                first(k, 1).start()
-                first(k, 0).start()
-
-        def h2():
-            for k in every:
-                own, one, rest = bank("own", k), bank("one", k), m ^ (3 - bit)
-                arrived(one.at[:, 1], sem["ar"].at[k, 1])
-                for z in range(4):
-                    own[z, rest] = (own[z, rest].astype(F32) + one[z, 1].astype(F32)).astype(BF)
-                second(k).start()
-
-        def h3():
-            for k in every:
-                own, one, two, out = (bank(n, k) for n in ("own", "one", "two", "out"))
-                arrived(one.at[:, 0], sem["ar"].at[k, 0])
-                arrived(two, sem["br"].at[k, 0])
-                for z in range(4):
-                    out[z] = (own[z, m].astype(F32) + one[z, 0].astype(F32) + two[z].astype(F32)).astype(BF)
-                first(k, 0).wait_send()
-                first(k, 1).wait_send()
-                second(k).wait_send()
-                over(k).wait_send()
-
-        return [h0, h1, h2, h3]
-
-
-class LineSum(Job):
-    def __init__(self, name, columns):
-        super().__init__(name)
-        self.secs = [sec for _, sec in columns]
-        n = len(columns)
-        for k, (v, _) in enumerate(columns):
-            self.add("ins", f"in{k}", (v, ANY))
-            self.add("outs", f"out{k}", ((2,) + v.shape[1:], F32, VM))
-            self.add("scratch", f"line{k}", pltpu.VMEM(v.shape, BF))
-            self.add("scratch", f"mine{k}", pltpu.VMEM(v.shape[1:], F32))
-        for k, width in (("s", 4), ("r", 4), ("c", 2)):
-            self.add("scratch", k, DMA((n, width)))
-
-    def steps(self, ns):
-        s, d, g, m, p = where_am_i()
-        send, recv, sem = self.ref(ns, "s"), self.ref(ns, "r"), self.ref(ns, "c")
-        every = list(enumerate(self.secs))
-
-        def near(k):
-            return pltpu.make_async_copy(self.ref(ns, f"in{k}").at[g], self.ref(ns, f"line{k}").at[0], send.at[k, 0])
-
-        def far(k, step):
-            to = (g + step) % 4
-            return remote(self.ref(ns, f"in{k}").at[to], self.ref(ns, f"line{k}").at[step], send.at[k, step], recv.at[k, step], (s, 4 * to + m))
-
-        def give(k):
-            return remote(self.ref(ns, f"mine{k}"), self.ref(ns, f"out{k}").at[s], sem.at[k, 0], sem.at[k, 1], (1 - s, d))
-
-        def begin():
-            for k, _ in every:
-                near(k).start()
-                for step in range(1, 4):
-                    far(k, step).start()
-
-        def end():
-            for k, sec in every:
-                line, mine, out = (self.ref(ns, f"{n}{k}") for n in ("line", "mine", "out"))
-                near(k).wait()
-                for step in range(1, 4):
-                    arrived(line.at[step], recv.at[k, step])
-                    far(k, step).wait_send()
-                mine[...] = sum(line[z].astype(F32) for z in range(4))
-                pl.when(s != sec)(give(k).start)
-
-                @pl.when(s == sec)
-                def _(out=out, mine=mine):
-                    out[s] = mine[...]
-
-            for k, sec in every:
-                pl.when(s != sec)(give(k).wait_send)
-                pl.when(s == sec)(lambda k=k: arrived(self.ref(ns, f"out{k}").at[1 - s], sem.at[k, 1]))
-
-        return [begin, lambda: None, lambda: None, end]
-
-
 def collect_land(land, out, send, recv):
     s, d, g, m, p = where_am_i()
     core, dp = device(d // 2, 0)
@@ -667,32 +343,18 @@
     return begin, end
 
 
-def last_kernel(count, ns, hook):
-    s, d, g, m, p = where_am_i()
-    greet_near(count)
-    hook(0)
-    tiny, small, ts, tr = ns.tiny, ns.small, ns.ts, ns.tr
-    over = remote(small.at[1 - s], tiny.at[0], ts.at[0], tr.at[0], (1 - s, d))
-    over.start()
-    arrived(tiny.at[0], tr.at[0])
-    over.wait_send()
-    tiny[1] = small[s] + tiny[0]
-    for base, peer in ((1, lambda step: (s, 4 * ((g + step) % 4) + m)), (5, lambda step: (s, d ^ step))):
-        sent = [remote(tiny.at[base], tiny.at[base + step], ts.at[base + step], tr.at[base + step], peer(step)) for step in range(1, 4)]
-        for c in sent:
-            c.start()
-        for step in range(1, 4):
-            arrived(tiny.at[base + step], tr.at[base + step])
-        for c in sent:
-            c.wait_send()
-        total = tiny[base] + tiny[base + 1] + tiny[base + 2] + tiny[base + 3]
-        if base == 1:
-            tiny[5] = total
-        else:
-            ns.total[...] = total
-    hook(1)
-    hook(2)
-    hook(3)
+def script(*actions):
+    queue = list(actions)
+
+    def hook(*_):
+        if queue:
+            queue.pop(0)()
+
+    return hook
+
+
+def nothing():
+    pass
 
 
 class Gather:
@@ -962,15 +624,6 @@
 
     pl.when(p > 0)(lambda: arrived(x14.at[pl.ds(0, 3)], ns.hr.at[0]))
     pl.when(p < count - 1)(lambda: arrived(x14.at[pl.ds(11, 3)], ns.hr.at[1]))
-
-    def script(*actions):
-        queue = list(actions)
-
-        def hook(*_):
-            if queue:
-                queue.pop(0)()
-
-        return hook
 
     cot_begin, cot_end = collect(ns.cot, ns.cot8, 0, ns.cs, ns.cr)
     act = deliver(0, ns.nat0, ns.act, ns.bounce, ns.ds_, ns.dr_, ns.db)
@@ -1048,17 +701,401 @@
     pl.when(p < count - 1)(edge(False).wait_send)
 
 
+class Reduce:
+    def __init__(self, sec, partial, bank, out, send, recv):
+        self.sec, self.partial, self.out, self.send, self.recv = sec, partial, out, send, recv
+        self.own, self.core, self.one, self.two, self.row, self.mine = bank
+        self.s, self.d, self.g, self.m, _ = where_am_i()
+        self.bit = 1 + self.s
+        self.rest = self.m ^ (3 - self.bit)
+
+    def near(self):
+        return pltpu.make_async_copy(half(self.partial, self.s), self.own, self.send.at[0])
+
+    def over(self):
+        return remote(half(self.partial, 1 - self.s), self.core, self.send.at[1], self.recv.at[1], (1 - self.s, self.d))
+
+    def first(self, index):
+        col = (self.m ^ self.bit, self.m ^ 3)[index]
+        return remote(self.own.at[:, col], self.one.at[:, index], self.send.at[2 + index], self.recv.at[2 + index], (self.s, self.d ^ self.bit))
+
+    def second(self):
+        return remote(self.own.at[:, self.rest], self.two, self.send.at[4], self.recv.at[4], (self.s, self.d ^ (3 - self.bit)))
+
+    def along(self, step):
+        to = (self.g + step) % 4
+        return remote(self.own.at[to, self.m], self.row.at[step - 1], self.send.at[4 + step], self.recv.at[4 + step], (self.s, 4 * to + self.m))
+
+    def give(self):
+        return remote(self.mine, self.out.at[self.s], self.send.at[8], self.recv.at[8], (1 - self.s, self.d))
+
+    def start(self):
+        self.over().start()
+        self.near().start()
+
+    def plane(self):
+        self.near().wait()
+        arrived(self.core, self.recv.at[1])
+        own, core, m, bit = self.own, self.core, self.m, self.bit
+
+        def add(k, carry):
+            z, col = k % 4, (m ^ 3, m ^ bit, m ^ (3 - bit), m)
+            for c in col:
+                own[z, c] = (own[z, c].astype(F32) + core[z, c].astype(F32)).astype(BF)
+            return carry
+
+        lax.fori_loop(0, 4, add, 0)
+        self.first(1).start()
+        self.first(0).start()
+
+    def onward(self):
+        own, one, rest = self.own, self.one, self.rest
+        arrived(one.at[:, 1], self.recv.at[3])
+
+        def add(z, carry):
+            own[z, rest] = (own[z, rest].astype(F32) + one[z, 1].astype(F32)).astype(BF)
+            return carry
+
+        lax.fori_loop(0, 4, add, 0)
+        self.second().start()
+
+    def line(self):
+        own, one, two, m = self.own, self.one, self.two, self.m
+        arrived(one.at[:, 0], self.recv.at[2])
+        arrived(two, self.recv.at[4])
+
+        def add(z, carry):
+            own[z, m] = (own[z, m].astype(F32) + one[z, 0].astype(F32) + two[z].astype(F32)).astype(BF)
+            return carry
+
+        lax.fori_loop(0, 4, add, 0)
+        for step in range(1, 4):
+            self.along(step).start()
+
+    def total(self):
+        for step in range(1, 4):
+            arrived(self.row.at[step - 1], self.recv.at[4 + step])
+        row = self.row
+        self.mine[...] = self.own[self.g, self.m].astype(F32) + row[0].astype(F32) + row[1].astype(F32) + row[2].astype(F32)
+        pl.when(self.s != self.sec)(lambda: self.give().start())
+
+        @pl.when(self.s == self.sec)
+        def _():
+            self.out[self.s] = self.mine[...]
+
+    def finish(self):
+        self.over().wait_send()
+        for index in range(2):
+            self.first(index).wait_send()
+        self.second().wait_send()
+        for step in range(1, 4):
+            self.along(step).wait_send()
+        pl.when(self.s != self.sec)(lambda: self.give().wait_send())
+        pl.when(self.s == self.sec)(lambda: arrived(self.out.at[1 - self.s], self.recv.at[8]))
+
+
+def reduce_bank(name, shape):
+    part = half_shape(shape)
+    out = {f"{name}_{k}": pltpu.VMEM(lead + part, BF) for k, lead in (("own", (4, 4)), ("core", (4, 4)), ("one", (4, 2)), ("two", (4,)), ("row", (3,)))}
+    out.update({f"{name}_mine": pltpu.VMEM(part, F32), f"{name}_s": DMA((9,)), f"{name}_r": DMA((9,))})
+    return out
+
+
+def reducer(ns, name, sec, partial, out):
+    bank = [getattr(ns, f"{name}_{k}") for k in ("own", "core", "one", "two", "row", "mine")]
+    return Reduce(sec, partial, bank, out, getattr(ns, f"{name}_s"), getattr(ns, f"{name}_r"))
+
+
+def loads(pairs, sems, first=0):
+    copies = [pltpu.make_async_copy(src, dst, sems.at[first + k]) for k, (src, dst) in enumerate(pairs)]
+    for c in copies:
+        c.start()
+    return [c.wait for c in copies]
+
+
+def back_ff_phase(sec, count, ns, top, kept, w_in, w_out, hook, done):
+    z_in, st, n_in, g_in, gp_in = kept
+    cells, wide = ns.dym.shape
+    hidden = w_in.shape[1]
+    chunks = cells // 128
+    ocean, small, dr_rows, dym = ns.ocean, ns.small, None, ns.dym
+    counted, mean, inverse, gain, shift = norm_terms(st, ns.par[sec])
+
+    def phase(w1, w2, z, n, g, gp, dn, dr):
+        def columns(h):
+            at, slot = pl.ds(256 * h, 256), h % 2
+            return [pltpu.make_async_copy(src.at[:, at], dst.at[slot], ns.col_sem.at[k, slot]) for k, (src, dst) in enumerate(((g_in, g), (gp_in, gp)))]
+
+        got_w2, got_w1, got_n, got_z = loads([(w_out, w2), (w_in, w1), (n_in, n), (z_in, z)], ns.load_sem)
+        for copy in columns(0):
+            copy.start()
+
+        def begin(c, total):
+            at = pl.ds(pl.multiple_of(c * 128, 128), 128)
+            if sec == 1:
+                block = top[:, c]
+                block = dot(block.reshape(-1, block.shape[-1]), ns.spread[...]).astype(BF)
+                grad = dot(ns.turn[...], block)
+            else:
+                grad = top[at]
+            grad = grad * lanes4(ocean[at], wide)
+            dym[at] = grad
+            low = grad.astype(BF)
+            dr[at] = low
+            return total + rows8(low.astype(F32))
+
+        total = lax.fori_loop(0, chunks, begin, jnp.zeros((8, wide), F32))
+        small[2:3] = total.sum(0, keepdims=True)
+        small[3:8] = jnp.zeros((5, wide), F32)
+        got_w2()
+        for h in range(hidden // 256):
+            at, slot = slice(256 * h, 256 * h + 256), h % 2
+            if h + 1 < hidden // 256:
+                for copy in columns(h + 1):
+                    copy.start()
+            dg = dot_nt(dr[...], w2[at])
+            if h == 0:
+                got_n()
+                got_w1()
+            for copy in columns(h):
+                copy.wait()
+            de = (dg * gp[slot].astype(F32)).astype(BF)
+            row, col = 3 + 256 * h // wide, 256 * h % wide
+            small[row : row + 1, col : col + 256] = de.astype(F32).sum(0, keepdims=True)
+            ns.dw1[:, at] = dot_tn(n[...], de).astype(BF)
+            ns.dw2[at] = dot_tn(g[slot], dr[...]).astype(BF)
+            part = dot_nt(de, w1[:, at])
+            if h == 0:
+                dn[...] = part
+            else:
+                dn[...] += part
+            hook(h)
+        done()
+        got_z()
+
+        def sums(c, carry):
+            at = pl.ds(pl.multiple_of(c * 128, 128), 128)
+            grad = dn[at]
+            return carry[0] + rows8(grad), carry[1] + rows8(grad * ((z[at] - mean) * inverse))
+
+        zero = jnp.zeros((8, wide), F32)
+        plain, scaled = lax.fori_loop(0, chunks, sums, (zero, zero))
+        small[0:1] = plain.sum(0, keepdims=True)
+        small[1:2] = scaled.sum(0, keepdims=True)
+        ns.stats[...] = small[...]
+        summed = all_sum(ns.stats, ns.slots, ns.send, ns.recv, count)
+        first = -inverse * gain * summed[0:1] / counted
+        second = -inverse * inverse * gain * summed[1:2] / counted
+
+        def end(c, carry):
+            at = pl.ds(pl.multiple_of(c * 128, 128), 128)
+            grad = inverse * gain * dn[at] + lanes4(ocean[at], wide) * (first + second * (z[at] - mean))
+            low = grad.astype(BF)
+            ns.dz[at] = low
+            ends = dot(ns.edges[...], low).astype(BF)
+            ns.packed[0, c] = ends[:48]
+            ns.packed[1, c] = ends[48:]
+            return carry
+
+        lax.fori_loop(0, chunks, end, 0)
+
+    field = lambda t: pltpu.VMEM((cells, wide), t)
+    pl.run_scoped(
+        phase, pltpu.VMEM(w_in.shape, BF), pltpu.VMEM(w_out.shape, BF), field(F32), field(BF),
+        pltpu.VMEM((2, cells, 256), BF), pltpu.VMEM((2, cells, 256), BF), field(F32), field(BF),
+    )
+    swap_rows(ns.packed, ns.halo, ns.hsend, ns.hrecv, count)
+
+
+def back_conv_phase(sec, cols, ns, a_in, tiny, hook):
+    cells, wide = ns.dz.shape
+    dz = ns.dz
+
+    def phase(S, kb, acc_dk, a):
+        (got_a,) = loads([(a_in, a)], ns.load_sem)
+        taps_to(kb, ns.par[sec], True)
+        acc_dk[...] = jnp.zeros(acc_dk.shape, F32)
+        lanes = S.shape[1]
+        for group in range(wide // 128 // lanes):
+            part = slice(group * lanes * 128, (group + 1) * lanes * 128)
+
+            def chunk(c, carry):
+                block = jnp.concatenate([dz[pl.ds(pl.multiple_of(c * 128, 128), 128), part], ns.halo[0, c, :, part], ns.halo[1, c, :, part]], axis=0)
+                shifted(block, ns.shifts[...], S, c)
+                return carry
+
+            lax.fori_loop(0, cols // 16, chunk, 0)
+            wrap(S, cols)
+            hook()
+            if group == 0:
+                got_a()
+            for lane in range(lanes):
+                at = slice((group * lanes + lane) * 128, (group * lanes + lane + 1) * 128)
+
+                def step(b, carry):
+                    rows = pl.ds(pl.multiple_of(b * 64, 64), 64)
+                    acc = ns.dym[rows, at].reshape(8, 8, 128)
+                    field = a[rows, at].astype(F32).reshape(8, 8, 128)
+                    for i in range(7):
+                        window = S[i, lane, pl.ds(b * 8, 14)]
+                        for j in range(7):
+                            acc = acc + window[j : j + 8] * kb[7 * i + j, :, at][None]
+                            acc_dk[7 * i + j, :, at] += (window[j : j + 8] * field).sum(0)
+                    dz[rows, at] = acc.reshape(64, 128).astype(BF)
+                    return carry
+
+                lax.fori_loop(0, cols // 8, step, 0)
+                hook()
+        for k in range(49):
+            tiny[48 - k : 49 - k] = acc_dk[k].sum(0, keepdims=True)
+        tiny[49:56] = jnp.zeros((7, wide), F32)
+
+    pl.run_scoped(
+        phase, pltpu.VMEM((7, 2, cols + 6, 8, 128), F32), pltpu.VMEM((49, 8, wide), F32), pltpu.VMEM((49, 8, wide), F32), pltpu.VMEM((cells, wide), BF)
+    )
+
+
+def back_mid_phase(ns, hook):
+    dh = ns.dz
+    cells, wide = dh.shape
+    blocks = cells // 256
+
+    def phase(skip, up, merge0, merge1, up_w, deep, down, pieces, dups, spreads):
+        got = loads(
+            [(ns.up, up), (ns.skip, skip), (ns.m1, merge1), (ns.m0, merge0), (ns.r1, up_w), (ns.deep, deep), (ns.pieces, pieces), (ns.r0, down)],
+            ns.load_sem,
+        )
+        for k in range(4):
+            got[k]()
+        ns.dm0[...] = dot_tn(up[...], dh[...]).astype(BF)
+        ns.dm1[...] = dot_tn(skip[...], dh[...]).astype(BF)
+        hook(0)
+        for b in range(blocks):
+            at = slice(256 * b, 256 * b + 256)
+            low = dot_nt(dh[at], merge1[...]).astype(BF)
+            ns.dym[at] = low.astype(F32)
+            for k in range(2):
+                ns.nat[:, 2 * b + k] = to_natural(low[128 * k : 128 * k + 128], ns.back[...], ns.gather[...])
+            lifted = dot_nt(dh[at], merge0[...]).astype(BF)
+            moved = dot(ns.patch[...], lifted).astype(BF)
+            for k in range(4):
+                dups[k // 2, 64 * b : 64 * b + 64, wide * (k % 2) : wide * (k % 2) + wide] = moved[64 * k : 64 * k + 64]
+        hook(1)
+        rows = up_w.shape[0] * up_w.shape[2]
+        got[4]()
+        ddeep = dot_nt(dups[0], up_w[:, 0].reshape(rows, -1)) + dot_nt(dups[1], up_w[:, 1].reshape(rows, -1))
+        got[5]()
+        for i in range(2):
+            ns.dr1[:, i] = dot_tn(deep[...], dups[i]).astype(BF).reshape(up_w.shape[0], up_w.shape[2], -1)
+        masked = (lanes4(ns.coarse[...], ddeep.shape[1]) * ddeep).astype(BF)
+        hook(2)
+        got[6]()
+        got[7]()
+        for k in range(4):
+            ns.dr0[wide * k : wide * k + wide] = dot_tn(pieces[k], masked).astype(BF)
+            spreads[k] = dot_nt(masked, down[wide * k : wide * k + wide])
+        hook(3)
+        for b in range(blocks):
+            value = jnp.concatenate([spreads[k, 64 * b : 64 * b + 64] for k in range(4)], axis=0)
+            high = value.astype(BF)
+            rest = (value - high.astype(F32)).astype(BF)
+            at = slice(256 * b, 256 * b + 256)
+            ns.dym[at] += dot(ns.unpatch[...], high) + dot(ns.unpatch[...], rest)
+
+    like = lambda ref: pltpu.VMEM(ref.shape, BF)
+    deep_cells = ns.deep.shape[0]
+    pl.run_scoped(
+        phase, like(ns.skip), like(ns.up), like(ns.m0), like(ns.m1), like(ns.r1), like(ns.deep), like(ns.r0), like(ns.pieces),
+        pltpu.VMEM((2, deep_cells, 2 * wide), BF), pltpu.VMEM((4, deep_cells, wide), F32),
+    )
+
+
+def back_decoder_kernel(fast, count, cols, ns):
+    greet_near(count)
+    act = deliver(1, ns.nat1, ns.act, ns.bounce, ns.ds_, ns.dr_, ns.db)
+    act[0]()
+    sums = []
+    if fast:
+        grid = lambda ref, like: ref.reshape((4, 4) + like.shape[-2:])
+        sums = [reducer(ns, f"w{k}", 1, ref, out) for k, (ref, out) in enumerate(((ns.dw1.reshape(4, 4, -1, ns.dw1.shape[1]), ns.gw1), (ns.dw2.reshape(4, 4, -1, ns.dw2.shape[1]), ns.gw2)))]
+
+    def all_(step):
+        return lambda: [getattr(r, step)() for r in sums]
+
+    back_ff_phase(1, count, ns, ns.top, (ns.z, ns.st, ns.n, ns.g, ns.gp), ns.w1, ns.w2, lambda h: act[1]() if h == 2 else None, all_("start"))
+    back_conv_phase(1, cols, ns, ns.a, ns.tiny, script(all_("plane"), nothing, all_("onward"), act[3], nothing, all_("line")))
+    ns.tiny[56:64] = ns.small[...]
+    back_mid_phase(ns, script(nothing, all_("total"), nothing, nothing))
+    all_("finish")()
+
+
+def back_encoder_kernel(fast, count, cols, ns):
+    s, d, g, m, p = where_am_i()
+    greet_near(count)
+    gi1 = deliver(1, ns.nat1, ns.gi, ns.bounce1, ns.ds1, ns.dr1_, ns.db1)
+    gi0 = deliver(0, ns.nat0, ns.gi, ns.bounce0, ns.ds0, ns.dr0_, ns.db0)
+    deep, mats = [], []
+    if fast:
+        deep = [reducer(ns, f"r{k}", sec, getattr(ns, part), getattr(ns, out)) for k, (sec, part, out) in enumerate(
+            ((0, "pr0", "gr0"), (1, "pr1", "gr1"), (0, "pm0", "gm0"), (1, "pm1", "gm1")))]
+        mats = [reducer(ns, f"w{k}", 0, ref, out) for k, (ref, out) in enumerate(((ns.dw1.reshape(4, 4, -1, ns.dw1.shape[1]), ns.gw1), (ns.dw2.reshape(4, 4, -1, ns.dw2.shape[1]), ns.gw2)))]
+
+    def all_(step, group):
+        return lambda: [getattr(r, step)() for r in group]
+
+    all_("start", deep)()
+    gi1[0]()
+    steps = {1: all_("plane", deep), 3: gi1[1]}
+    back_ff_phase(0, count, ns, ns.top, (ns.z, ns.st, ns.n, ns.g, ns.gp), ns.w1, ns.w2, lambda h: steps.get(h, nothing)(), all_("start", mats))
+    back_conv_phase(0, cols, ns, ns.a, ns.tiny0, script(
+        all_("onward", deep), all_("plane", mats), all_("line", deep), lambda: (all_("onward", mats)(), gi1[3]()), nothing, all_("line", mats)))
+    ns.tiny0[56:64] = ns.small[...]
+
+    def out(c, carry):
+        cells = ns.dz[pl.ds(pl.multiple_of(c * 128, 128), 128)]
+        ns.nat0[:, c] = to_natural(cells, ns.back[...], ns.gather[...])
+        return carry
+
+    lax.fori_loop(0, cols // 16, out, 0)
+    gi0[0]()
+    all_("total", deep)()
+    if fast:
+        sm, tiny, ts, tr = ns.sm, ns.tiny, ns.ts, ns.tr
+        sm[0] = ns.tiny0[...]
+        sm[1] = ns.tiny1[...]
+        over = remote(sm.at[1 - s], tiny.at[0], ts.at[0], tr.at[0], (1 - s, d))
+        over.start()
+        arrived(tiny.at[0], tr.at[0])
+        over.wait_send()
+        tiny[1] = sm[s] + tiny[0]
+        for base, peer in ((1, lambda step: (s, 4 * ((g + step) % 4) + m)), (5, lambda step: (s, d ^ step))):
+            sent = [remote(tiny.at[base], tiny.at[base + step], ts.at[base + step], tr.at[base + step], peer(step)) for step in range(1, 4)]
+            for c in sent:
+                c.start()
+            if base == 1:
+                gi0[1]()
+            for step in range(1, 4):
+                arrived(tiny.at[base + step], tr.at[base + step])
+            for c in sent:
+                c.wait_send()
+            total = tiny[base] + tiny[base + 1] + tiny[base + 2] + tiny[base + 3]
+            if base == 1:
+                tiny[5] = total
+            else:
+                ns.total[...] = total
+    else:
+        gi0[1]()
+        ns.total[...] = ns.tiny0[...]
+    all_("total", mats)()
+    all_("finish", deep + mats)()
+    gi0[3]()
+
+
 class Names:
     pass
 
 
-def build(name, body, ins, outs, scratch=None, jobs=(), cid=None, limit=60, **more):
-    ins, outs, scratch, alias = dict(ins), dict(outs), dict(scratch or {}), {}
-    for job in jobs:
-        ins.update(job.ins)
-        outs.update(job.outs)
-        scratch.update(job.scratch)
-        alias.update(job.alias)
+def build(name, body, ins, outs, scratch, alias, cid, limit):
     ins = {k: v if isinstance(v, tuple) else (v, VM) for k, v in ins.items()}
     outs = {k: v if len(v) == 3 else v + (VM,) for k, v in outs.items()}
     names = list(ins) + list(outs) + list(scratch)
@@ -1067,23 +1104,14 @@
         ns = Names()
         for k, ref in zip(names, refs):
             setattr(ns, k, ref)
-        steps = [job.steps(ns) for job in jobs]
-
-        def hook(k):
-            for step in steps:
-                step[k]()
-
-        body(ns, hook)
-
-    params = dict(vmem_limit_bytes=limit * MEGA)
-    if cid is not None:
-        params.update(collective_id=cid, has_side_effects=True)
+        body(ns)
+
     order_in, order_out = list(ins), list(outs)
     results = pl.pallas_call(
         kernel, name=name, out_shape=[jax.ShapeDtypeStruct(v[0], v[1]) for v in outs.values()],
         in_specs=[v[1] for v in ins.values()], out_specs=[v[2] for v in outs.values()], scratch_shapes=list(scratch.values()),
         input_output_aliases={order_in.index(a): order_out.index(b) for a, b in alias.items()},
-        compiler_params=pltpu.CompilerParams(**params), **more,
+        compiler_params=pltpu.CompilerParams(vmem_limit_bytes=limit * MEGA, collective_id=cid, has_side_effects=True),
     )(*[v[0] for v in ins.values()])
     out = Names()
     for k, v in zip(order_out, results):
@@ -1127,36 +1155,6 @@
     field = lambda t: ((cells, cw), t)
     natural = ((8, tiles, 16, c), BF)
     edge_rows = ((2, tiles, 48, cw), BF)
-    exchange = dict(stats=pltpu.VMEM((8, cw), F32), slots=pltpu.VMEM((count // 2 + 1, 8, cw), F32), send=DMA((count,)), recv=DMA((count,)))
-    shift_space = dict(S=pltpu.VMEM((7, cw // 128, cols + 6, 8, 128), F32), kb=pltpu.VMEM((49, 8, cw), F32))
-    conv_outs = dict(z=((cols, 8, cw), F32), st=((8, cw), F32))
-
-    def only(ns, hook):
-        greet_near(count)
-        for k in range(4):
-            hook(k)
-
-
-    def backward(name, cid, jobs, sec, top, conv, w1, w2, kept):
-        return build(
-            name, functools.partial(back_ff_kernel, sec, count),
-            dict(top=top, z=conv.z.reshape(cells, cw), st=conv.st, par=par, w1=w1, w2=w2, n=kept.n, g=kept.g, gp=kept.gp, ocean=ocean,
-                 spread=mats["spread"], turn=mats["turn"], edges=mats["edges"]),
-            dict(dym=field(F32), dw1=((cw, hw), BF), dw2=((hw, cw), BF), small=((8, cw), F32), dz=field(BF), halo=edge_rows),
-            dict(dn=pltpu.VMEM((cells, cw), F32), dr=pltpu.VMEM((cells, cw), BF), packed=pltpu.VMEM(*edge_rows), hsend=DMA((2,)), hrecv=DMA((2,)), **exchange),
-            jobs, cid,
-        )
-
-    def backward_conv(name, cid, jobs, sec, back, a):
-        outs = dict(dh=field(BF), dk=((56, cw), F32))
-        if sec == 0:
-            outs["nat"] = natural
-        return build(
-            name, functools.partial(back_conv_kernel, sec, count, cols),
-            dict(dz=back.dz, halo=back.halo, perm=mats["shifts"], par=par, dym=back.dym, a=a, back=mats["back"], gather=mats["gather"]),
-            outs, dict(acc_dk=pltpu.VMEM((49, 8, cw), F32), **shift_space), jobs, cid,
-        )
-
     shapes = [(padded(c), hw), (padded(hid), cw), (4 * padded(c), nw), (padded(c), cw)]
     names = dict(w1_0=0, w2_0=1, r0=2, m0=3, m1=3, r1=2, w1_1=0, w2_1=1)
     ins = dict(x=x, land=grow(land, (8, land_cols)), mine=mine, mine_bias=mine_bias, cot=cot)
@@ -1191,65 +1189,88 @@
     scratch.update({k: pltpu.VMEM((4, 4) + shapes[v], BF) for k, v in names.items()})
     if fast:
         scratch.update({f"shard{k}": pltpu.VMEM((2,) + shapes[k], BF) for k in range(4)})
-    fw = build("forward", lambda ns, hook: forward_kernel(fast, count, cols, ns), ins, outs, scratch, (), 1, 63)
+    fw = build("forward", lambda ns: forward_kernel(fast, count, cols, ns), ins, outs, scratch, {}, 1, 63)
     par, ocean, coarse, bias = fw.par, fw.ocean, fw.coarse, fw.bias
     w1_0, w2_0, w1_1, w2_1 = (v.reshape(r) for v, r in zip((fw.w1_0_out, fw.w2_0_out, fw.w1_1_out, fw.w2_1_out), ((cw, hw), (hw, cw)) * 2))
     r0, r1 = fw.r0_out.reshape(4 * cw, nw), fw.r1_out.reshape(GROUPS, 2, padded(n), 2 * cw)
-    mm = jnp.stack([fw.m0_out.reshape(cw, cw), fw.m1_out.reshape(cw, cw)])
-
-    class Kept:
-        def __init__(self, k):
-            self.z, self.st, self.n, self.g, self.gp, self.a = (getattr(fw, f"{v}{k}") for v in ("z", "st", "n", "g", "gp", "a"))
-
-    conv0, conv1 = Kept(0), Kept(1)
-    ff0, ff1 = conv0, conv1
-
-    view = lambda v, k: v.reshape((4, 4) + shapes[k])
-    back1 = backward("dec_back", 6, [Deliver("act", 1, fw.nat1, fw.act)], 1, fw.cot8, conv1, w1_1, w2_1, ff1)
-    jobs = [PlaneSum("ps", [view(back1.dw1, 0), view(back1.dw2, 1)])] if fast else []
-    bconv1 = backward_conv("dec_back_conv", 7, jobs, 1, back1, conv1.a)
-    jobs = [LineSum("ls", [(bconv1.psout0, 1), (bconv1.psout1, 1)])] if fast else []
-    bmid = build(
-        "back_mid", functools.partial(back_mid_kernel, count),
-        dict(dh=bconv1.dh, up=fw.up, skip=fw.skip, deep=fw.deep, pieces=fw.pieces, down=r0, up_w=r1, merge=mm, coarse=coarse,
-             patch=mats["patch"], unpatch=mats["unpatch"], back=mats["back"], gather=mats["gather"]),
-        dict(dmerge=((2, cw, cw), BF), dup_w=((GROUPS, 2, padded(n), 2 * cw), BF), ddown=((4 * cw, nw), BF), dy=field(F32), nat=natural),
-        dict(dskip=pltpu.VMEM((cells, cw), BF), dups=pltpu.VMEM((2, deep_cells, 2 * cw), BF), spreads=pltpu.VMEM((4, deep_cells, cw), F32)), jobs, 8,
-    )
-    jobs = []
+
+    def kept(k):
+        names = ("z", "st", "n", "g", "gp", "a")
+        ins = {v: at_any(getattr(fw, f"{v}{k}")) for v in names}
+        ins["z"] = at_any(ins["z"][0].reshape(cells, cw))
+        ins["st"] = getattr(fw, f"st{k}")
+        return ins
+
+    mats_of = lambda *names: {k: mats[k] for k in names}
+    common = dict(par=par, ocean=ocean, **mats_of("shifts", "edges", "back", "gather"))
+    outs_w = dict(gw1=((2,) + half_shape(shapes[0]), F32), gw2=((2,) + half_shape(shapes[1]), F32)) if fast else {}
+    wide_w = dict(dw1=((cw, hw), BF), dw2=((hw, cw), BF))
+    rows_of = lambda names: {k: pltpu.VMEM(*v) for k, v in names.items()}
+    small_space = dict(
+        dz=pltpu.VMEM(*field(BF)), packed=pltpu.VMEM(*edge_rows), halo=pltpu.VMEM(*edge_rows), small=pltpu.VMEM((8, cw), F32),
+        stats=pltpu.VMEM((8, cw), F32), slots=pltpu.VMEM((count // 2 + 1, 8, cw), F32), send=DMA((count,)), recv=DMA((count,)),
+        hsend=DMA((2,)), hrecv=DMA((2,)), load_sem=DMA((8,)), col_sem=DMA((2, 2)),
+    )
+    banks = {}
     if fast:
-        dm = bmid.dmerge.reshape((2, 4, 4) + shapes[3])
-        jobs = [PlaneSum("ps", [view(bmid.ddown, 2), view(bmid.dup_w, 2), (dm, 0), (dm, 1)])]
-    back0 = backward("enc_back", 9, jobs, 0, bmid.dy, conv0, w1_0, w2_0, ff0)
-    jobs = [Deliver("gi", 1, bmid.nat)]
+        banks = {**reduce_bank("w0", shapes[0]), **reduce_bank("w1", shapes[1])}
+    give_w = not fast
+    bounce = natural + (ANY,)
+    dec_outs = dict(
+        act=((4, 4, tiles, 16, c), BF, ANY), bounce=bounce, tiny=((64, cw), F32), dym=field(F32), nat=natural,
+        dm0=((cw, cw), BF), dm1=((cw, cw), BF), dr1=((GROUPS, 2, padded(n), 2 * cw), BF), dr0=((4 * cw, nw), BF), **outs_w,
+    )
+    if give_w:
+        dec_outs.update(wide_w)
+    dec = build(
+        "decoder_back", lambda ns: back_decoder_kernel(fast, count, cols, ns),
+        dict(
+            nat1=at_any(fw.nat1), act_in=at_any(fw.act), top=fw.cot8, w1=at_any(w1_1), w2=at_any(w2_1), **kept(1),
+            up=at_any(fw.up), skip=at_any(fw.skip), deep=at_any(fw.deep), pieces=at_any(fw.pieces), r0=at_any(r0), r1=at_any(r1),
+            m0=at_any(fw.m0_out.reshape(cw, cw)), m1=at_any(fw.m1_out.reshape(cw, cw)), coarse=coarse,
+            **common, **mats_of("spread", "turn", "patch", "unpatch"),
+        ),
+        dec_outs, dict(ds_=DMA((2, 2)), dr_=DMA((4,)), db=DMA((2,)), **small_space, **banks, **({} if give_w else rows_of(wide_w))), {"act_in": "act"}, 2, 63,
+    )
+    enc_ins = dict(
+        nat1=at_any(dec.nat), top=dec.dym, tiny1=dec.tiny, w1=at_any(w1_0), w2=at_any(w2_0), **kept(0), **common,
+    )
+    enc_outs = dict(gi=((4, 4, tiles, 16, c), BF, ANY), bounce0=bounce, bounce1=bounce, total=((64, cw), F32), **outs_w)
+    enc_banks = dict(banks)
     if fast:
-        jobs += [PlaneSum("ps", [view(back0.dw1, 0), view(back0.dw2, 1)]), LineSum("ls", [(getattr(back0, f"psout{k}"), k % 2) for k in range(4)])]
-    bconv0 = backward_conv("enc_back_conv", 10, jobs, 0, back0, conv0.a)
-
-    tiny = jnp.stack([jnp.concatenate([dk, small], axis=0) for dk, small in ((bconv0.dk, back0.small), (bconv1.dk, back1.small))])
-    jobs = [Deliver("gi", 0, bconv0.nat, bconv0.giout)]
+        view = lambda v, k: at_any(v.reshape((4, 4) + shapes[k]))
+        enc_ins.update(pr0=view(dec.dr0, 2), pr1=view(dec.dr1, 2), pm0=view(dec.dm0, 3), pm1=view(dec.dm1, 3))
+        for name, k in (("r0", 2), ("r1", 2), ("r2", 3), ("r3", 3)):
+            enc_banks.update(reduce_bank(name, shapes[k]))
+        for name, k in (("gr0", 2), ("gr1", 2), ("gm0", 3), ("gm1", 3)):
+            enc_outs[name] = ((2,) + half_shape(shapes[k]), F32)
+        enc_banks.update(sm=pltpu.VMEM((2, 64, cw), F32), tiny=pltpu.VMEM((9, 64, cw), F32), ts=DMA((9,)), tr=DMA((9,)))
+    if give_w:
+        enc_outs.update(wide_w)
+    enc = build(
+        "encoder_back", lambda ns: back_encoder_kernel(fast, count, cols, ns), enc_ins, enc_outs,
+        dict(
+            nat0=pltpu.VMEM(*natural), dym=pltpu.VMEM(*field(F32)), tiny0=pltpu.VMEM((64, cw), F32), ds0=DMA((2, 2)), dr0_=DMA((4,)), db0=DMA((2,)),
+            ds1=DMA((2, 2)), dr1_=DMA((4,)), db1=DMA((2,)), **small_space, **enc_banks, **({} if give_w else rows_of(wide_w)),
+        ),
+        {}, 3, 63,
+    )
+    last, tiny = enc, enc.total
     if fast:
-        jobs += [LineSum("ls", [(bconv0.psout0, 0), (bconv0.psout1, 0)])]
-        last = build(
-            "last", functools.partial(last_kernel, count), dict(small=tiny), dict(total=((64, cw), F32)),
-            dict(tiny=pltpu.VMEM((9, 64, cw), F32), ts=DMA((9,)), tr=DMA((9,))), jobs, 11,
-        )
-        tiny = last.total
         rows_of = lambda v: v.reshape(-1, v.shape[-1])
-        gw1 = unpack_in(rows_of(jnp.where(s == 0, last.lsout0, bmid.lsout0)), c, hid)
-        gw2 = unpack_in(jnp.where(s == 0, last.lsout1, bmid.lsout1).transpose(1, 0, 2).reshape(padded(hid), cw), hid, c)
-        gres = jnp.where(s == 0, unpack_down(rows_of(bconv0.lsout0), c, n), unpack_up(rows_of(bconv0.lsout1), c, n))
-        gmm = unpack_in(rows_of(jnp.where(s == 0, bconv0.lsout2, bconv0.lsout3)), c, c)
+        gw1 = unpack_in(rows_of(jnp.where(s == 0, enc.gw1, dec.gw1)), c, hid)
+        gw2 = unpack_in(jnp.where(s == 0, enc.gw2, dec.gw2).transpose(1, 0, 2).reshape(padded(hid), cw), hid, c)
+        gres = jnp.where(s == 0, unpack_down(rows_of(enc.gr0), c, n), unpack_up(rows_of(enc.gr1), c, n))
+        gmm = unpack_in(rows_of(jnp.where(s == 0, enc.gm0, enc.gm1)), c, c)
     else:
-        last = build("last", only, {}, {}, {}, jobs, 11)
         scatter = lambda v: lax.psum_scatter(v.astype(F32).reshape(-1), both, scatter_dimension=0, tiled=True)
-        gw1 = scatter(jnp.stack([unpack_in(v, c, hid) for v in (back0.dw1, back1.dw1)]))
-        gw2 = scatter(jnp.stack([unpack_in(v, hid, c) for v in (back0.dw2, back1.dw2)]))
-        gres = scatter(jnp.stack([unpack_down(bmid.ddown, c, n), unpack_up(bmid.dup_w, c, n)]))
-        gmm = scatter(jnp.stack([unpack_in(bmid.dmerge[k], c, c) for k in range(2)]))
-        tiny = lax.psum(tiny, both)[s]
-    activations = back1.actout.reshape(1, batches, height, cols, c)
-    grad_input = last.giout.astype(F32).reshape(1, batches, height, cols, c)
+        gw1 = scatter(jnp.stack([unpack_in(v, c, hid) for v in (enc.dw1, dec.dw1)]))
+        gw2 = scatter(jnp.stack([unpack_in(v, hid, c) for v in (enc.dw2, dec.dw2)]))
+        gres = scatter(jnp.stack([unpack_down(dec.dr0, c, n), unpack_up(dec.dr1, c, n)]))
+        gmm = scatter(jnp.stack([unpack_in(v, c, c) for v in (dec.dm0, dec.dm1)]))
+        tiny = lax.psum(jnp.stack([enc.total, dec.tiny]), both)[s]
+    activations = dec.act.reshape(1, batches, height, cols, c)
+    grad_input = last.gi.astype(F32).reshape(1, batches, height, cols, c)
     narrow = lambda v: v.reshape(-1, GROUPS, padded(c))[:, :, : c // GROUPS].reshape(-1, c)
     fine = narrow(tiny[:59])
     grad_bias_in = tiny[59:63].reshape(-1)[:hw].reshape(GROUPS, -1)[:, : hid // GROUPS].reshape(1, hid)

time: 517 us -> 433 us (0.84)
  the two profiles are of different devices: /device:TPU:8 before, /device:TPU:0 now
where the time goes in v3:
time: 433 us; the launch traced here: 426 us
  Pallas kernels  376 us (87%)
  local copies, waits for them, and re-layouts  30.2 us (7%)
  other arithmetic  19.1 us (4%)
    pallas_call x3, Pallas kernels, build(): pl.pallas_call(kernel, name=name, out_shape=[jax.ShapeDtypeStruct(v[0], v...  376 us

profile of v3, /device:TPU:0, one launch (start us, length us, event | category | flops | bytes accessed | tf_op | source)
XLA Modules:
  0.0 426.2 jit_solution(13078918912000554699)
XLA Ops:
  0.6 0.5 broadcast.57
  1.2 1.3 reduce.25
  2.5 1.3 reduce.24
  3.9 1.3 reduce.23
  5.2 1.3 pad.40.refs_1_
  6.5 0.7 reduce.3
  7.2 0.1 reshape.168
  7.3 0.1 reshape.169
  7.4 0.8 convert_element_type.35
  8.2 0.6 pad.44.refs_3_
  8.8 0.2 reshape.177
  9.1 0.8 squeeze_reshape.11.refs_8_
  9.9 1.3 convert_reduce_fusion.2
  11.2 0.4 reshape.171
  11.6 0.8 squeeze_reshape.9.refs_5_
  12.4 1.3 convert_reduce_fusion.1
  13.8 1.8 convert_reduce_fusion
  15.6 1.0 copy.48
  16.6 0.2 concatenate.19
  16.8 0.2 concatenate.18
  17.1 0.2 concatenate.17
  17.3 0.3 select_maximum_fusion
  17.5 0.1 copy.52
  17.7 0.7 pad.42.refs_2_
  18.3 0.9 reshape.172
  19.2 0.4 copy.63
  19.7 0.8 copy.56.refs_6_
  20.4 1.2 reshape.173
  21.6 0.1 pad.47
  21.7 0.3 reshape.174
  22.1 2.0 reshape.175
  24.1 0.3 pad_bitcast_fusion
  24.3 1.2 copy.54
  25.5 0.2 reshape.176
  25.8 0.1 copy.55
  25.9 0.7 broadcast_select_fusion.1.refs_7_
  26.7 165.1 %forward.1 = (f32[2,56,512]{2,1,0:T(8,128)}, f32[2,8,1792]{2,1,0:T(8,128)}, f32[1280,128]{1,0:T(8,128)}, f32[320,128]{1,0:T(8,128)}, f32[8,512]{1,0:T(8,128)}, /...) custom-call(bf16[4,4,10,16,400]{4,3,2,1,0:T(8,128)(2,1)} %bitcast.70, ...), custom_call_target="tpu_custom_call" | custom-call | tf_op jit(solution)/shard_map/forward/pallas_call | solution.py:1110
  191.7 90.0 %decoder_back.1 = (bf16[4,4,10,16,400]{4,3,2,1,0:T(8,128)(2,1)}, bf16[8,10,16,400]{3,2,1,0:T(8,128)(2,1)}, f32[64,512]{1,0:T(8,128)}, f32[1280,512]{1,0:T(8,128)...) custom-call(bf16[8,10,16,400]{3,2,1,0:T(8,128)(2,1)} %get-tuple-elem, ...), custom_call_target="tpu_custom_call", output_to_operand_aliasing={{0}: (1, {})} | custom-call | tf_op jit(solution)/shard_map/decoder_back/pallas_call | solution.py:1110
  281.7 120.6 %encoder_back.1 = (bf16[4,4,10,16,400]{4,3,2,1,0:T(8,128)(2,1)}, bf16[8,10,16,400]{3,2,1,0:T(8,128)(2,1)}, bf16[8,10,16,400]{3,2,1,0:T(8,128)(2,1)}, f32[64,512]...) custom-call(bf16[8,10,16,400]{3,2,1,0:T(8,128)(2,1)} %get-tuple-elem, ...), custom_call_target="tpu_custom_call" | custom-call | tf_op jit(solution)/shard_map/encoder_back/pallas_call | solution.py:1110
  402.4 1.0 select_bitcast_fusion
  403.5 1.0 broadcast_select_fusion.2
  404.4 0.7 slice_bitcast_fusion
  405.3 0.7 reshape.198
  405.9 0.2 reshape_reshape.15
  406.1 1.0 broadcast_in_dim_reshape.6
  407.2 0.1 copy.58
  407.3 0.1 reshape_reshape.19
  407.5 0.8 reshape.201
  408.3 0.1 copy.57
  408.4 0.5 slice_reduce_fusion
  409.0 0.7 slice.64
  409.6 0.7 slice.59
  410.3 0.7 slice.57
  411.0 0.8 copy.62
  411.7 0.4 copy.59
  412.2 1.4 broadcast_in_dim_reshape.7
  413.6 0.3 reshape_reshape.17
  413.9 1.0 reshape.199
  414.9 0.3 copy.60
  415.3 1.7 copy.61
  417.0 1.5 reshape.200
  418.5 1.1 broadcast_select_fusion
  419.5 5.0 %convert.1 = f32[1,4,4,160,400]{4,3,2,1,0:T(8,128)} convert(bf16[1,4,4,160,400]{4,3,2,1,0:T(8,128)(2,1)} %bitcast.72) | non-fusion elementwise | flops 1024000 | bytes 6144000 | tf_op jit(solution)/shard_map/reshape | solution.py:1273
  424.5 1.5 copy.67
  (28 shorter events, 0.4 us)
Async XLA Ops:
  281.7 120.7 %copy-start.4 = (f32[2,112,256]{2,1,0:T(8,128)S(1)}, f32[2,112,256]{2,1,0:T(8,128)}, u32[]{:S(2)}) copy-start(f32[2,112,256]{2,1,0:T(8,128)} %get-tuple-element.102) | copy-start | bytes 688132
  281.7 121.7 %copy-start.3 = (f32[2,16,1792]{2,1,0:T(8,128)S(1)}, f32[2,16,1792]{2,1,0:T(8,128)}, u32[]{:S(2)}) copy-start(f32[2,16,1792]{2,1,0:T(8,128)} %get-tuple-element.100) | copy-start | bytes 688132
  402.4 4.9 %copy-start.6 = (f32[2,16,512]{2,1,0:T(8,128)S(1)}, f32[2,16,512]{2,1,0:T(8,128)}, u32[]{:S(2)}) copy-start(f32[2,16,512]{2,1,0:T(8,128)} %get-tuple-element.105) | copy-start | bytes 196612
  402.4 4.9 %copy-start.7 = (f32[2,16,512]{2,1,0:T(8,128)S(1)}, f32[2,16,512]{2,1,0:T(8,128)}, u32[]{:S(2)}) copy-start(f32[2,16,512]{2,1,0:T(8,128)} %get-tuple-element.106) | copy-start | bytes 196612
  402.4 5.9 %copy-start.5 = (f32[64,512]{1,0:T(8,128)S(1)}, f32[64,512]{1,0:T(8,128)}, u32[]{:S(2)}) copy-start(f32[64,512]{1,0:T(8,128)} %get-tuple-element.98) | copy-start | bytes 393220
  407.3 6.3 %copy-start.2 = (f32[2,64,1024]{2,1,0:T(8,128)S(1)}, f32[2,64,1024]{2,1,0:T(8,128)}, u32[]{:S(2)}) copy-start(f32[2,64,1024]{2,1,0:T(8,128)} %get-tuple-element.103) | copy-start | bytes 1572868
  412.2 2.7 copy-start.1
  419.5 5.0 %copy-start = (bf16[4,4,10,16,400]{4,3,2,1,0:T(8,128)(2,1)S(1)}, bf16[4,4,10,16,400]{4,3,2,1,0:T(8,128)(2,1)}, u32[]{:S(2)}) copy-start(bf16[4,4,10,16,400]{4,3,2,1,0:T(8,128)(2,1)} %get-tuple-element.81) | copy-start | bytes 6144004

commit v4 on v3

--- a/solution.py
+++ b/solution.py
@@ -201,9 +201,10 @@
     return value.reshape(-1, 8, value.shape[-1]).sum(0)
 
 
-def to_natural(cells, back, gather):
-    turned = dot(dot(back, cells).astype(BF), gather).astype(BF)
-    return turned.reshape(8, 16, turned.shape[-1])
+def to_natural(cells, back, gather, out):
+    narrow = dot(cells, gather).astype(BF)
+    for c in range(out.shape[1]):
+        out[:, c] = dot(back, narrow[128 * c : 128 * c + 128]).astype(BF).reshape(8, 16, narrow.shape[1])
 
 
 def shifted(chunk, perm, S, c):
@@ -219,8 +220,23 @@
 
 
 def taps_to(kb, par, flip):
-    for k in range(49):
-        kb[k] = jnp.broadcast_to(par[(48 - k if flip else k) : (48 - k if flip else k) + 1], kb.shape[1:])
+    for lane in range(kb.shape[0]):
+        at = slice(128 * lane, 128 * lane + 128)
+        for k in range(49):
+            tap = 48 - k if flip else k
+            kb[lane, k] = jnp.broadcast_to(par[tap : tap + 1, at], (8, 128))
+
+
+def taps_at(S, kb, lane, tile, first, sums):
+    for i in range(7):
+        window = [S[i, lane, first + t] for t in range(len(sums) + 6)]
+        taps = [kb[tile, 7 * i + j] for j in range(7)]
+        for k in range(len(sums)):
+            total = window[k] * taps[0]
+            for j in range(1, 7):
+                total = total + window[k + j] * taps[j]
+            sums[k] = sums[k] + total
+    return sums
 
 
 def norm_terms(st, par):
@@ -353,7 +369,7 @@
     return hook
 
 
-def nothing():
+def nothing(*_):
     pass
 
 
@@ -453,111 +469,108 @@
         ocean[pl.ds(pl.multiple_of(c * 128, 128), 128)] = dot(jnp.where(at == 16 * c, spread, 0.0).astype(BF), ones)
         return carry
 
-    lax.fori_loop(0, ocean.shape[0] // 128, chunk, 0)
+    lax.fori_loop(0, ocean.shape[0] // 128, chunk, 0, unroll=True)
     for b in range(ocean.shape[0] // 256):
         moved = dot(patch, ocean[256 * b : 256 * b + 256].astype(BF))
         coarse[64 * b : 64 * b + 64] = moved[:64] * moved[64:128] * moved[128:192] * moved[192:]
 
 
 def conv_phase(sec, cols, ns, hook):
-    S, kb, ocean, z, stats = ns.S, ns.kb, ns.ocean, ns.z, ns.stats
-    taps_to(kb, ns.par[sec], False)
-    lanes = S.shape[1]
-    wide = kb.shape[2]
+    ocean, z, stats = ns.ocean, ns.z, ns.stats
+    wide, tiles = z.shape[2], cols // 16
 
     def count_cells(b, t):
         return t + ocean[pl.ds(pl.multiple_of(b * 64, 64), 64)].reshape(8, 8, 128).sum(0)
 
-    tally = lax.fori_loop(0, cols // 8, count_cells, jnp.zeros((8, 128), F32))
-    for group in range(wide // 128 // lanes):
-        part = slice(group * lanes * 128, (group + 1) * lanes * 128)
-
-        def chunk(c, carry):
-            cells = pl.ds(pl.multiple_of(c * 128, 128), 128)
-            if sec == 0:
-                block = ns.x14[:, c]
-                block = dot(block.reshape(-1, block.shape[-1]), ns.spread[:, part]).astype(BF)
-                moved = shifted(block, ns.natural[...], S, c)
-                ns.a0[cells, part] = moved[384:512].astype(BF)
-            else:
-                shifted(jnp.concatenate([ns.a1[cells, part], ns.halo[0, c, :, part], ns.halo[1, c, :, part]], axis=0), ns.shifts[...], S, c)
-            return carry
-
-        lax.fori_loop(0, cols // 16, chunk, 0)
-        wrap(S, cols)
-        hook()
-        for lane in range(lanes):
-            at = slice((group * lanes + lane) * 128, (group * lanes + lane + 1) * 128)
-
-            def step(b, carry):
-                first, second = carry
-                acc = jnp.zeros((8, 8, 128), F32)
-                for i in range(7):
-                    window = S[i, lane, pl.ds(b * 8, 14)]
-                    for j in range(7):
-                        acc = acc + window[j : j + 8] * kb[7 * i + j, :, at][None]
-                z[pl.ds(b * 8, 8), :, at] = acc
-                kept = acc * ocean[pl.ds(pl.multiple_of(b * 64, 64), 64)].reshape(8, 8, 128)
-                return first + kept.sum(0), second + (kept * acc).sum(0)
-
-            zero = jnp.zeros((8, 128), F32)
-            first, second = lax.fori_loop(0, cols // 8, step, (zero, zero))
-            stats[0:1, at] = first.sum(0, keepdims=True)
-            stats[1:2, at] = second.sum(0, keepdims=True)
-            stats[2:3, at] = tally.sum(0, keepdims=True)
-            stats[3:8, at] = jnp.zeros((5, 128), F32)
+    def phase(S, kb, *laid):
+        taps_to(kb, ns.par[sec], False)
+        tally = lax.fori_loop(0, cols // 8, count_cells, jnp.zeros((8, 128), F32))
+        lanes = S.shape[1]
+        if sec == 0:
+            (laid,) = laid
+
+            def lay(r, carry):
+                row = ns.x14[r]
+                laid[r] = dot(row.reshape(cols, row.shape[2]), ns.spread[...]).astype(BF).reshape(tiles, 16, wide)
+                return carry
+
+            lax.fori_loop(0, 14, lay, 0, unroll=True)
+        for group in range(wide // 128 // lanes):
+            part = slice(group * lanes * 128, (group + 1) * lanes * 128)
+
+            def chunk(c, carry):
+                cells = pl.ds(pl.multiple_of(c * 128, 128), 128)
+                if sec == 0:
+                    moved = shifted(laid[:, c, :, part].reshape(224, lanes * 128), ns.natural[...], S, c)
+                    ns.a0[cells, part] = moved[384:512].astype(BF)
+                else:
+                    shifted(jnp.concatenate([ns.a1[cells, part], ns.halo[0, c, :, part], ns.halo[1, c, :, part]], axis=0), ns.shifts[...], S, c)
+                return carry
+
+            lax.fori_loop(0, tiles, chunk, 0)
+            wrap(S, cols)
             hook()
-
-
-def ff_phase(sec, ns, st, w1, w2, res, y, nat, kept, hook):
+            for lane in range(lanes):
+                at = slice((group * lanes + lane) * 128, (group * lanes + lane + 1) * 128)
+
+                def step(b, carry):
+                    first, second = carry
+                    sums = taps_at(S, kb, lane, group * lanes + lane, b * 16, [jnp.zeros((8, 128), F32)] * 16)
+                    for k, total in enumerate(sums):
+                        z[b * 16 + k, :, at] = total
+                        kept = total * ocean[pl.ds(pl.multiple_of(b * 128 + 8 * k, 8), 8)]
+                        first = first + kept
+                        second = second + kept * total
+                    return first, second
+
+                zero = jnp.zeros((8, 128), F32)
+                first, second = lax.fori_loop(0, tiles, step, (zero, zero))
+                stats[0:1, at] = first.sum(0, keepdims=True)
+                stats[1:2, at] = second.sum(0, keepdims=True)
+                stats[2:3, at] = tally.sum(0, keepdims=True)
+                stats[3:8, at] = jnp.zeros((5, 128), F32)
+                hook()
+
+    space = [pltpu.VMEM((7, 2, cols + 6, 8, 128), F32), pltpu.VMEM((wide // 128, 49, 8, 128), F32)]
+    pl.run_scoped(phase, *space, *([pltpu.VMEM((14, tiles, 16, wide), BF)] if sec == 0 else []))
+
+
+def gelu_terms(e):
+    phi = 0.5 + 0.5 * lax.erf(e * np.float32(0.5**0.5))
+    return phi, phi + e * (np.float32((2 * np.pi) ** -0.5) * jnp.exp(-0.5 * e * e))
+
+
+def ff_phase(sec, ns, st, w1, w2, res, y, nat, hook):
     par = ns.par[sec]
     counted, mean, inverse, gain, shift = norm_terms(st, par)
-    wide = ns.z.shape[2]
-    steps = ns.z.shape[0] // 32
-    stage, sems = (ns.n_st, ns.g_st, ns.gp_st), ns.ff_sem
+    cells, wide = res.shape
     w1, w2 = w1.reshape(wide, -1), w2.reshape(-1, wide)
     hidden = w1.shape[1]
 
-    def outs(b, slot):
-        at = pl.ds(pl.multiple_of(b * 256, 256), 256)
-        return [pltpu.make_async_copy(src.at[slot], dst.at[at], sems.at[k, slot]) for k, (src, dst) in enumerate(zip(stage, kept))]
-
-    def block(b, carry):
-        slot = b % 2
-
-        @pl.when(b >= 2)
-        def _():
-            for copy in outs(b - 2, slot):
-                copy.wait()
-
-        z = ns.z[pl.ds(b * 32, 32)].reshape(256, wide)
-        at = pl.ds(pl.multiple_of(b * 256, 256), 256)
-        normed = ((z - mean) * inverse * gain + shift).astype(BF)
-        ns.n_st[slot] = normed
-        acc = jnp.zeros((256, wide), F32)
-        for h in range(0, hidden, 256):
-            cut = slice(h, h + 256)
-            e = dot(normed, w1[:, cut]) + ns.bias[sec, 0:1, cut]
-            phi = 0.5 + 0.5 * lax.erf(e * np.float32(0.5**0.5))
-            act = (e * phi).astype(BF)
-            ns.g_st[slot, :, cut] = act
-            ns.gp_st[slot, :, cut] = (phi + e * (np.float32((2 * np.pi) ** -0.5) * jnp.exp(-0.5 * e * e))).astype(BF)
-            acc = acc + dot(act, w2[cut])
-        out = (lanes4(ns.ocean[at], wide) * (res[at].astype(F32) + (acc + par[51:52]))).astype(BF)
-        if y is not None:
-            y[at] = out
-        for k in range(2):
-            nat[:, 2 * b + k] = to_natural(out[128 * k : 128 * k + 128], ns.back[...], ns.gather[...])
-        for copy in outs(b, slot):
-            copy.start()
-        for k in range(steps):
-            pl.when(b == k)(functools.partial(hook, k))
-        return carry
-
-    lax.fori_loop(0, steps, block, 0)
-    for b in (steps - 2, steps - 1):
-        for copy in outs(b, b % 2):
-            copy.wait()
+    def phase(n, g, r):
+        def norm(b, carry):
+            z = ns.z[pl.ds(b * 32, 32)].reshape(256, wide)
+            n[pl.ds(pl.multiple_of(b * 256, 256), 256)] = ((z - mean) * inverse * gain + shift).astype(BF)
+            return carry
+
+        lax.fori_loop(0, cells // 256, norm, 0, unroll=True)
+        for h in range(hidden // 256):
+            at = slice(256 * h, 256 * h + 256)
+            e = dot(n[...], w1[:, at]) + ns.bias[sec, 0:1, at]
+            g[:, at] = (e * gelu_terms(e)[0]).astype(BF)
+            hook(h)
+        r[...] = dot(g[...], w2[...])
+        hook(hidden // 256)
+
+        def end(b, carry):
+            at = pl.ds(pl.multiple_of(b * 256, 256), 256)
+            y[at] = (lanes4(ns.ocean[at], wide) * (res[at].astype(F32) + (r[at] + par[51:52]))).astype(BF)
+            return carry
+
+        lax.fori_loop(0, cells // 256, end, 0, unroll=True)
+        to_natural(y[...], ns.back[...], ns.gather[...], nat)
+
+    pl.run_scoped(phase, pltpu.VMEM((cells, wide), BF), pltpu.VMEM((cells, hidden), BF), pltpu.VMEM((cells, wide), F32))
 
 
 def forward_kernel(fast, count, cols, ns):
@@ -582,6 +595,13 @@
             mats[name] = Gather(getattr(ns, f"shard{index}").at[sec], full, ns.gs.at[k], ns.gr.at[k])
         else:
             mats[name] = Load(getattr(ns, name + "_in"), full, ns.gs.at[k])
+    kept = dict(z0=ns.z, z1=ns.z, a0=ns.a0, a1=ns.a1, skip=ns.skip, up=ns.up, pieces=ns.pieces, deep=ns.deep, nat0=ns.nat0, nat1=ns.nat1)
+    keeps = {name: lambda k=k, name=name, ref=ref: pltpu.make_async_copy(ref, getattr(ns, name + "_out"), ns.keep.at[k]) for k, (name, ref) in enumerate(kept.items())}
+
+    def keep(*names):
+        for name in names:
+            keeps[name]().start()
+
     saves = {name: lambda k=k, name=name, full=full: pltpu.make_async_copy(full, getattr(ns, name + "_out"), ns.save.at[k]) for k, (name, full) in enumerate(fulls.items())}
 
     def do(step, *names):
@@ -593,11 +613,13 @@
         for name in names:
             saves[name]().start()
 
-    if fast:
-        for k in range(2, 6):
-            near[k].wait()
-            arrived(pairs[k][1].at[1 - s], ns.pr.at[k])
-    do("start", "w1_0", "w2_0")
+    for k in range(2, len(pairs)):
+        near[k].wait()
+        arrived(pairs[k][1].at[1 - s], ns.pr.at[k])
+        if k == 3:
+            do("start", "w1_0", "w2_0")
+    if not fast:
+        do("start", "w1_0", "w2_0")
     do("start", "r0")
     land_end()
     masks(ns.land2, ns.ocean, ns.coarse, ns.pick[...], ns.patch[...])
@@ -626,24 +648,24 @@
     pl.when(p < count - 1)(lambda: arrived(x14.at[pl.ds(11, 3)], ns.hr.at[1]))
 
     cot_begin, cot_end = collect(ns.cot, ns.cot8, 0, ns.cs, ns.cr)
-    act = deliver(0, ns.nat0, ns.act, ns.bounce, ns.ds_, ns.dr_, ns.db)
+
+    do("onward", "w1_0", "w2_0")
 
     conv_phase(0, cols, ns, script(
-        lambda: (do("onward", "w1_0", "w2_0"), do("start", "m0", "m1", "r1")),
-        lambda: do("plane", "r0"),
+        nothing,
+        lambda: (do("plane", "r0"), do("start", "r1", "m0", "m1")),
+        nothing,
+        nothing,
         lambda: do("over", "w1_0", "w2_0"),
         lambda: do("onward", "r0"),
-        lambda: do("start", "w1_1", "w2_1"),
-        lambda: do("plane", "m0", "m1", "r1"),
     ))
     ns.st0[...] = all_sum(ns.stats, ns.slots, ns.send, ns.recv, count)
-    keep_z = pltpu.make_async_copy(ns.z, ns.z0, ns.keep.at[0])
-    keep_z.start()
+    keep("z0", "a0")
     whole("w1_0", "w2_0")
-    ff0 = {0: lambda: do("over", "r0"), 1: lambda: do("onward", "m0", "m1", "r1"), 4: lambda: do("plane", "w1_1", "w2_1")}
-    ff_phase(0, ns, ns.st0, ns.w1_0, ns.w2_0, ns.a0, ns.skip, ns.nat0, (ns.n0, ns.g0, ns.gp0), lambda k: ff0.get(k, lambda: None)())
-
-    whole("r0")
+    ff0 = {1: lambda: (do("plane", "r1", "m0", "m1"), do("start", "w1_1", "w2_1")), 7: lambda: do("over", "r0")}
+    ff_phase(0, ns, ns.st0, ns.w1_0, ns.w2_0, ns.a0, ns.skip, ns.nat0, lambda k: ff0.get(k, nothing)())
+    keep("skip", "nat0")
+
     skip, pieces, wide = ns.skip, ns.pieces, ns.skip.shape[1]
     blocks = skip.shape[0] // 256
     down, up_w = ns.r0.reshape(4 * wide, -1), ns.r1.reshape(GROUPS, 2, ns.r1.shape[2] // 2, -1)
@@ -652,12 +674,16 @@
         moved = dot(ns.patch[...], skip[256 * b : 256 * b + 256]).astype(BF)
         for k in range(4):
             pieces[k, 64 * b : 64 * b + 64] = moved[64 * k : 64 * k + 64]
+    do("onward", "r1", "m0", "m1")
+    do("plane", "w1_1", "w2_1")
+    whole("r0")
     value = sum(dot(pieces[k], down[wide * k : wide * k + wide]) for k in range(4))
     deep_value = (lanes4(ns.coarse[...], value.shape[1]) * value).astype(BF)
     ns.deep[...] = deep_value
+    keep("pieces", "deep")
     do("over", "m0", "m1", "r1")
     do("onward", "w1_1", "w2_1")
-    act[0]()
+    cot_begin()
     whole("m0", "m1", "r1")
     rows = up_w.shape[0] * up_w.shape[2]
     lifted = [dot(deep_value, up_w[:, i].reshape(rows, -1)).astype(BF) for i in range(2)]
@@ -667,6 +693,8 @@
             [lifted[i][64 * b : 64 * b + 64, wide * j : wide * j + wide] for i in range(2) for j in range(2)], axis=0
         )
         ns.up[at] = dot(ns.unpatch[...], stacked).astype(BF)
+    for b in range(blocks):
+        at = slice(256 * b, 256 * b + 256)
         joined = dot(ns.up[at], merge[0][...]) + dot(skip[at], merge[1][...])
         ns.h[at] = joined
         low = joined.astype(BF)
@@ -676,25 +704,23 @@
             ns.packed[0, 2 * b + k] = ends[:48]
             ns.packed[1, 2 * b + k] = ends[48:]
     swap_rows(ns.packed, ns.halo, ns.es, ns.er, count)
-    keep_z.wait()
-    cot_begin()
-
-    conv_phase(1, cols, ns, script(
-        act[1],
-        lambda: do("over", "w1_1", "w2_1"),
-        lambda: whole("w1_1", "w2_1"),
-    ))
+    keep("up", "a1")
+    keeps["z0"]().wait()
+
+    conv_phase(1, cols, ns, script(nothing, nothing, lambda: do("over", "w1_1", "w2_1")))
     ns.st1[...] = all_sum(ns.stats, ns.slots1, ns.send1, ns.recv1, count)
-    keep_z1 = pltpu.make_async_copy(ns.z, ns.z1, ns.keep.at[0])
-    keep_z1.start()
-    ff_phase(1, ns, ns.st1, ns.w1_1, ns.w2_1, ns.h, None, ns.nat1, (ns.n1, ns.g1, ns.gp1), lambda k: None)
+    keep("z1")
+    whole("w1_1", "w2_1")
+    ff_phase(1, ns, ns.st1, ns.w1_1, ns.w2_1, ns.h, ns.y1, ns.nat1, nothing)
+    keep("nat1")
 
     cot_end()
-    act[3]()
     for name, save in saves.items():
         save().wait()
         do("finish", name)
-    keep_z1.wait()
+    for name, copy in keeps.items():
+        if name != "z0":
+            copy().wait()
     for c in far:
         c.wait_send()
     pl.when(p > 0)(edge(True).wait_send)
@@ -814,21 +840,15 @@
 
 
 def back_ff_phase(sec, count, ns, top, kept, w_in, w_out, hook, done):
-    z_in, st, n_in, g_in, gp_in = kept
+    z_in, st = kept
     cells, wide = ns.dym.shape
     hidden = w_in.shape[1]
     chunks = cells // 128
-    ocean, small, dr_rows, dym = ns.ocean, ns.small, None, ns.dym
+    ocean, small, dym = ns.ocean, ns.small, ns.dym
     counted, mean, inverse, gain, shift = norm_terms(st, ns.par[sec])
 
-    def phase(w1, w2, z, n, g, gp, dn, dr):
-        def columns(h):
-            at, slot = pl.ds(256 * h, 256), h % 2
-            return [pltpu.make_async_copy(src.at[:, at], dst.at[slot], ns.col_sem.at[k, slot]) for k, (src, dst) in enumerate(((g_in, g), (gp_in, gp)))]
-
-        got_w2, got_w1, got_n, got_z = loads([(w_out, w2), (w_in, w1), (n_in, n), (z_in, z)], ns.load_sem)
-        for copy in columns(0):
-            copy.start()
+    def phase(w1, w2, z, n, de, dn, dr):
+        got_z, got_w1, got_w2 = loads([(z_in, z), (w_in, w1), (w_out, w2)], ns.load_sem)
 
         def begin(c, total):
             at = pl.ds(pl.multiple_of(c * 128, 128), 128)
@@ -844,34 +864,32 @@
             dr[at] = low
             return total + rows8(low.astype(F32))
 
-        total = lax.fori_loop(0, chunks, begin, jnp.zeros((8, wide), F32))
+        total = lax.fori_loop(0, chunks, begin, jnp.zeros((8, wide), F32), unroll=True)
         small[2:3] = total.sum(0, keepdims=True)
         small[3:8] = jnp.zeros((5, wide), F32)
+        got_z()
+
+        def norm(c, carry):
+            at = pl.ds(pl.multiple_of(c * 128, 128), 128)
+            n[at] = ((z[at] - mean) * inverse * gain + shift).astype(BF)
+            return carry
+
+        lax.fori_loop(0, chunks, norm, 0, unroll=True)
+        got_w1()
         got_w2()
         for h in range(hidden // 256):
-            at, slot = slice(256 * h, 256 * h + 256), h % 2
-            if h + 1 < hidden // 256:
-                for copy in columns(h + 1):
-                    copy.start()
-            dg = dot_nt(dr[...], w2[at])
-            if h == 0:
-                got_n()
-                got_w1()
-            for copy in columns(h):
-                copy.wait()
-            de = (dg * gp[slot].astype(F32)).astype(BF)
+            at = slice(256 * h, 256 * h + 256)
+            e = dot(n[...], w1[:, at]) + ns.bias[sec, 0:1, at]
+            phi, slope = gelu_terms(e)
+            ns.dw2[at] = dot_tn((e * phi).astype(BF), dr[...]).astype(BF)
+            low = (dot_nt(dr[...], w2[at]) * slope).astype(BF)
+            de[:, at] = low
             row, col = 3 + 256 * h // wide, 256 * h % wide
-            small[row : row + 1, col : col + 256] = de.astype(F32).sum(0, keepdims=True)
-            ns.dw1[:, at] = dot_tn(n[...], de).astype(BF)
-            ns.dw2[at] = dot_tn(g[slot], dr[...]).astype(BF)
-            part = dot_nt(de, w1[:, at])
-            if h == 0:
-                dn[...] = part
-            else:
-                dn[...] += part
+            small[row : row + 1, col : col + 256] = low.astype(F32).sum(0, keepdims=True)
+            ns.dw1[:, at] = dot_tn(n[...], low).astype(BF)
             hook(h)
         done()
-        got_z()
+        dn[...] = dot_nt(de[...], w1[...])
 
         def sums(c, carry):
             at = pl.ds(pl.multiple_of(c * 128, 128), 128)
@@ -879,7 +897,7 @@
             return carry[0] + rows8(grad), carry[1] + rows8(grad * ((z[at] - mean) * inverse))
 
         zero = jnp.zeros((8, wide), F32)
-        plain, scaled = lax.fori_loop(0, chunks, sums, (zero, zero))
+        plain, scaled = lax.fori_loop(0, chunks, sums, (zero, zero), unroll=True)
         small[0:1] = plain.sum(0, keepdims=True)
         small[1:2] = scaled.sum(0, keepdims=True)
         ns.stats[...] = small[...]
@@ -897,12 +915,11 @@
             ns.packed[1, c] = ends[48:]
             return carry
 
-        lax.fori_loop(0, chunks, end, 0)
+        lax.fori_loop(0, chunks, end, 0, unroll=True)
 
     field = lambda t: pltpu.VMEM((cells, wide), t)
     pl.run_scoped(
-        phase, pltpu.VMEM(w_in.shape, BF), pltpu.VMEM(w_out.shape, BF), field(F32), field(BF),
-        pltpu.VMEM((2, cells, 256), BF), pltpu.VMEM((2, cells, 256), BF), field(F32), field(BF),
+        phase, pltpu.VMEM(w_in.shape, BF), pltpu.VMEM(w_out.shape, BF), field(F32), field(BF), pltpu.VMEM((cells, hidden), BF), field(F32), field(BF),
     )
     swap_rows(ns.packed, ns.halo, ns.hsend, ns.hrecv, count)
 
@@ -911,10 +928,9 @@
     cells, wide = ns.dz.shape
     dz = ns.dz
 
-    def phase(S, kb, acc_dk, a):
+    def phase(S, kb, a, field, acc_dk):
         (got_a,) = loads([(a_in, a)], ns.load_sem)
         taps_to(kb, ns.par[sec], True)
-        acc_dk[...] = jnp.zeros(acc_dk.shape, F32)
         lanes = S.shape[1]
         for group in range(wide // 128 // lanes):
             part = slice(group * lanes * 128, (group + 1) * lanes * 128)
@@ -932,26 +948,38 @@
             for lane in range(lanes):
                 at = slice((group * lanes + lane) * 128, (group * lanes + lane + 1) * 128)
 
+                field[...] = a[:, at].astype(F32).reshape(field.shape)
+
                 def step(b, carry):
-                    rows = pl.ds(pl.multiple_of(b * 64, 64), 64)
-                    acc = ns.dym[rows, at].reshape(8, 8, 128)
-                    field = a[rows, at].astype(F32).reshape(8, 8, 128)
+                    rows = pl.ds(pl.multiple_of(b * 128, 128), 128)
+                    above = ns.dym[rows, at].reshape(16, 8, 128)
+                    sums = taps_at(S, kb, lane, group * lanes + lane, b * 16, [above[k] for k in range(16)])
+                    dz[rows, at] = jnp.concatenate(sums, axis=0).astype(BF)
+                    return carry
+
+                lax.fori_loop(0, cols // 16, step, 0)
+                acc_dk[...] = jnp.zeros(acc_dk.shape, F32)
+
+                def tap_sums(b, carry):
+                    here = [field[b * 16 + k] for k in range(16)]
                     for i in range(7):
-                        window = S[i, lane, pl.ds(b * 8, 14)]
+                        window = [S[i, lane, b * 16 + t] for t in range(22)]
                         for j in range(7):
-                            acc = acc + window[j : j + 8] * kb[7 * i + j, :, at][None]
-                            acc_dk[7 * i + j, :, at] += (window[j : j + 8] * field).sum(0)
-                    dz[rows, at] = acc.reshape(64, 128).astype(BF)
+                            total = window[j] * here[0]
+                            for k in range(1, 16):
+                                total = total + window[j + k] * here[k]
+                            acc_dk[7 * i + j] += total
                     return carry
 
-                lax.fori_loop(0, cols // 8, step, 0)
+                lax.fori_loop(0, cols // 16, tap_sums, 0)
+                for k in range(49):
+                    tiny[48 - k : 49 - k, at] = acc_dk[k].sum(0, keepdims=True)
                 hook()
-        for k in range(49):
-            tiny[48 - k : 49 - k] = acc_dk[k].sum(0, keepdims=True)
         tiny[49:56] = jnp.zeros((7, wide), F32)
 
     pl.run_scoped(
-        phase, pltpu.VMEM((7, 2, cols + 6, 8, 128), F32), pltpu.VMEM((49, 8, wide), F32), pltpu.VMEM((49, 8, wide), F32), pltpu.VMEM((cells, wide), BF)
+        phase, pltpu.VMEM((7, 2, cols + 6, 8, 128), F32), pltpu.VMEM((wide // 128, 49, 8, 128), F32), pltpu.VMEM((cells, wide), BF),
+        pltpu.VMEM((cols, 8, 128), F32), pltpu.VMEM((49, 8, 128), F32),
     )
 
 
@@ -960,40 +988,46 @@
     cells, wide = dh.shape
     blocks = cells // 256
 
-    def phase(skip, up, merge0, merge1, up_w, deep, down, pieces, dups, spreads):
+    def phase(skip, up, merge0, merge1, up_w, deep, down, pieces, dups, spreads, dskip):
         got = loads(
-            [(ns.up, up), (ns.skip, skip), (ns.m1, merge1), (ns.m0, merge0), (ns.r1, up_w), (ns.deep, deep), (ns.pieces, pieces), (ns.r0, down)],
+            [(ns.m1, merge1), (ns.m0, merge0), (ns.up, up), (ns.skip, skip), (ns.r1, up_w), (ns.deep, deep), (ns.pieces, pieces), (ns.r0, down)],
             ns.load_sem,
         )
-        for k in range(4):
+        for k in range(2):
             got[k]()
-        ns.dm0[...] = dot_tn(up[...], dh[...]).astype(BF)
-        ns.dm1[...] = dot_tn(skip[...], dh[...]).astype(BF)
-        hook(0)
         for b in range(blocks):
             at = slice(256 * b, 256 * b + 256)
             low = dot_nt(dh[at], merge1[...]).astype(BF)
             ns.dym[at] = low.astype(F32)
-            for k in range(2):
-                ns.nat[:, 2 * b + k] = to_natural(low[128 * k : 128 * k + 128], ns.back[...], ns.gather[...])
+            dskip[at] = low
             lifted = dot_nt(dh[at], merge0[...]).astype(BF)
             moved = dot(ns.patch[...], lifted).astype(BF)
             for k in range(4):
                 dups[k // 2, 64 * b : 64 * b + 64, wide * (k % 2) : wide * (k % 2) + wide] = moved[64 * k : 64 * k + 64]
+        to_natural(dskip[...], ns.back[...], ns.gather[...], ns.nat)
+        hook(0)
+        got[2]()
+        got[3]()
+        ns.dm0[...] = dot_tn(up[...], dh[...]).astype(BF)
+        ns.dm1[...] = dot_tn(skip[...], dh[...]).astype(BF)
         hook(1)
         rows = up_w.shape[0] * up_w.shape[2]
         got[4]()
         ddeep = dot_nt(dups[0], up_w[:, 0].reshape(rows, -1)) + dot_nt(dups[1], up_w[:, 1].reshape(rows, -1))
         got[5]()
         for i in range(2):
-            ns.dr1[:, i] = dot_tn(deep[...], dups[i]).astype(BF).reshape(up_w.shape[0], up_w.shape[2], -1)
+            up_w[:, i] = dot_tn(deep[...], dups[i]).astype(BF).reshape(up_w.shape[0], up_w.shape[2], -1)
+        saves = [pltpu.make_async_copy(up_w, ns.dr1, ns.load_sem.at[0]), pltpu.make_async_copy(down, ns.dr0, ns.load_sem.at[1])]
+        saves[0].start()
         masked = (lanes4(ns.coarse[...], ddeep.shape[1]) * ddeep).astype(BF)
         hook(2)
         got[6]()
         got[7]()
         for k in range(4):
-            ns.dr0[wide * k : wide * k + wide] = dot_tn(pieces[k], masked).astype(BF)
             spreads[k] = dot_nt(masked, down[wide * k : wide * k + wide])
+            down[wide * k : wide * k + wide] = dot_tn(pieces[k], masked).astype(BF)
+        saves[1].start()
+        saves[0].wait()
         hook(3)
         for b in range(blocks):
             value = jnp.concatenate([spreads[k, 64 * b : 64 * b + 64] for k in range(4)], axis=0)
@@ -1001,64 +1035,77 @@
             rest = (value - high.astype(F32)).astype(BF)
             at = slice(256 * b, 256 * b + 256)
             ns.dym[at] += dot(ns.unpatch[...], high) + dot(ns.unpatch[...], rest)
+        saves[1].wait()
 
     like = lambda ref: pltpu.VMEM(ref.shape, BF)
     deep_cells = ns.deep.shape[0]
     pl.run_scoped(
         phase, like(ns.skip), like(ns.up), like(ns.m0), like(ns.m1), like(ns.r1), like(ns.deep), like(ns.r0), like(ns.pieces),
-        pltpu.VMEM((2, deep_cells, 2 * wide), BF), pltpu.VMEM((4, deep_cells, wide), F32),
+        pltpu.VMEM((2, deep_cells, 2 * wide), BF), pltpu.VMEM((4, deep_cells, wide), F32), pltpu.VMEM((cells, wide), BF),
     )
 
 
-def back_decoder_kernel(fast, count, cols, ns):
-    greet_near(count)
-    act = deliver(1, ns.nat1, ns.act, ns.bounce, ns.ds_, ns.dr_, ns.db)
-    act[0]()
-    sums = []
-    if fast:
-        grid = lambda ref, like: ref.reshape((4, 4) + like.shape[-2:])
-        sums = [reducer(ns, f"w{k}", 1, ref, out) for k, (ref, out) in enumerate(((ns.dw1.reshape(4, 4, -1, ns.dw1.shape[1]), ns.gw1), (ns.dw2.reshape(4, 4, -1, ns.dw2.shape[1]), ns.gw2)))]
-
-    def all_(step):
-        return lambda: [getattr(r, step)() for r in sums]
-
-    back_ff_phase(1, count, ns, ns.top, (ns.z, ns.st, ns.n, ns.g, ns.gp), ns.w1, ns.w2, lambda h: act[1]() if h == 2 else None, all_("start"))
-    back_conv_phase(1, cols, ns, ns.a, ns.tiny, script(all_("plane"), nothing, all_("onward"), act[3], nothing, all_("line")))
-    ns.tiny[56:64] = ns.small[...]
-    back_mid_phase(ns, script(nothing, all_("total"), nothing, nothing))
-    all_("finish")()
-
-
-def back_encoder_kernel(fast, count, cols, ns):
+def with_names(ns, **names):
+    out = Names()
+    out.__dict__.update(ns.__dict__)
+    out.__dict__.update(names)
+    return out
+
+
+def back_kernel(fast, count, cols, ns):
     s, d, g, m, p = where_am_i()
     greet_near(count)
-    gi1 = deliver(1, ns.nat1, ns.gi, ns.bounce1, ns.ds1, ns.dr1_, ns.db1)
-    gi0 = deliver(0, ns.nat0, ns.gi, ns.bounce0, ns.ds0, ns.dr0_, ns.db0)
-    deep, mats = [], []
+    acts = [deliver(k, getattr(ns, f"nat{k}"), ns.act, getattr(ns, f"bounce{k}"), ns.ds.at[k], ns.dr.at[k], ns.db.at[k]) for k in range(2)]
+    gi1, gi0 = (deliver(1 - k, ns.nat, ns.gi, getattr(ns, f"bounce{2 + k}"), ns.ds.at[2 + k], ns.dr.at[2 + k], ns.db.at[2 + k]) for k in range(2))
+    w_dec = w_enc = m_all = r_up = r_down = []
     if fast:
-        deep = [reducer(ns, f"r{k}", sec, getattr(ns, part), getattr(ns, out)) for k, (sec, part, out) in enumerate(
-            ((0, "pr0", "gr0"), (1, "pr1", "gr1"), (0, "pm0", "gm0"), (1, "pm1", "gm1")))]
-        mats = [reducer(ns, f"w{k}", 0, ref, out) for k, (ref, out) in enumerate(((ns.dw1.reshape(4, 4, -1, ns.dw1.shape[1]), ns.gw1), (ns.dw2.reshape(4, 4, -1, ns.dw2.shape[1]), ns.gw2)))]
-
-    def all_(step, group):
-        return lambda: [getattr(r, step)() for r in group]
-
-    all_("start", deep)()
-    gi1[0]()
-    steps = {1: all_("plane", deep), 3: gi1[1]}
-    back_ff_phase(0, count, ns, ns.top, (ns.z, ns.st, ns.n, ns.g, ns.gp), ns.w1, ns.w2, lambda h: steps.get(h, nothing)(), all_("start", mats))
-    back_conv_phase(0, cols, ns, ns.a, ns.tiny0, script(
-        all_("onward", deep), all_("plane", mats), all_("line", deep), lambda: (all_("onward", mats)(), gi1[3]()), nothing, all_("line", mats)))
+        cut = lambda ref: ref.reshape(4, 4, ref.shape[0] // 16, ref.shape[1])
+        w_dec = [reducer(ns, "w0", 1, cut(ns.dw1), ns.gw1_1), reducer(ns, "w1", 1, cut(ns.dw2), ns.gw2_1)]
+        w_enc = [reducer(ns, "w0", 0, cut(ns.dw1), ns.gw1_0), reducer(ns, "w1", 0, cut(ns.dw2), ns.gw2_0)]
+        m_all = [reducer(ns, f"m{k}", k, cut(getattr(ns, f"dm{k}")), getattr(ns, f"gm{k}")) for k in range(2)]
+        r_up = [reducer(ns, "r1", 1, ns.dr1.reshape(4, 4, -1, ns.dr1.shape[3]), ns.gr1)]
+        r_down = [reducer(ns, "r0", 0, ns.dr0.reshape(4, 4, -1, ns.dr0.shape[1]), ns.gr0)]
+
+    def do(*steps):
+        def action(*_):
+            for step in steps:
+                if isinstance(step, tuple):
+                    for r in step[0]:
+                        getattr(r, step[1])()
+                else:
+                    step()
+
+        return action
+
+    def keep_dw(sec):
+        if not fast:
+            copies = [pltpu.make_async_copy(ns.dw1, getattr(ns, f"dw1_{sec}"), ns.ps.at[0]), pltpu.make_async_copy(ns.dw2, getattr(ns, f"dw2_{sec}"), ns.ps.at[1])]
+            for copy in copies:
+                copy.start()
+            for copy in copies:
+                copy.wait()
+
+    def at_step(**actions):
+        return lambda h: actions.get(f"h{h}", nothing)()
+
+    do(*(act[0] for act in acts))()
+    dec = with_names(ns, halo=ns.halo1, slots=ns.slots1, send=ns.send1, recv=ns.recv1, hsend=ns.hsend1, hrecv=ns.hrecv1)
+    back_ff_phase(1, count, dec, ns.top, (ns.z1, ns.st1), ns.w1_1, ns.w2_1, at_step(h3=do(*(act[1] for act in acts))), do((w_dec, "start"), lambda: keep_dw(1)))
+    back_conv_phase(1, cols, dec, ns.a1, ns.tiny1, script(
+        do((w_dec, "plane")), nothing, do(*(act[3] for act in acts)), do((w_dec, "onward")), nothing, do((w_dec, "line"))))
+    ns.tiny1[56:64] = ns.small[...]
+    back_mid_phase(ns, script(gi1[0], do((m_all, "start")), do((w_dec, "total"), gi1[1]), do((r_up, "start"), (m_all, "plane"))))
+    do((r_down, "start"), (w_dec, "finish"))()
+
+    back_ff_phase(0, count, ns, ns.dym, (ns.z0, ns.st0), ns.w1_0, ns.w2_0, at_step(
+        h0=do((r_up, "plane")), h2=do((m_all, "onward")), h4=do((r_down, "plane")),
+    ), do((w_enc, "start"), (m_all, "line"), lambda: keep_dw(0)))
+    do((r_up, "onward"), (w_enc, "plane"))()
+    back_conv_phase(0, cols, ns, ns.a0, ns.tiny0, script(
+        do((r_down, "onward"), (r_up, "line")), do((m_all, "total")), do((w_enc, "onward")), do((r_down, "line"), gi1[3]), do((r_up, "total")), do((w_enc, "line"))))
     ns.tiny0[56:64] = ns.small[...]
-
-    def out(c, carry):
-        cells = ns.dz[pl.ds(pl.multiple_of(c * 128, 128), 128)]
-        ns.nat0[:, c] = to_natural(cells, ns.back[...], ns.gather[...])
-        return carry
-
-    lax.fori_loop(0, cols // 16, out, 0)
+    to_natural(ns.dz[...], ns.back[...], ns.gather[...], ns.nat)
     gi0[0]()
-    all_("total", deep)()
     if fast:
         sm, tiny, ts, tr = ns.sm, ns.tiny, ns.ts, ns.tr
         sm[0] = ns.tiny0[...]
@@ -1074,6 +1121,7 @@
                 c.start()
             if base == 1:
                 gi0[1]()
+                do((r_down, "total"))()
             for step in range(1, 4):
                 arrived(tiny.at[base + step], tr.at[base + step])
             for c in sent:
@@ -1085,10 +1133,7 @@
                 ns.total[...] = total
     else:
         gi0[1]()
-        ns.total[...] = ns.tiny0[...]
-    all_("total", mats)()
-    all_("finish", deep + mats)()
-    gi0[3]()
+    do((w_enc, "total"), (m_all + r_up + r_down + w_enc, "finish"), gi0[3])()
 
 
 class Names:
@@ -1168,109 +1213,71 @@
     ins.update({k: mats[k] for k in ("spread", "gather", "natural", "shifts", "patch", "unpatch", "edges", "back", "pick")})
     outs = dict(
         par=((2, 56, cw), F32), bias=((2, 8, hw), F32), ocean=((cells, 128), F32), coarse=((deep_cells, 128), F32),
-        st0=((8, cw), F32), st1=((8, cw), F32), a0=field(BF), a1=field(BF), skip=field(BF), up=field(BF),
-        pieces=((4, deep_cells, cw), BF), deep=((deep_cells, nw), BF), nat1=natural,
-        z0=((cols, 8, cw), F32, ANY), z1=((cols, 8, cw), F32, ANY), cot8=natural + (ANY,), act=((4, 4, tiles, 16, c), BF, ANY),
+        st0=((8, cw), F32), st1=((8, cw), F32), cot8=natural + (ANY,),
     )
-    for k in range(2):
-        outs.update({f"n{k}": field(BF) + (ANY,), f"g{k}": ((cells, hw), BF, ANY), f"gp{k}": ((cells, hw), BF, ANY)})
+    held = dict(
+        a0=field(BF), a1=field(BF), skip=field(BF), up=field(BF), pieces=((4, deep_cells, cw), BF), deep=((deep_cells, nw), BF), nat0=natural, nat1=natural,
+    )
+    outs.update({k + "_out": v + (ANY,) for k, v in held.items()}, z0_out=((cols, 8, cw), F32, ANY), z1_out=((cols, 8, cw), F32, ANY))
     outs.update({k + "_out": ((4, 4) + shapes[v], BF, ANY) for k, v in names.items()})
     scratch = dict(
         x14=pltpu.VMEM((14, tiles, 16, c), BF), land2=pltpu.VMEM((2, 8, land_cols), jnp.int32),
-        S=pltpu.VMEM((7, 2, cols + 6, 8, 128), F32), kb=pltpu.VMEM((49, 8, cw), F32), z=pltpu.VMEM((cols, 8, cw), F32),
-        h=pltpu.VMEM((cells, cw), F32), n_st=pltpu.VMEM((2, 256, cw), BF), g_st=pltpu.VMEM((2, 256, hw), BF), gp_st=pltpu.VMEM((2, 256, hw), BF),
-        nat0=pltpu.VMEM(*natural), bounce=pltpu.VMEM(*natural), halo=pltpu.VMEM(*edge_rows), packed=pltpu.VMEM(*edge_rows),
+        z=pltpu.VMEM((cols, 8, cw), F32),
+        h=pltpu.VMEM((cells, cw), F32),
+        halo=pltpu.VMEM(*edge_rows), packed=pltpu.VMEM(*edge_rows), y1=pltpu.VMEM(*field(BF)),
         stats=pltpu.VMEM((8, cw), F32), slots=pltpu.VMEM((count // 2 + 1, 8, cw), F32), slots1=pltpu.VMEM((count // 2 + 1, 8, cw), F32),
         send=DMA((count,)), recv=DMA((count,)), send1=DMA((count,)), recv1=DMA((count,)),
         xs=DMA((4,)), xr=DMA((2,)), ls=DMA((4,)), lr=DMA((2,)), hs=DMA((2,)), hr=DMA((2,)), ps=DMA((6, 2)), pr=DMA((6,)), cs=DMA((4,)), cr=DMA((2,)),
-        ds_=DMA((2, 2)), dr_=DMA((4,)), db=DMA((2,)), es=DMA((2,)), er=DMA((2,)), gs=DMA((8, 12)), gr=DMA((8, 12)), save=DMA((8,)), keep=DMA((2,)),
-        ff_sem=DMA((3, 2)),
+        es=DMA((2,)), er=DMA((2,)), gs=DMA((8, 12)), gr=DMA((8, 12)), save=DMA((8,)), keep=DMA((10,)),
     )
-    scratch.update({k: pltpu.VMEM((4, 4) + shapes[v], BF) for k, v in names.items()})
+    scratch.update({k: pltpu.VMEM((4, 4) + shapes[v], BF) for k, v in names.items()}, **{k: pltpu.VMEM(*v) for k, v in held.items()})
     if fast:
         scratch.update({f"shard{k}": pltpu.VMEM((2,) + shapes[k], BF) for k in range(4)})
     fw = build("forward", lambda ns: forward_kernel(fast, count, cols, ns), ins, outs, scratch, {}, 1, 63)
-    par, ocean, coarse, bias = fw.par, fw.ocean, fw.coarse, fw.bias
-    w1_0, w2_0, w1_1, w2_1 = (v.reshape(r) for v, r in zip((fw.w1_0_out, fw.w2_0_out, fw.w1_1_out, fw.w2_1_out), ((cw, hw), (hw, cw)) * 2))
-    r0, r1 = fw.r0_out.reshape(4 * cw, nw), fw.r1_out.reshape(GROUPS, 2, padded(n), 2 * cw)
-
-    def kept(k):
-        names = ("z", "st", "n", "g", "gp", "a")
-        ins = {v: at_any(getattr(fw, f"{v}{k}")) for v in names}
-        ins["z"] = at_any(ins["z"][0].reshape(cells, cw))
-        ins["st"] = getattr(fw, f"st{k}")
-        return ins
-
-    mats_of = lambda *names: {k: mats[k] for k in names}
-    common = dict(par=par, ocean=ocean, **mats_of("shifts", "edges", "back", "gather"))
-    outs_w = dict(gw1=((2,) + half_shape(shapes[0]), F32), gw2=((2,) + half_shape(shapes[1]), F32)) if fast else {}
     wide_w = dict(dw1=((cw, hw), BF), dw2=((hw, cw), BF))
-    rows_of = lambda names: {k: pltpu.VMEM(*v) for k, v in names.items()}
-    small_space = dict(
-        dz=pltpu.VMEM(*field(BF)), packed=pltpu.VMEM(*edge_rows), halo=pltpu.VMEM(*edge_rows), small=pltpu.VMEM((8, cw), F32),
-        stats=pltpu.VMEM((8, cw), F32), slots=pltpu.VMEM((count // 2 + 1, 8, cw), F32), send=DMA((count,)), recv=DMA((count,)),
-        hsend=DMA((2,)), hrecv=DMA((2,)), load_sem=DMA((8,)), col_sem=DMA((2, 2)),
+    bounce = natural + (ANY,)
+    names = ("par", "ocean", "coarse", "bias", "st0", "st1")
+    ins = dict(top=fw.cot8, **{k: getattr(fw, k) for k in names})
+    ins.update({k: mats[k] for k in ("shifts", "edges", "back", "gather", "spread", "turn", "patch", "unpatch")})
+    ins.update({k: at_any(getattr(fw, k + "_out")) for k in ("nat0", "nat1", "a0", "a1", "up", "skip", "deep", "pieces")})
+    ins.update({k: at_any(getattr(fw, k + "_out").reshape(cells, cw)) for k in ("z0", "z1")})
+    views = dict(w1_0=(cw, hw), w2_0=(hw, cw), w1_1=(cw, hw), w2_1=(hw, cw), m0=(cw, cw), m1=(cw, cw), r0=(4 * cw, nw), r1=(GROUPS, 2, padded(n), 2 * cw))
+    ins.update({k: at_any(getattr(fw, k + "_out").reshape(v)) for k, v in views.items()})
+    outs = dict(
+        act=((4, 4, tiles, 16, c), BF, ANY), gi=((4, 4, tiles, 16, c), BF, ANY), tiny0=((64, cw), F32), tiny1=((64, cw), F32),
+        dm0=((cw, cw), BF), dm1=((cw, cw), BF), dr0=(views["r0"], BF, ANY), dr1=(views["r1"], BF, ANY), **{f"bounce{k}": bounce for k in range(4)},
     )
-    banks = {}
+    space = {k: pltpu.VMEM(*v) for k, v in dict(dym=field(F32), dz=field(BF), packed=edge_rows, halo=edge_rows, halo1=edge_rows, nat=natural, **wide_w).items()}
+    space.update(small=pltpu.VMEM((8, cw), F32), stats=pltpu.VMEM((8, cw), F32))
+    for k in ("", "1"):
+        space.update({"slots" + k: pltpu.VMEM((count // 2 + 1, 8, cw), F32), "send" + k: DMA((count,)), "recv" + k: DMA((count,)), "hsend" + k: DMA((2,)), "hrecv" + k: DMA((2,))})
+    space.update(load_sem=DMA((8,)), ds=DMA((4, 2, 2)), dr=DMA((4, 4)), db=DMA((4, 2)), ps=DMA((2,)))
     if fast:
-        banks = {**reduce_bank("w0", shapes[0]), **reduce_bank("w1", shapes[1])}
-    give_w = not fast
-    bounce = natural + (ANY,)
-    dec_outs = dict(
-        act=((4, 4, tiles, 16, c), BF, ANY), bounce=bounce, tiny=((64, cw), F32), dym=field(F32), nat=natural,
-        dm0=((cw, cw), BF), dm1=((cw, cw), BF), dr1=((GROUPS, 2, padded(n), 2 * cw), BF), dr0=((4 * cw, nw), BF), **outs_w,
-    )
-    if give_w:
-        dec_outs.update(wide_w)
-    dec = build(
-        "decoder_back", lambda ns: back_decoder_kernel(fast, count, cols, ns),
-        dict(
-            nat1=at_any(fw.nat1), act_in=at_any(fw.act), top=fw.cot8, w1=at_any(w1_1), w2=at_any(w2_1), **kept(1),
-            up=at_any(fw.up), skip=at_any(fw.skip), deep=at_any(fw.deep), pieces=at_any(fw.pieces), r0=at_any(r0), r1=at_any(r1),
-            m0=at_any(fw.m0_out.reshape(cw, cw)), m1=at_any(fw.m1_out.reshape(cw, cw)), coarse=coarse,
-            **common, **mats_of("spread", "turn", "patch", "unpatch"),
-        ),
-        dec_outs, dict(ds_=DMA((2, 2)), dr_=DMA((4,)), db=DMA((2,)), **small_space, **banks, **({} if give_w else rows_of(wide_w))), {"act_in": "act"}, 2, 63,
-    )
-    enc_ins = dict(
-        nat1=at_any(dec.nat), top=dec.dym, tiny1=dec.tiny, w1=at_any(w1_0), w2=at_any(w2_0), **kept(0), **common,
-    )
-    enc_outs = dict(gi=((4, 4, tiles, 16, c), BF, ANY), bounce0=bounce, bounce1=bounce, total=((64, cw), F32), **outs_w)
-    enc_banks = dict(banks)
-    if fast:
-        view = lambda v, k: at_any(v.reshape((4, 4) + shapes[k]))
-        enc_ins.update(pr0=view(dec.dr0, 2), pr1=view(dec.dr1, 2), pm0=view(dec.dm0, 3), pm1=view(dec.dm1, 3))
-        for name, k in (("r0", 2), ("r1", 2), ("r2", 3), ("r3", 3)):
-            enc_banks.update(reduce_bank(name, shapes[k]))
-        for name, k in (("gr0", 2), ("gr1", 2), ("gm0", 3), ("gm1", 3)):
-            enc_outs[name] = ((2,) + half_shape(shapes[k]), F32)
-        enc_banks.update(sm=pltpu.VMEM((2, 64, cw), F32), tiny=pltpu.VMEM((9, 64, cw), F32), ts=DMA((9,)), tr=DMA((9,)))
-    if give_w:
-        enc_outs.update(wide_w)
-    enc = build(
-        "encoder_back", lambda ns: back_encoder_kernel(fast, count, cols, ns), enc_ins, enc_outs,
-        dict(
-            nat0=pltpu.VMEM(*natural), dym=pltpu.VMEM(*field(F32)), tiny0=pltpu.VMEM((64, cw), F32), ds0=DMA((2, 2)), dr0_=DMA((4,)), db0=DMA((2,)),
-            ds1=DMA((2, 2)), dr1_=DMA((4,)), db1=DMA((2,)), **small_space, **enc_banks, **({} if give_w else rows_of(wide_w)),
-        ),
-        {}, 3, 63,
-    )
-    last, tiny = enc, enc.total
+        for name, k in (("w0", 0), ("w1", 1), ("m0", 3), ("m1", 3), ("r0", 2), ("r1", 2)):
+            space.update(reduce_bank(name, shapes[k]))
+        for name, k in (("gw1_0", 0), ("gw2_0", 1), ("gw1_1", 0), ("gw2_1", 1), ("gr0", 2), ("gr1", 2), ("gm0", 3), ("gm1", 3)):
+            outs[name] = ((2,) + half_shape(shapes[k]), F32)
+        outs["total"] = ((64, cw), F32)
+        space.update(sm=pltpu.VMEM((2, 64, cw), F32), tiny=pltpu.VMEM((9, 64, cw), F32), ts=DMA((9,)), tr=DMA((9,)))
+    else:
+        outs.update({f"{k}_{sec}": v + (ANY,) for k, v in wide_w.items() for sec in range(2)})
+    bw = build("backward", lambda ns: back_kernel(fast, count, cols, ns), ins, outs, space, {}, 2, 63)
     if fast:
         rows_of = lambda v: v.reshape(-1, v.shape[-1])
-        gw1 = unpack_in(rows_of(jnp.where(s == 0, enc.gw1, dec.gw1)), c, hid)
-        gw2 = unpack_in(jnp.where(s == 0, enc.gw2, dec.gw2).transpose(1, 0, 2).reshape(padded(hid), cw), hid, c)
-        gres = jnp.where(s == 0, unpack_down(rows_of(enc.gr0), c, n), unpack_up(rows_of(enc.gr1), c, n))
-        gmm = unpack_in(rows_of(jnp.where(s == 0, enc.gm0, enc.gm1)), c, c)
+        tiny = bw.total
+        gw1 = unpack_in(rows_of(jnp.where(s == 0, bw.gw1_0, bw.gw1_1)), c, hid)
+        gw2 = unpack_in(jnp.where(s == 0, bw.gw2_0, bw.gw2_1).transpose(1, 0, 2).reshape(padded(hid), cw), hid, c)
+        gres = jnp.where(s == 0, unpack_down(rows_of(bw.gr0), c, n), unpack_up(rows_of(bw.gr1), c, n))
+        gmm = unpack_in(rows_of(jnp.where(s == 0, bw.gm0, bw.gm1)), c, c)
     else:
         scatter = lambda v: lax.psum_scatter(v.astype(F32).reshape(-1), both, scatter_dimension=0, tiled=True)
-        gw1 = scatter(jnp.stack([unpack_in(v, c, hid) for v in (enc.dw1, dec.dw1)]))
-        gw2 = scatter(jnp.stack([unpack_in(v, hid, c) for v in (enc.dw2, dec.dw2)]))
-        gres = scatter(jnp.stack([unpack_down(dec.dr0, c, n), unpack_up(dec.dr1, c, n)]))
-        gmm = scatter(jnp.stack([unpack_in(v, c, c) for v in (dec.dm0, dec.dm1)]))
-        tiny = lax.psum(jnp.stack([enc.total, dec.tiny]), both)[s]
-    activations = dec.act.reshape(1, batches, height, cols, c)
-    grad_input = last.gi.astype(F32).reshape(1, batches, height, cols, c)
+        gw1 = scatter(jnp.stack([unpack_in(v, c, hid) for v in (bw.dw1_0, bw.dw1_1)]))
+        gw2 = scatter(jnp.stack([unpack_in(v, hid, c) for v in (bw.dw2_0, bw.dw2_1)]))
+        gres = scatter(jnp.stack([unpack_down(bw.dr0, c, n), unpack_up(bw.dr1, c, n)]))
+        gmm = scatter(jnp.stack([unpack_in(v, c, c) for v in (bw.dm0, bw.dm1)]))
+        tiny = lax.psum(jnp.stack([bw.tiny0, bw.tiny1]), both)[s]
+    activations = bw.act.reshape(1, batches, height, cols, c)
+    grad_input = bw.gi.astype(F32).reshape(1, batches, height, cols, c)
     narrow = lambda v: v.reshape(-1, GROUPS, padded(c))[:, :, : c // GROUPS].reshape(-1, c)
     fine = narrow(tiny[:59])
     grad_bias_in = tiny[59:63].reshape(-1)[:hw].reshape(GROUPS, -1)[:, : hid // GROUPS].reshape(1, hid)

time: 433 us -> 376 us (0.87)
  the two profiles are of different devices: /device:TPU:0 before, /device:TPU:8 now
where the time goes in v4:
time: 376 us; the launch traced here: 369 us
  Pallas kernels  320 us (85%)
  local copies, waits for them, and re-layouts  29.3 us (8%)
  other arithmetic  17.9 us (5%)
    pallas_call x2, Pallas kernels, build(): pl.pallas_call(kernel, name=name, out_shape=[jax.ShapeDtypeStruct(v[0], v...  320 us

profile of v4, /device:TPU:8, one launch (start us, length us, event | category | flops | bytes accessed | tf_op | source)
XLA Modules:
  0.0 368.7 jit_solution(6118783830394011637)
XLA Ops:
  0.7 0.5 broadcast.57
  1.2 1.3 reduce.25
  2.5 1.3 reduce.24
  3.9 1.3 reduce.23
  5.2 1.3 pad.40.refs_1_
  6.5 0.7 reduce.3
  7.2 0.1 reshape.156
  7.3 0.1 reshape.157
  7.4 0.8 convert_element_type.35
  8.2 0.6 pad.44.refs_3_
  8.8 0.2 reshape.165
  9.1 0.8 squeeze_reshape.11.refs_8_
  9.9 1.3 convert_reduce_fusion.2
  11.2 0.4 reshape.159
  11.6 0.8 squeeze_reshape.9.refs_5_
  12.5 1.3 convert_reduce_fusion.1
  13.8 0.8 convert_reduce_fusion
  14.6 0.1 copy.47
  14.8 0.2 concatenate.19
  15.0 0.2 concatenate.18
  15.2 0.2 concatenate.17
  15.4 0.3 select_maximum_fusion
  15.7 0.1 copy.51
  15.8 0.7 pad.42.refs_2_
  16.5 0.9 reshape.160
  17.4 0.4 copy.62
  17.9 0.8 copy.55.refs_6_
  18.6 1.2 reshape.161
  19.8 0.1 pad.47
  19.9 0.3 reshape.162
  20.3 2.0 reshape.163
  22.2 0.3 pad_bitcast_fusion
  22.5 1.2 copy.53
  23.7 0.2 reshape.164
  23.9 0.1 copy.54
  24.1 0.7 broadcast_select_fusion.1.refs_7_
  24.8 136.7 %forward.1 = (f32[2,56,512]{2,1,0:T(8,128)}, f32[2,8,1792]{2,1,0:T(8,128)}, f32[1280,128]{1,0:T(8,128)}, f32[320,128]{1,0:T(8,128)}, f32[8,512]{1,0:T(8,128)}, /...) custom-call(bf16[4,4,10,16,400]{4,3,2,1,0:T(8,128)(2,1)} %bitcast.62, ...), custom_call_target="tpu_custom_call" | custom-call | tf_op jit(solution)/shard_map/forward/pallas_call | solution.py:1155
  161.5 183.3 %backward.1 = (bf16[4,4,10,16,400]{4,3,2,1,0:T(8,128)(2,1)}, bf16[4,4,10,16,400]{4,3,2,1,0:T(8,128)(2,1)}, f32[64,512]{1,0:T(8,128)}, f32[64,512]{1,0:T(8,128)},...) custom-call(bf16[8,10,16,400]{3,2,1,0:T(8,128)(2,1)} %get-tuple-elem, ...), custom_call_target="tpu_custom_call" | custom-call | tf_op jit(solution)/shard_map/backward/pallas_call | solution.py:1155
  344.8 0.8 slice_bitcast_fusion
  345.6 0.1 reshape.181
  345.7 0.7 reshape.182
  346.4 0.9 broadcast_select_fusion.3
  347.2 0.1 reshape_reshape.19
  347.4 0.8 reshape.185
  348.2 1.0 broadcast_select_fusion.2
  349.2 0.2 reshape_reshape.15
  349.4 1.0 broadcast_in_dim_reshape.6
  350.4 0.1 copy.57
  350.6 0.1 copy.56
  350.7 0.5 slice_reduce_fusion
  351.2 0.7 slice.64
  351.9 0.7 slice.59
  352.6 0.7 slice.57
  353.2 0.8 copy.61
  354.0 0.4 copy.58
  354.5 1.4 broadcast_in_dim_reshape.7
  355.8 0.3 reshape_reshape.17
  356.2 1.0 reshape.183
  357.2 0.3 copy.59
  357.5 1.7 copy.60
  359.2 1.5 reshape.184
  360.7 1.1 broadcast_select_fusion
  361.8 5.0 %convert.1 = f32[1,4,4,160,400]{4,3,2,1,0:T(8,128)} convert(bf16[1,4,4,160,400]{4,3,2,1,0:T(8,128)(2,1)} %bitcast.65) | non-fusion elementwise | flops 1024000 | bytes 6144000 | tf_op jit(solution)/shard_map/reshape | solution.py:1280
  366.7 1.5 copy.65
  (27 shorter events, 0.3 us)
Async XLA Ops:
  0.6 13.2 %copy-start.3 = (f32[1,80000]{1,0:T(1,128)S(1)}, f32[1,80000]{1,0:T(1,128)}, u32[]{:S(2)}) copy-start(f32[1,80000]{1,0:T(1,128)} %param.32) | copy-start | bytes 960004
  0.7 14.0 %copy-start.7 = (f32[1,49,400]{2,0,1:T(1,128)S(1)}, f32[1,49,400]{2,0,1:T(1,128)}, u32[]{:S(2)}) copy-start(f32[1,49,400]{2,0,1:T(1,128)} %param.25) | copy-start | bytes 235204
  344.8 5.6 %copy-start.4 = (f32[2,112,256]{2,1,0:T(8,128)S(1)}, f32[2,112,256]{2,1,0:T(8,128)}, u32[]{:S(2)}) copy-start(f32[2,112,256]{2,1,0:T(8,128)} %get-tuple-element.77) | copy-start | bytes 688132
  344.8 5.6 %copy-start.5 = (f32[2,112,256]{2,1,0:T(8,128)S(1)}, f32[2,112,256]{2,1,0:T(8,128)}, u32[]{:S(2)}) copy-start(f32[2,112,256]{2,1,0:T(8,128)} %get-tuple-element.78) | copy-start | bytes 688132
  347.3 3.2 copy-start.6
  350.7 5.1 %copy-start.2 = (f32[2,64,1024]{2,1,0:T(8,128)S(1)}, f32[2,64,1024]{2,1,0:T(8,128)}, u32[]{:S(2)}) copy-start(f32[2,64,1024]{2,1,0:T(8,128)} %get-tuple-element.79) | copy-start | bytes 1572868
  355.8 1.3 copy-start.1
  361.8 5.0 %copy-start = (bf16[4,4,10,16,400]{4,3,2,1,0:T(8,128)(2,1)S(1)}, bf16[4,4,10,16,400]{4,3,2,1,0:T(8,128)(2,1)}, u32[]{:S(2)}) copy-start(bf16[4,4,10,16,400]{4,3,2,1,0:T(8,128)(2,1)} %get-tuple-element.72) | copy-start | bytes 6144004

commit v5 on v4

--- a/solution.py
+++ b/solution.py
@@ -31,7 +31,7 @@
     return out.astype(ml_dtypes.bfloat16)
 
 
-def matrices(channels):
+def matrices(channels, hidden, deep):
     group, wide = channels // GROUPS, padded(channels)
     spread = selector(channels, GROUPS * wide, [(c, c // group * wide + c % group) for c in range(channels)])
     natural = selector(896, 224, [(i * 128 + q * 8 + p, (p + i) * 16 + q) for i in range(7) for q in range(16) for p in range(8)])
@@ -49,8 +49,18 @@
         [((i * 2 + j) * 64 + b * 4 + a, (2 * b + j) * 8 + 2 * a + i) for i in range(2) for j in range(2) for b in range(16) for a in range(4)],
     )
     pick = selector(128, 16, [(q * 8 + p, p // 4 * 8 + p % 4) for q in range(16) for p in range(8)])
+
+    def widen(width):
+        group, wide = width // GROUPS, padded(width)
+        return selector(width, GROUPS * wide, [(v, v // group * wide + v % group) for v in range(width)])
+
+    half_hidden = widen(hidden)[: hidden // 2, : GROUPS * padded(hidden) // 2]
+    deep_spread = widen(deep)
+    band = channels // GROUPS
+    rows = selector(4 * wide, -(-4 * band // 16) * 16, [(k * wide + r, k * band + r) for k in range(4) for r in range(band)])
     return dict(
-        pick=pick, spread=spread, gather=np.ascontiguousarray(spread.T), natural=natural, shifts=shifts, turn=turn,
+        half_hidden=half_hidden, half_hidden_back=np.ascontiguousarray(half_hidden.T), deep_spread=deep_spread,
+        deep_back=np.ascontiguousarray(deep_spread.T), rows=rows, pick=pick, spread=spread, gather=np.ascontiguousarray(spread.T), natural=natural, shifts=shifts, turn=turn,
         back=np.ascontiguousarray(turn.T), edges=edges, patch=patch, unpatch=np.ascontiguousarray(patch.T),
     )
 
@@ -573,6 +583,144 @@
     pl.run_scoped(phase, pltpu.VMEM((cells, wide), BF), pltpu.VMEM((cells, hidden), BF), pltpu.VMEM((cells, wide), F32))
 
 
+def parts3(value):
+    high = value.astype(BF)
+    rest = value - high.astype(F32)
+    middle = rest.astype(BF)
+    return high, middle, (rest - middle.astype(F32)).astype(BF)
+
+
+def select(value, matrix):
+    return sum(dot(v, matrix) for v in parts3(value))
+
+
+def pack_shards(ns, swap):
+    s = lax.axis_index("section")
+    c, wide = ns.spread.shape
+    hid, n = 2 * ns.half_hidden.shape[0], ns.deep_spread.shape[0]
+
+    def phase(nat, half_hidden, deep_spread):
+        got = loads([(ns.half_hidden, half_hidden), (ns.deep_spread, deep_spread)], ns.keep)
+
+        def rows(flat, width):
+            count = flat.shape[1] // width
+            tall = -(-count // 16) * 16
+            nat[tall - 16 : tall] = jnp.zeros((16, nat.shape[1]), F32)
+            for r in range(count):
+                nat[r : r + 1, 0:width] = flat[0:1, r * width : r * width + width]
+            return tall
+
+        tall = rows(ns.w_in, hid)
+        got[0]()
+        size = half_hidden.shape[1]
+        for q in range(2):
+            ns.shard0[s, :, size * q : size * q + size] = dot(nat[0:tall, hid // 2 * q : hid // 2 * q + hid // 2].astype(BF), half_hidden[...]).astype(BF)
+        swap(0)
+        tall = rows(ns.w_out, c)
+        ns.shard1[s] = dot(nat[0:tall, 0:c].astype(BF), ns.spread[...]).astype(BF)
+        swap(1)
+        got[1]()
+
+        @pl.when(s == 0)
+        def _():
+            tall = rows(ns.resample, n)
+            laid = dot(nat[0:tall, 0:n].astype(BF), deep_spread[...]).astype(BF)
+            ns.shard2[0] = dot(ns.rows[...], laid).astype(BF)
+
+        @pl.when(s == 1)
+        def _():
+            tall = rows(ns.resample, 4 * c)
+            for q in range(4):
+                ns.shard2[1, tall * (q // 2) : tall * (q // 2) + tall, wide * (q % 2) : wide * (q % 2) + wide] = dot(
+                    nat[0:tall, c * q : c * q + c].astype(BF), ns.spread[...]).astype(BF)
+
+        swap(2)
+        tall = rows(ns.merge, c)
+        ns.shard3[s] = dot(nat[0:tall, 0:c].astype(BF), ns.spread[...]).astype(BF)
+        swap(3)
+        nat[48:64] = jnp.zeros((16, nat.shape[1]), F32)
+        nat[0:49, 0:c] = ns.kernel[0]
+        for k, ref in enumerate((ns.bn_gain, ns.bn_bias, ns.bias_out)):
+            nat[49 + k : 50 + k, 0:c] = ref[...]
+        ns.par[s] = select(nat[0:56, 0:c], ns.spread[...])
+        swap(4)
+        nat[0:8] = jnp.zeros((8, nat.shape[1]), F32)
+        nat[0:1, 0:hid] = ns.bias_in[...]
+        for q in range(2):
+            ns.bias[s, :, size * q : size * q + size] = select(nat[0:8, hid // 2 * q : hid // 2 * q + hid // 2], half_hidden[...])
+        swap(5)
+
+    pl.run_scoped(phase, pltpu.VMEM((112, max(hid, 4 * c)), F32), pltpu.VMEM(ns.half_hidden.shape, BF), pltpu.VMEM(ns.deep_spread.shape, BF))
+
+
+def unpack_sums(ns, first, second):
+    s = lax.axis_index("section")
+    wide, c = ns.gather.shape
+    hid, n = 2 * ns.half_hidden_back.shape[1], ns.deep_back.shape[1]
+
+    def phase(nat, half_back, deep_back):
+        got = loads([(ns.half_hidden_back, half_back), (ns.deep_back, deep_back)], ns.load_sem)
+        got[0]()
+        got[1]()
+
+        def narrow(value, matrix):
+            return dot(value.astype(BF), matrix) + dot((value - value.astype(BF).astype(F32)).astype(BF), matrix)
+
+        def rows(out, width, count):
+            for r in range(count):
+                out[0:1, r * width : r * width + width] = nat[r : r + 1, 0:width]
+
+        first()
+        nat[0:64, 0:c] = narrow(ns.total[...], ns.gather[...])
+        ns.gk[0] = nat[0:49, 0:c]
+        ns.gs[...] = nat[56:57, 0:c]
+        ns.gg[...] = nat[57:58, 0:c]
+        ns.gbo[...] = nat[58:59, 0:c]
+        size = half_back.shape[0]
+        flat = jnp.concatenate([ns.total[59 + k : 60 + k] for k in range(-(-2 * size // wide))], axis=1)
+        for q in range(2):
+            ns.gbi[0:1, hid // 2 * q : hid // 2 * q + hid // 2] = narrow(jnp.broadcast_to(flat[:, size * q : size * q + size], (8, size)), half_back[...])[0:1]
+        merge = ns.gm.reshape(-1, wide)
+        nat[0 : merge.shape[0], 0:c] = narrow(merge[...], ns.gather[...])
+        rows(ns.gmm, c, ns.gmm.shape[1] // c)
+        deep = ns.gr.reshape(-1, ns.gr.shape[2])
+
+        @pl.when(s == 0)
+        def _():
+            nat[0 : deep.shape[0], 0:n] = narrow(deep[...], deep_back[...])
+            band, high = c // GROUPS, deep.shape[0] // 4
+            for k in range(4):
+                for r in range(band):
+                    at = n * (band * k + r)
+                    ns.gres[0:1, at : at + n] = nat[high * k + r : high * k + r + 1, 0:n]
+
+        @pl.when(s == 1)
+        def _():
+            high = deep.shape[0] // 2
+            for j in range(2):
+                nat[0 : deep.shape[0], 0:c] = narrow(deep[:, wide * j : wide * j + wide], ns.gather[...])
+                for i in range(2):
+                    for r in range(n // GROUPS):
+                        at = 4 * c * r + c * (2 * i + j)
+                        ns.gres[0:1, at : at + c] = nat[high * i + r : high * i + r + 1, 0:c]
+
+        second()
+        grad = ns.gw1.reshape(-1, ns.gw1.shape[2])
+        for q in range(2):
+            nat[0 : grad.shape[0], hid // 2 * q : hid // 2 * q + hid // 2] = narrow(grad[:, size * q : size * q + size], half_back[...])
+        rows(ns.gwi, hid, ns.gwi.shape[1] // hid)
+        for k in range(2):
+            lanes = wide // 2
+            part = narrow(ns.gw2[k], ns.gather[lanes * k : lanes * k + lanes])
+            if k == 0:
+                nat[0 : ns.gw2.shape[1], 0:c] = part
+            else:
+                nat[0 : ns.gw2.shape[1], 0:c] += part
+        rows(ns.gwo, c, ns.gwo.shape[1] // c)
+
+    pl.run_scoped(phase, pltpu.VMEM((128, max(hid, 4 * c)), F32), pltpu.VMEM(ns.half_hidden_back.shape, BF), pltpu.VMEM(ns.deep_back.shape, BF))
+
+
 def forward_kernel(fast, count, cols, ns):
     s, d, g, m, p = where_am_i()
     greet_near(count)
@@ -581,11 +729,14 @@
     land_begin, land_end = collect_land(ns.land, ns.land2, ns.ls, ns.lr)
     x_begin()
     land_begin()
-    pairs = [(ns.mine, ns.par), (ns.mine_bias, ns.bias)] + [(getattr(ns, f"mine{k}"), getattr(ns, f"shard{k}")) for k in range(4) if fast]
-    far = [remote(src, dst.at[s], ns.ps.at[k, 0], ns.pr.at[k], (1 - s, d)) for k, (src, dst) in enumerate(pairs)]
-    near = [pltpu.make_async_copy(src, dst.at[s], ns.ps.at[k, 1]) for k, (src, dst) in enumerate(pairs)]
-    for c in far + near:
-        c.start()
+    swapped = [getattr(ns, f"shard{k}") for k in range(4)] + [ns.par, ns.bias] if fast else [ns.par, ns.bias]
+
+    def swap(k):
+        return remote(swapped[k].at[s], swapped[k].at[s], ns.ps.at[k], ns.pr.at[k], (1 - s, d))
+
+    def swap_in(k):
+        arrived(swapped[k].at[1 - s], ns.pr.at[k])
+
     fulls = dict(w1_0=ns.w1_0, w2_0=ns.w2_0, r0=ns.r0, m0=ns.m0, m1=ns.m1, r1=ns.r1, w1_1=ns.w1_1, w2_1=ns.w2_1)
     which = dict(w1_0=(0, 0), w2_0=(1, 0), r0=(2, 0), r1=(2, 1), m0=(3, 0), m1=(3, 1), w1_1=(0, 1), w2_1=(1, 1))
     mats = {}
@@ -613,12 +764,27 @@
         for name in names:
             saves[name]().start()
 
-    for k in range(2, len(pairs)):
-        near[k].wait()
-        arrived(pairs[k][1].at[1 - s], ns.pr.at[k])
-        if k == 3:
-            do("start", "w1_0", "w2_0")
-    if not fast:
+    def give(k):
+        swap(k).start()
+        if k == 1:
+            swap_in(0)
+            do("start", "w1_0")
+        if k == 2:
+            swap_in(1)
+            do("start", "w2_0")
+
+    if fast:
+        pack_shards(ns, give)
+        swap_in(2)
+        swap_in(3)
+    else:
+        near = [pltpu.make_async_copy(src, dst.at[s], ns.keep.at[k]) for k, (src, dst) in enumerate(((ns.mine, ns.par), (ns.mine_bias, ns.bias)))]
+        for c in near:
+            c.start()
+        for c in near:
+            c.wait()
+        for k in range(2):
+            swap(k).start()
         do("start", "w1_0", "w2_0")
     do("start", "r0")
     land_end()
@@ -632,9 +798,8 @@
     pl.when(p > 0)(edge(True).start)
     pl.when(p < count - 1)(edge(False).start)
     do("plane", "w1_0", "w2_0")
-    for k in range(2):
-        near[k].wait()
-        arrived(pairs[k][1].at[1 - s], ns.pr.at[k])
+    swap_in(len(swapped) - 2)
+    swap_in(len(swapped) - 1)
 
     @pl.when(p == 0)
     def _():
@@ -721,8 +886,8 @@
     for name, copy in keeps.items():
         if name != "z0":
             copy().wait()
-    for c in far:
-        c.wait_send()
+    for k in range(len(swapped)):
+        swap(k).wait_send()
     pl.when(p > 0)(edge(True).wait_send)
     pl.when(p < count - 1)(edge(False).wait_send)
 
@@ -945,10 +1110,8 @@
             hook()
             if group == 0:
                 got_a()
-            for lane in range(lanes):
-                at = slice((group * lanes + lane) * 128, (group * lanes + lane + 1) * 128)
-
-                field[...] = a[:, at].astype(F32).reshape(field.shape)
+            tiles = [(lane, slice((group * lanes + lane) * 128, (group * lanes + lane + 1) * 128)) for lane in range(lanes)]
+            for lane, at in tiles:
 
                 def step(b, carry):
                     rows = pl.ds(pl.multiple_of(b * 128, 128), 128)
@@ -958,6 +1121,9 @@
                     return carry
 
                 lax.fori_loop(0, cols // 16, step, 0)
+            hook()
+            for lane, at in tiles:
+                field[...] = a[:, at].astype(F32).reshape(field.shape)
                 acc_dk[...] = jnp.zeros(acc_dk.shape, F32)
 
                 def tap_sums(b, carry):
@@ -974,7 +1140,7 @@
                 lax.fori_loop(0, cols // 16, tap_sums, 0)
                 for k in range(49):
                     tiny[48 - k : 49 - k, at] = acc_dk[k].sum(0, keepdims=True)
-                hook()
+            hook()
         tiny[49:56] = jnp.zeros((7, wide), F32)
 
     pl.run_scoped(
@@ -1060,11 +1226,11 @@
     w_dec = w_enc = m_all = r_up = r_down = []
     if fast:
         cut = lambda ref: ref.reshape(4, 4, ref.shape[0] // 16, ref.shape[1])
-        w_dec = [reducer(ns, "w0", 1, cut(ns.dw1), ns.gw1_1), reducer(ns, "w1", 1, cut(ns.dw2), ns.gw2_1)]
-        w_enc = [reducer(ns, "w0", 0, cut(ns.dw1), ns.gw1_0), reducer(ns, "w1", 0, cut(ns.dw2), ns.gw2_0)]
-        m_all = [reducer(ns, f"m{k}", k, cut(getattr(ns, f"dm{k}")), getattr(ns, f"gm{k}")) for k in range(2)]
-        r_up = [reducer(ns, "r1", 1, ns.dr1.reshape(4, 4, -1, ns.dr1.shape[3]), ns.gr1)]
-        r_down = [reducer(ns, "r0", 0, ns.dr0.reshape(4, 4, -1, ns.dr0.shape[1]), ns.gr0)]
+        w_dec = [reducer(ns, "w0", 1, cut(ns.dw1), ns.gw1), reducer(ns, "w1", 1, cut(ns.dw2), ns.gw2)]
+        w_enc = [reducer(ns, "w0", 0, cut(ns.dw1), ns.gw1), reducer(ns, "w1", 0, cut(ns.dw2), ns.gw2)]
+        m_all = [reducer(ns, f"m{k}", k, cut(getattr(ns, f"dm{k}")), ns.gm) for k in range(2)]
+        r_up = [reducer(ns, "r1", 1, ns.dr1.reshape(4, 4, -1, ns.dr1.shape[3]), ns.gr)]
+        r_down = [reducer(ns, "r0", 0, ns.dr0.reshape(4, 4, -1, ns.dr0.shape[1]), ns.gr)]
 
     def do(*steps):
         def action(*_):
@@ -1101,11 +1267,14 @@
         h0=do((r_up, "plane")), h2=do((m_all, "onward")), h4=do((r_down, "plane")),
     ), do((w_enc, "start"), (m_all, "line"), lambda: keep_dw(0)))
     do((r_up, "onward"), (w_enc, "plane"))()
+    def give_dh():
+        to_natural(ns.dz[...], ns.back[...], ns.gather[...], ns.nat)
+        gi0[0]()
+
     back_conv_phase(0, cols, ns, ns.a0, ns.tiny0, script(
-        do((r_down, "onward"), (r_up, "line")), do((m_all, "total")), do((w_enc, "onward")), do((r_down, "line"), gi1[3]), do((r_up, "total")), do((w_enc, "line"))))
+        do((r_down, "onward"), (r_up, "line")), do((m_all, "total"), gi1[3]), do((w_enc, "onward"), (r_down, "line")), do((r_up, "total")),
+        do(give_dh, (w_enc, "line")), gi0[1]))
     ns.tiny0[56:64] = ns.small[...]
-    to_natural(ns.dz[...], ns.back[...], ns.gather[...], ns.nat)
-    gi0[0]()
     if fast:
         sm, tiny, ts, tr = ns.sm, ns.tiny, ns.ts, ns.tr
         sm[0] = ns.tiny0[...]
@@ -1120,7 +1289,6 @@
             for c in sent:
                 c.start()
             if base == 1:
-                gi0[1]()
                 do((r_down, "total"))()
             for step in range(1, 4):
                 arrived(tiny.at[base + step], tr.at[base + step])
@@ -1131,9 +1299,9 @@
                 tiny[5] = total
             else:
                 ns.total[...] = total
-    else:
-        gi0[1]()
-    do((w_enc, "total"), (m_all + r_up + r_down + w_enc, "finish"), gi0[3])()
+    if fast:
+        unpack_sums(ns, do((m_all + r_up + r_down, "finish")), do((w_enc, "total"), (w_enc, "finish")))
+    gi0[3]()
 
 
 class Names:
@@ -1174,25 +1342,21 @@
     fast = dps == GROUPS
     assert batches == 4 and height == 4 and dps % 4 == 0 and sections == 2 and cols % 32 == 0
     s = lax.axis_index("section")
-    mats = {k: jnp.asarray(v) for k, v in matrices(c).items()}
+    mats = {k: jnp.asarray(v) for k, v in matrices(c, hid, n).items()}
     tiles = cols // 16
     both = ("section", "dp")
 
     def packs(parts, w1, w2, rd, ru):
         return pack_in(w1, parts, c, hid), pack_in(w2, parts, hid, c), pack_down(rd, parts, c, n), pack_up(ru, parts, c, n)
 
-    shards = []
-    if fast:
-        w1, w2, rd, ru = packs(1, *(v.astype(BF) for v in (w_in, w_out, resample, resample)))
-        shards = [w1[0], w2[0], jnp.where(s == 0, rd, ru)[0], pack_in(merge.astype(BF), 1, c, c)[0]]
-    else:
+    if not fast:
         flat = [lax.all_gather(v.astype(BF).reshape(-1), both, axis=0, tiled=True) for v in (w_in, w_out, resample, merge)]
         halves = [v.reshape(2, -1) for v in flat]
         whole = [packs(GROUPS, halves[0][k], halves[1][k], halves[2][k], halves[2][k]) for k in range(2)]
-
-    rows = jnp.concatenate([kernel[0], bn_gain, bn_bias, bias_out], axis=0)
-    mine = grow(grow(rows.reshape(-1, GROUPS, c // GROUPS), (52, GROUPS, padded(c))).reshape(52, cw), (56, cw))
-    mine_bias = grow(grow(bias_in.reshape(GROUPS, -1), (GROUPS, padded(hid))).reshape(1, hw), (8, hw))
+        rows = jnp.concatenate([kernel[0], bn_gain, bn_bias, bias_out], axis=0)
+        mine = grow(grow(rows.reshape(-1, GROUPS, c // GROUPS), (52, GROUPS, padded(c))).reshape(52, cw), (56, cw))
+        mine_bias = grow(grow(bias_in.reshape(GROUPS, -1), (GROUPS, padded(hid))).reshape(1, hw), (8, hw))
+
     x = inputs.reshape(batches, height, tiles, 16, c)
     cot = cotangent.reshape(batches, height, tiles, 16, c)
     land_cols = -(-cols // 128) * 128
@@ -1202,15 +1366,18 @@
     edge_rows = ((2, tiles, 48, cw), BF)
     shapes = [(padded(c), hw), (padded(hid), cw), (4 * padded(c), nw), (padded(c), cw)]
     names = dict(w1_0=0, w2_0=1, r0=2, m0=3, m1=3, r1=2, w1_1=0, w2_1=1)
-    ins = dict(x=x, land=grow(land, (8, land_cols)), mine=mine, mine_bias=mine_bias, cot=cot)
+    ins = dict(x=x, land=grow(land, (8, land_cols)), cot=cot)
     if fast:
-        ins.update({f"mine{k}": v for k, v in enumerate(shards)})
+        ins.update(half_hidden=mats["half_hidden"], deep_spread=mats["deep_spread"])
     else:
+        ins.update(mine=mine, mine_bias=mine_bias)
         given = dict(w1_0=whole[0][0], w2_0=whole[0][1], r0=whole[0][2], r1=whole[1][3], w1_1=whole[1][0], w2_1=whole[1][1])
         given.update(m0=pack_in(halves[3][0], GROUPS, c, c), m1=pack_in(halves[3][1], GROUPS, c, c))
         ins.update({k + "_in": v.reshape((4, 4) + shapes[names[k]]) for k, v in given.items()})
     ins = {k: at_any(v) for k, v in ins.items()}
-    ins.update({k: mats[k] for k in ("spread", "gather", "natural", "shifts", "patch", "unpatch", "edges", "back", "pick")})
+    ins.update({k: mats[k] for k in ("spread", "gather", "natural", "shifts", "patch", "unpatch", "edges", "back", "pick", "rows")})
+    if fast:
+        ins.update(w_in=w_in, w_out=w_out, resample=resample, merge=merge.reshape(1, -1), kernel=kernel, bn_gain=bn_gain, bn_bias=bn_bias, bias_in=bias_in, bias_out=bias_out)
     outs = dict(
         par=((2, 56, cw), F32), bias=((2, 8, hw), F32), ocean=((cells, 128), F32), coarse=((deep_cells, 128), F32),
         st0=((8, cw), F32), st1=((8, cw), F32), cot8=natural + (ANY,),
@@ -1227,7 +1394,7 @@
         halo=pltpu.VMEM(*edge_rows), packed=pltpu.VMEM(*edge_rows), y1=pltpu.VMEM(*field(BF)),
         stats=pltpu.VMEM((8, cw), F32), slots=pltpu.VMEM((count // 2 + 1, 8, cw), F32), slots1=pltpu.VMEM((count // 2 + 1, 8, cw), F32),
         send=DMA((count,)), recv=DMA((count,)), send1=DMA((count,)), recv1=DMA((count,)),
-        xs=DMA((4,)), xr=DMA((2,)), ls=DMA((4,)), lr=DMA((2,)), hs=DMA((2,)), hr=DMA((2,)), ps=DMA((6, 2)), pr=DMA((6,)), cs=DMA((4,)), cr=DMA((2,)),
+        xs=DMA((4,)), xr=DMA((2,)), ls=DMA((4,)), lr=DMA((2,)), hs=DMA((2,)), hr=DMA((2,)), ps=DMA((6,)), pr=DMA((6,)), cs=DMA((4,)), cr=DMA((2,)),
         es=DMA((2,)), er=DMA((2,)), gs=DMA((8, 12)), gr=DMA((8, 12)), save=DMA((8,)), keep=DMA((10,)),
     )
     scratch.update({k: pltpu.VMEM((4, 4) + shapes[v], BF) for k, v in names.items()}, **{k: pltpu.VMEM(*v) for k, v in held.items()})
@@ -1255,29 +1422,26 @@
     if fast:
         for name, k in (("w0", 0), ("w1", 1), ("m0", 3), ("m1", 3), ("r0", 2), ("r1", 2)):
             space.update(reduce_bank(name, shapes[k]))
-        for name, k in (("gw1_0", 0), ("gw2_0", 1), ("gw1_1", 0), ("gw2_1", 1), ("gr0", 2), ("gr1", 2), ("gm0", 3), ("gm1", 3)):
-            outs[name] = ((2,) + half_shape(shapes[k]), F32)
-        outs["total"] = ((64, cw), F32)
+        for name, k in (("gw1", 0), ("gw2", 1), ("gr", 2), ("gm", 3)):
+            space[name] = pltpu.VMEM((2,) + half_shape(shapes[k]), F32)
+        space["total"] = pltpu.VMEM((64, cw), F32)
+        outs.update(gwi=(w_in.shape, F32), gwo=(w_out.shape, F32), gres=(resample.shape, F32), gmm=((1, merge.shape[0]), F32))
+        outs.update(gk=((1, 49, c), F32), gg=((1, c), F32), gs=((1, c), F32), gbo=((1, c), F32), gbi=((1, hid), F32))
+        ins.update(half_hidden_back=at_any(mats["half_hidden_back"]), deep_back=at_any(mats["deep_back"]))
         space.update(sm=pltpu.VMEM((2, 64, cw), F32), tiny=pltpu.VMEM((9, 64, cw), F32), ts=DMA((9,)), tr=DMA((9,)))
     else:
         outs.update({f"{k}_{sec}": v + (ANY,) for k, v in wide_w.items() for sec in range(2)})
     bw = build("backward", lambda ns: back_kernel(fast, count, cols, ns), ins, outs, space, {}, 2, 63)
-    if fast:
-        rows_of = lambda v: v.reshape(-1, v.shape[-1])
-        tiny = bw.total
-        gw1 = unpack_in(rows_of(jnp.where(s == 0, bw.gw1_0, bw.gw1_1)), c, hid)
-        gw2 = unpack_in(jnp.where(s == 0, bw.gw2_0, bw.gw2_1).transpose(1, 0, 2).reshape(padded(hid), cw), hid, c)
-        gres = jnp.where(s == 0, unpack_down(rows_of(bw.gr0), c, n), unpack_up(rows_of(bw.gr1), c, n))
-        gmm = unpack_in(rows_of(jnp.where(s == 0, bw.gm0, bw.gm1)), c, c)
-    else:
-        scatter = lambda v: lax.psum_scatter(v.astype(F32).reshape(-1), both, scatter_dimension=0, tiled=True)
-        gw1 = scatter(jnp.stack([unpack_in(v, c, hid) for v in (bw.dw1_0, bw.dw1_1)]))
-        gw2 = scatter(jnp.stack([unpack_in(v, hid, c) for v in (bw.dw2_0, bw.dw2_1)]))
-        gres = scatter(jnp.stack([unpack_down(bw.dr0, c, n), unpack_up(bw.dr1, c, n)]))
-        gmm = scatter(jnp.stack([unpack_in(v, c, c) for v in (bw.dm0, bw.dm1)]))
-        tiny = lax.psum(jnp.stack([bw.tiny0, bw.tiny1]), both)[s]
     activations = bw.act.reshape(1, batches, height, cols, c)
     grad_input = bw.gi.astype(F32).reshape(1, batches, height, cols, c)
+    if fast:
+        return activations, grad_input, bw.gk, bw.gg, bw.gs, bw.gbi, bw.gbo, bw.gwi, bw.gwo, bw.gres, bw.gmm.reshape(-1)
+    scatter = lambda v: lax.psum_scatter(v.astype(F32).reshape(-1), both, scatter_dimension=0, tiled=True)
+    gw1 = scatter(jnp.stack([unpack_in(v, c, hid) for v in (bw.dw1_0, bw.dw1_1)]))
+    gw2 = scatter(jnp.stack([unpack_in(v, hid, c) for v in (bw.dw2_0, bw.dw2_1)]))
+    gres = scatter(jnp.stack([unpack_down(bw.dr0, c, n), unpack_up(bw.dr1, c, n)]))
+    gmm = scatter(jnp.stack([unpack_in(v, c, c) for v in (bw.dm0, bw.dm1)]))
+    tiny = lax.psum(jnp.stack([bw.tiny0, bw.tiny1]), both)[s]
     narrow = lambda v: v.reshape(-1, GROUPS, padded(c))[:, :, : c // GROUPS].reshape(-1, c)
     fine = narrow(tiny[:59])
     grad_bias_in = tiny[59:63].reshape(-1)[:hw].reshape(GROUPS, -1)[:, : hid // GROUPS].reshape(1, hid)

time: 376 us -> 351 us (0.934)
  local copies, waits for them, and re-layouts: 29.3 us -> 11.8 us
  other arithmetic: 17.9 us -> 6.45 us
  Pallas kernels: 320 us -> 325 us
    reshape x16 -> x1, local copies, waits for them, and re-layouts: 9.72 us -> 1.42 us  [on_device(): merge.reshape(1, -1)]
    another operation x8 -> x0, local copies, waits for them, and re-layouts: 5.3 us -> none  [the longest x1 1.38 us: on_device(): gw2[None]]
    unnamed x23 -> x26, local copies, waits for them, and re-layouts: 4.15 us -> 9.09 us
    pallas_call x2, Pallas kernels: 320 us -> 325 us  [build(): pl.pallas_call(kernel, name=name, out_shape=[jax.ShapeDtypeStruct(v[0], v...]
    slice x10 -> x0, local copies, waits for them, and re-layouts: 4.87 us -> none  [the longest x1 1.69 us: unpack_up(): value.transpose(0, 2, 1, 3, 4)[:, :n // GROUPS, :, :, :c // GROUPS]]
    unnamed x4 -> x0, other arithmetic: 4.75 us -> none
    convert_element_type x4 -> x0, other arithmetic: 4.27 us -> none  [the longest x3 3.49 us: on_device(): v.astype(BF)]
where the time goes in v5:
time: 351 us; the launch traced here: 344 us
  Pallas kernels  325 us (93%)
  local copies, waits for them, and re-layouts  11.8 us (3%)
  other arithmetic  6.45 us (2%)
    pallas_call x2, Pallas kernels, build(): pl.pallas_call(kernel, name=name, out_shape=[jax.ShapeDtypeStruct(v[0], v...  325 us
    unnamed x26, local copies, waits for them, and re-layouts  9.09 us

profile of v5, /device:TPU:8, one launch (start us, length us, event | category | flops | bytes accessed | tf_op | source)
XLA Modules:
  0.0 344.1 jit_solution(8743569503037625825)
XLA Ops:
  0.6 1.3 pad.4.refs_1_
  1.9 1.4 reshape.75.refs_18_
  3.4 1.5 copy.38.refs_19_
  4.9 138.0 %forward.1 = (f32[2,56,512]{2,1,0:T(8,128)}, f32[2,8,1792]{2,1,0:T(8,128)}, f32[1280,128]{1,0:T(8,128)}, f32[320,128]{1,0:T(8,128)}, f32[8,512]{1,0:T(8,128)}, /...) custom-call(bf16[4,4,10,16,400]{4,3,2,1,0:T(8,128)(2,1)} %bitcast.20, ...), custom_call_target="tpu_custom_call" | custom-call | tf_op jit(solution)/shard_map/forward/pallas_call | solution.py:1323
  142.9 186.9 %backward.1 = (bf16[4,4,10,16,400]{4,3,2,1,0:T(8,128)(2,1)}, bf16[4,4,10,16,400]{4,3,2,1,0:T(8,128)(2,1)}, f32[64,512]{1,0:T(8,128)}, f32[64,512]{1,0:T(8,128)},...) custom-call(bf16[8,10,16,400]{3,2,1,0:T(8,128)(2,1)} %get-tuple-elem, ...), custom_call_target="tpu_custom_call" | custom-call | tf_op jit(solution)/shard_map/backward/pallas_call | solution.py:1323
  329.8 1.5 reduce
  331.3 1.6 copy.39
  332.9 0.0 copy-start
  332.9 5.0 %convert.1 = f32[1,4,4,160,400]{4,3,2,1,0:T(8,128)} convert(bf16[1,4,4,160,400]{4,3,2,1,0:T(8,128)(2,1)} %bitcast.22) | non-fusion elementwise | flops 1024000 | bytes 6144000 | tf_op jit(solution)/shard_map/reshape | solution.py:1436
  337.9 0.0 copy-done
  337.9 0.0 copy-start.7
  337.9 0.0 copy-start.6
  337.9 0.0 copy-start.4
  337.9 0.0 copy-start.5
  337.9 0.0 copy-start.3
  337.9 0.0 copy-start.2
  337.9 0.0 copy-start.1
  337.9 1.5 copy.48
  339.4 0.0 copy-done.7
  339.4 0.6 copy.49
  340.0 0.0 copy-done.6
  340.0 0.6 copy.50
  340.6 0.0 copy-done.4
  340.6 0.6 copy.51
  341.2 0.0 copy-done.5
  341.2 0.6 copy.52
  341.8 0.0 copy-done.3
  341.8 0.7 copy.53
  342.4 0.0 copy-done.2
  342.4 0.7 copy.54
  343.1 0.0 copy-done.1
  343.1 0.7 copy.55
Async XLA Ops:
  332.9 5.0 %copy-start = (bf16[4,4,10,16,400]{4,3,2,1,0:T(8,128)(2,1)S(1)}, bf16[4,4,10,16,400]{4,3,2,1,0:T(8,128)(2,1)}, u32[]{:S(2)}) copy-start(bf16[4,4,10,16,400]{4,3,2,1,0:T(8,128)(2,1)} %get-tuple-element.72) | copy-start | bytes 6144004
  337.9 1.5 copy-start.7
  337.9 2.1 copy-start.6
  337.9 2.7 copy-start.4
  337.9 3.3 copy-start.5
  337.9 3.9 %copy-start.3 = (f32[1,40000]{1,0:T(1,128)S(1)}, f32[1,40000]{1,0:T(1,128)}, u32[]{:S(2)}) copy-start(f32[1,40000]{1,0:T(1,128)} %get-tuple-element.112) | copy-start | bytes 480004
  337.9 4.5 %copy-start.2 = (f32[1,40000]{1,0:T(1,128)S(1)}, f32[1,40000]{1,0:T(1,128)}, u32[]{:S(2)}) copy-start(f32[1,40000]{1,0:T(1,128)} %get-tuple-element.113) | copy-start | bytes 480004
  337.9 5.2 %copy-start.1 = (f32[1,80000]{1,0:T(1,128)S(1)}, f32[1,80000]{1,0:T(1,128)}, u32[]{:S(2)}) copy-start(f32[1,80000]{1,0:T(1,128)} %get-tuple-element.114) | copy-start | bytes 960004
